TPU v7x, 512 devices: a whole 4x8x8 slice. The times are simulated.
512 devices in a mesh: col: 32 (over y, z_lo), grp: 16 (over z_hi, x, core).
Axes of the slice: x: 4, y: 8, z: 8 (z_hi: 2, z_lo: 4; z = z_hi * 4 + z_lo), core: 2. Of those that a mesh axis runs over, the one named last changes fastest.
Arguments:
- events: bfloat16 [512, 256, 1024], P(('col', 'grp')), may hold values from -6 to 6
- item_ids: int32 [512, 256], P(('col', 'grp')), may hold values from 0 to 8191
- lengths: int32 [512], P(('col', 'grp')), may hold values from 1 to 256, 98304 in all
- uvqk_weight: bfloat16 [1024, 4096], P('col'), may hold values from -0.1875 to 0.1875
- out_weight: bfloat16 [1024, 1024], P('col'), may hold values from -0.1875 to 0.1875
- cotangent: bfloat16 [512, 256, 1024], P(('col', 'grp')), may hold values from -0.625 to 0.625
Outputs:
- table_grad: float32 [16, 8192, 1024], P('grp', None, 'col')
- out_weight_grad: float32 [1024, 1024], P('col')
All inputs are finite; a program needn't handle non-finite values. No bound on the sum of `lengths` on one device may be relied on, other than what follows from the above.
Results may differ from a plain program's by a relative error of at most 0.0073.
Values may be sent and summed in bfloat16 or wider, within the bound.
No kernel may reach another device: no remote copies, remote signals or barrier semaphores. Data moves between devices by JAX's collectives and lax.ppermute only.
A program may use at most 128 MiB of HBM per device.

v0:
```python
import jax
import jax.numpy as jnp
from jax import lax
from jax.sharding import PartitionSpec as P

HEADS = 8
ITEMS = 8192


EPSILON = 1e-05


def centre(values):
    mean_val = jnp.mean(values, axis=-1, keepdims=True)
    shifted = values - mean_val
    scale_inv = lax.rsqrt(jnp.mean(shifted * shifted, axis=-1, keepdims=True) + EPSILON)
    return (shifted * scale_inv, scale_inv)


def norm_back(grad, normed, scale_inv):
    first = jnp.mean(grad, axis=-1, keepdims=True)
    second = jnp.mean(grad * normed, axis=-1, keepdims=True)
    return scale_inv * (grad - first - normed * second)


def silu_slope(values):
    sig = jax.nn.sigmoid(values)
    return sig * (1.0 + values * (1.0 - sig))


def history_grads(events, length, cotangent, full_in, full_out):
    seq_len = events.shape[0]
    width = events.shape[1]
    head_dim = width // HEADS
    normed_in, inv_in = centre(events.astype(jnp.float32))
    normed_b = normed_in.astype(jnp.bfloat16)
    pre_act = jnp.dot(normed_b, full_in, preferred_element_type=jnp.float32)
    activ = jax.nn.silu(pre_act)
    gate_u = activ[:, :width]
    val_b = activ[:, width : 2 * width].astype(jnp.bfloat16).reshape(seq_len, HEADS, head_dim)
    query_b = activ[:, 2 * width : 3 * width].astype(jnp.bfloat16).reshape(seq_len, HEADS, head_dim)
    key_b = activ[:, 3 * width :].astype(jnp.bfloat16).reshape(seq_len, HEADS, head_dim)
    scale = head_dim ** (-0.5)
    positions = jnp.arange(seq_len, dtype=jnp.int32)
    live = positions < length
    causal = (positions[:, None] >= positions[None, :]) & live[:, None] & live[None, :]
    mask_f = causal.astype(jnp.float32)
    inv_len = 1.0 / length.astype(jnp.float32)
    scores = jnp.einsum("ihd,jhd->hij", query_b, key_b, preferred_element_type=jnp.float32) * scale
    weights_b = (jax.nn.silu(scores) * mask_f * inv_len).astype(jnp.bfloat16)
    attended = jnp.einsum(
        "hij,jhd->ihd", weights_b, val_b, preferred_element_type=jnp.float32
    ).reshape(seq_len, width)
    normed_att, inv_att = centre(attended)
    mixed_b = (normed_att * gate_u).astype(jnp.bfloat16)
    upstream = cotangent * live[:, None].astype(jnp.bfloat16)
    grad_mixed = jnp.dot(upstream, full_out.T, preferred_element_type=jnp.float32)
    grad_gate = grad_mixed * normed_att
    grad_att_b = (
        norm_back(grad_mixed * gate_u, normed_att, inv_att)
        .astype(jnp.bfloat16)
        .reshape(seq_len, HEADS, head_dim)
    )
    grad_weights = jnp.einsum("ihd,jhd->hij", grad_att_b, val_b, preferred_element_type=jnp.float32)
    grad_val = jnp.einsum("hij,ihd->jhd", weights_b, grad_att_b, preferred_element_type=jnp.float32)
    grad_scores = (grad_weights * mask_f * inv_len * silu_slope(scores) * scale).astype(
        jnp.bfloat16
    )
    grad_query = jnp.einsum("hij,jhd->ihd", grad_scores, key_b, preferred_element_type=jnp.float32)
    grad_key = jnp.einsum("hij,ihd->jhd", grad_scores, query_b, preferred_element_type=jnp.float32)
    grad_act = jnp.concatenate(
        [
            grad_gate,
            grad_val.reshape(seq_len, width),
            grad_query.reshape(seq_len, width),
            grad_key.reshape(seq_len, width),
        ],
        axis=1,
    )
    grad_pre = (grad_act * silu_slope(pre_act)).astype(jnp.bfloat16)
    grad_normed = jnp.dot(grad_pre, full_in.T, preferred_element_type=jnp.float32)
    grad_events = norm_back(grad_normed, normed_in, inv_in) + upstream.astype(jnp.float32)
    return (grad_events.astype(jnp.bfloat16), mixed_b, upstream)


def per_device(events, item_ids, lengths, uvqk_weight, out_weight, cotangent):
    full_in, full_out = (
        lax.all_gather(uvqk_weight, "col", axis=0, tiled=True),
        lax.all_gather(out_weight, "col", axis=0, tiled=True),
    )
    grad_rows, mixed_b, upstream = history_grads(
        events[0], lengths[0], cotangent[0], full_in, full_out
    )
    group_ids = lax.all_gather(item_ids, "col", axis=0, tiled=True)
    received = lax.all_to_all(grad_rows, "col", split_axis=1, concat_axis=0, tiled=True)
    table = jax.ops.segment_sum(
        received.astype(jnp.float32), group_ids.reshape(-1), num_segments=ITEMS
    )
    partial_grad = lax.psum_scatter(
        lax.dot_general(
            mixed_b, upstream, (((0,), (0,)), ((), ())), preferred_element_type=jnp.float32
        ),
        "col",
        scatter_dimension=0,
        tiled=True,
    )
    summed = lax.psum(partial_grad, "grp")
    return (table[None], summed)


def solution(mesh):
    return jax.shard_map(
        per_device,
        mesh=mesh,
        in_specs=(
            P(("col", "grp"), None, None),
            P(("col", "grp"), None),
            P(("col", "grp")),
            P("col", None),
            P("col", None),
            P(("col", "grp"), None, None),
        ),
        out_specs=(P("grp", None, "col"), P("col", None)),
        check_vma=False,
    )
```

profile of v0, /device:TPU:1, one launch (start us, length us, event | category | flops | bytes accessed | tf_op | source)
XLA Modules:
  0.0 733.1 jit_solution(11585829999016161266)
XLA Ops:
  7.2 0.0 all-gather.6.cloned.1.call-start
  7.2 0.7 all-gather.6.cloned.1.call-update
  7.9 0.0 all-gather.4.cloned.1.call-start
  7.9 0.7 all-gather.4.cloned.1.call-update
  8.6 0.0 reduce-scatter.2.cloned.1.call-start
  9.4 1.2 convert_reduce_fusion
  10.6 1.3 fusion.17
  11.9 0.1 fusion.44
  12.1 195.8 %all-gather.6.cloned.1.call-done = bf16[1024,4096]{1,0:T(8,128)(2,1)} async-done(((bf16[32,4096]{1,0:T(8,128)(2,1)}), bf16[1024,4096]{1,0:T(8,128)(2,1)}) %all-gather.6.cloned.1.call-update) | async-done | bytes 8388624 | tf_op jit(solution)/shard_map/all_gather | solution.py:88
  207.9 9.3 %fusion.50 = (bf16[256,4096]{1,0:T(8,128)(2,1)S(1)}, f32[256,4096]{1,0:T(8,128)}, f32[256,4096]{1,0:T(8,128)}) fusion(bf16[1024,4096]{1,0:T(8,128)(2,1)} %all-gather.6.cloned.1.call-done, bf16[1,256,1024]{2,1,0:T(8,128)(2,1)} %param.6, f32[256]{0:T(256)S(1)} %add_rsqrt_fusion.1, f32[256]{0:T(256)S(1)} %broadcast_multiply_fusion.5), kind=kOutput, calls=%fused_computation.75 | convolution fusion | flops 2153775104 | bytes 19400704 | tf_op jit(solution)/shard_map/dot_general | solution.py:37
  217.2 0.1 slice_bitcast_fusion
  217.3 0.0 copy-start.7
  217.3 0.2 copy.73
  217.5 0.0 copy-start.5
  217.5 0.2 copy.74
  217.7 0.0 copy-start.4
  217.8 0.8 copy-done.4
  218.5 2.2 multiply_convert_fusion.1
  220.7 0.0 copy-done.5
  220.7 0.0 copy-start.2
  220.7 0.0 copy-start.1
  220.7 0.0 copy-done.7
  220.7 0.5 fusion.52
  221.2 0.5 copy-done.2
  221.8 0.3 copy.67
  222.1 0.2 fusion.19
  222.3 0.0 copy-done.1
  222.3 4.1 fusion.22
  226.4 0.0 reduce-scatter.2.cloned.1.call-update
  226.5 0.0 copy-start.8
  226.5 117.9 %all-gather.4.cloned.1.call-done = bf16[1024,1024]{1,0:T(8,128)(2,1)} async-done(((bf16[32,1024]{1,0:T(8,128)(2,1)}), bf16[1024,1024]{1,0:T(8,128)(2,1)}) %all-gather.4.cloned.1.call-update) | async-done | bytes 2097168 | tf_op jit(solution)/shard_map/all_gather | solution.py:89
  344.3 0.0 copy-start.11
  344.3 2.9 fusion.48
  347.3 2.6 fusion.20
  349.9 0.0 copy-done.8
  349.9 0.0 copy-done.11
  349.9 1.1 multiply_convert_fusion
  351.1 0.0 copy-done.9
  351.1 0.1 copy-done.6
  351.1 1.3 fusion.54
  352.5 2.5 copy.70
  355.0 2.6 fusion.53
  357.6 2.6 copy.69
  360.2 0.0 copy-done.3
  360.2 1.4 fusion.25
  361.6 0.3 copy.68
  361.9 0.0 copy-done
  361.9 10.7 %fusion.49 = (f32[256]{0:T(256)S(1)}, f32[256]{0:T(256)S(1)}, f32[256,1024]{1,0:T(8,128)S(1)}) fusion(f32[256]{0:T(256)S(1)} %add_rsqrt_fusion.1, f32[256]{0:T(256)S(1)} %broadcast_multiply_fusion.5, bf16[1,256,1024]{2,1,0:T(8,128)(2,1)S(1)} %copy-done, bf16[1024,4096]{1,0:T(8,128)(2,1)} %all-gather.6.cloned.1.call-done, f32[256,1024]{1,0:T(8,128)} %copy.70, ...), kind=kOutput, calls=%fused_computation.74 | convolution fusion | flops 2161638912 | bytes 18354176 | tf_op jit(solution)/shard_map/dot_general | solution.py:81
  372.6 0.0 copy-start.10
  372.7 0.4 fusion.16
  373.1 1.0 copy.63
  374.1 7.1 all-to-all-start
  381.2 0.0 all-reduce.2.cloned.1.call-start
  381.3 0.0 copy-done.10
  381.3 68.0 %all-gather = s32[32,1,256]{2,1,0:T(1,128)S(1)} all-gather(s32[1,1,256]{2,1,0:T(1,128)S(1)} %bitcast.105), channel_id=1, replica_groups=mesh['col'=32,'grp'=16] {'col'}, dimensions={0}, use_global_device_ids=true | all-gather | bytes 33792 | tf_op jit(solution)/shard_map/all_gather | solution.py:94
  449.4 70.0 %reduce-scatter.2.cloned.1.call-done = f32[32,1024]{1,0:T(8,128)} async-done(((f32[1024,1024]{1,0:T(8,128)}), f32[32,1024]{1,0:T(8,128)}) %reduce-scatter.2.cloned.1.call-update) | async-done | bytes 131088 | tf_op jit(solution)/shard_map/reduce_scatter | solution.py:99
  519.3 0.0 all-reduce.2.cloned.1.call-update
  519.4 0.0 all-to-all-done
  519.4 0.1 convert_bitcast_fusion.1
  519.5 2.6 copy.71
  522.1 46.5 %scatter_custom_fusion = f32[8192,32]{1,0:T(8,128)} fusion(s32[8192]{0:T(1024)S(1)} %bitcast.104, f32[8192,32]{1,0:T(8,128)} %bitcast.96, f32[]{:T(128)} %constant.20.clone.1), kind=kCustom, calls=%fused_computation.8 | custom fusion | flops 262144 | bytes 1049088 | tf_op jit(solution)/shard_map/scatter-add | solution.py:96
  568.6 3.6 copy.66
  572.2 152.8 %all-reduce.2.cloned.1.call-done = f32[32,1024]{1,0:T(8,128)} async-done(((f32[32,1024]{1,0:T(8,128)}), f32[32,1024]{1,0:T(8,128)}) %all-reduce.2.cloned.1.call-update) | async-done | bytes 131088 | tf_op jit(solution)/shard_map/psum | solution.py:107
  725.0 1.6 copy.97
  (13 shorter events, 0.1 us)
Async XLA Ops:
  7.2 200.7 %all-gather.6.cloned.1.call-start = ((), (), s32[]{:S(2)}) async-start(), calls=%async_computation.3 | async-start | bytes 8650752 | tf_op jit(solution)/shard_map/all_gather | solution.py:88
  7.9 336.4 %all-gather.4.cloned.1.call-start = ((), (), s32[]{:S(2)}) async-start(), calls=%async_computation.2 | async-start | bytes 2162688 | tf_op jit(solution)/shard_map/all_gather | solution.py:89
  8.6 510.7 %reduce-scatter.2.cloned.1.call-start = ((), (), s32[]{:S(2)}) async-start(), calls=%async_computation.4 | async-start | bytes 4325376 | tf_op jit(solution)/shard_map/reduce_scatter | solution.py:99
  217.3 3.4 copy-start.7
  217.5 3.2 copy-start.5
  217.7 0.8 copy-start.4
  220.7 1.0 copy-start.2
  220.7 1.6 copy-start.1
  226.5 123.4 %copy-start.8 = (bf16[32,8,8,128]{3,2,1,0:T(8,128)(2,1)S(1)}, bf16[32,8,8,128]{3,2,1,0:T(8,128)(2,1)}, u32[]{:S(2)}) copy-start(bf16[32,8,8,128]{3,2,1,0:T(8,128)(2,1)} %copy-done.7) | copy-start | bytes 1572868
  344.3 5.6 copy-start.11
  349.9 1.2 copy-start.9
  349.9 1.2 copy-start.6
  351.1 9.0 %copy-start.3 = (bf16[8,256,256]{2,1,0:T(8,128)(2,1)S(1)}, bf16[8,256,256]{2,1,0:T(8,128)(2,1)}, u32[]{:S(2)}) copy-start(bf16[8,256,256]{2,1,0:T(8,128)(2,1)} %copy-done.2) | copy-start | bytes 3145732
  355.0 6.9 copy-start
  372.6 8.7 %copy-start.10 = (s32[1,256]{1,0:T(1,128)S(1)}, s32[1,256]{1,0:T(1,128)}, u32[]{:S(2)}) copy-start(s32[1,256]{1,0:T(1,128)} %param.7) | copy-start | bytes 3076
  374.1 145.3 %all-to-all-start = ((bf16[256,32,32]{0,2,1:T(8,128)(2,1)}), bf16[256,32,32]{0,2,1:T(8,128)(2,1)S(1)}, u32[]{:S(2)}, u32[]{:S(2)}) async-start(bf16[256,32,32]{0,2,1:T(8,128)(2,1)} %bitcast.13), calls=%async_computation | async-start | bytes 1048576 | tf_op jit(solution)/shard_map/all_to_all | solution.py:95
  381.2 343.7 %all-reduce.2.cloned.1.call-start = ((), (), s32[]{:S(2)}) async-start(), calls=%async_computation.5 | async-start | bytes 262144 | tf_op jit(solution)/shard_map/psum | solution.py:107
Sparse Core Ops, SparseCore 0:
  10.1 197.7 all-gather.5
  209.9 134.3 all-gather.3
  347.2 172.1 reduce-scatter.1
  522.1 202.8 all-reduce.1
where the time goes:
time: 734 us; the launch traced here: 733 us
  waiting for transfers between devices  538 us (73%)
  blocking collectives  68 us (9%)
  other arithmetic  52.5 us (7%)
  matrix products  36.2 us (5%)
  local copies, waits for them, and re-layouts  16.5 us (2%)
  between operations  14.7 us (2%)
    all_gather x1, waiting for transfers between devices, per_device(): lax.all_gather(uvqk_weight, 'col', axis=0, tiled=True)  196 us
    psum x1, waiting for transfers between devices, per_device(): summed = lax.psum(partial_grad, 'grp')  153 us
    all_gather x1, waiting for transfers between devices, per_device(): lax.all_gather(out_weight, 'col', axis=0, tiled=True)  118 us
    reduce_scatter x1, waiting for transfers between devices, per_device(): lax.psum_scatter(lax.dot_general(mixed_b, upstream, (((0,), (0,)), ((), (...  70 us
    all_gather x1, blocking collectives, per_device(): group_ids = lax.all_gather(item_ids, 'col', axis=0, tiled=True)  68 us
    scatter-add x1, other arithmetic, per_device(): jax.ops.segment_sum(received.astype(jnp.float32), group_ids.reshape(-1),...  46.5 us
  transfers between devices with their start and end apart: 5, of which 4 were waited for; matrix products, arithmetic and copies ran while one was open for 14% of the time, Pallas kernels for 0%

commit v1 on v0

v1 whole, which is shorter than its diff:
```python
import functools

import jax
import jax.numpy as jnp
from jax import lax
from jax.experimental import pallas as pl
from jax.experimental.pallas import tpu as pltpu
from jax.sharding import Mesh
from jax.sharding import PartitionSpec as P

HEADS = 8
ITEMS = 8192
SEQ = 256
WIDTH = 1024
HD = 128
EPSILON = 1e-05
BF = jnp.bfloat16
F32 = jnp.float32

AXES = ("y", "zl", "zh", "x", "c")
COL = ("y", "zl")
GRP = ("zh", "x", "c")
SIZES = (8, 4, 2, 4, 2)

NT = (((1,), (1,)), ((), ()))
TN = (((0,), (0,)), ((), ()))
NN = (((1,), (0,)), ((), ()))


def dot(a, b, dims=NN):
    return lax.dot_general(a, b, dims, preferred_element_type=F32)


def sigmoid(v):
    return 0.5 * jnp.tanh(0.5 * v) + 0.5


def score_mask(length):
    rows = lax.broadcasted_iota(jnp.int32, (SEQ, SEQ), 0)
    cols = lax.broadcasted_iota(jnp.int32, (SEQ, SEQ), 1)
    inv_len = 1.0 / jnp.full((1, 1), length, jnp.int32).astype(F32)
    return jnp.where((rows >= cols) & (rows < length), inv_len, 0.0)


SCALE = HD**-0.5


def forward_kernel(scalars, normed, keep_up, send_up, *refs):
    weights = refs[:HEADS]
    pre_out, natt_out, inv_out, keep_out, send_out, mixed = refs[HEADS:]
    mask = score_mask(scalars[0])
    total = jnp.zeros((SEQ, 1), F32)
    for r in range(HEADS):
        pre = dot(normed[...], weights[r][:, : 4 * HD])
        pre_out[r] = pre
        val, query, key = (
            (pre[:, k * HD : (k + 1) * HD] * sigmoid(pre[:, k * HD : (k + 1) * HD])).astype(BF)
            for k in (1, 2, 3)
        )
        scores = dot(query, key, NT) * SCALE
        attn = (scores * sigmoid(scores) * mask).astype(BF)
        att = dot(attn, val)
        natt_out[r] = att
        total = total + jnp.sum(att, axis=1, keepdims=True)
    mean = total * (1.0 / WIDTH)
    square = jnp.zeros((SEQ, 1), F32)
    for r in range(HEADS):
        shifted = natt_out[r] - mean
        square = square + jnp.sum(shifted * shifted, axis=1, keepdims=True)
    inv = lax.rsqrt(square * (1.0 / WIDTH) + EPSILON)
    inv_out[...] = jnp.broadcast_to(inv, (SEQ, HD))
    for r in range(HEADS):
        natt = (natt_out[r] - mean) * inv
        natt_out[r] = natt
        gate = pre_out[r, :, :HD]
        mixed[r] = (natt * (gate * sigmoid(gate))).astype(BF)
    for r in range(HEADS):
        rows = pl.ds(pl.multiple_of(scalars[1 + r] * HD, HD), HD)
        kept = dot(mixed[r], keep_up[...], TN).astype(BF)
        sent = dot(mixed[r], send_up[...], TN).astype(BF)
        for b in range(4):
            keep_out[b, rows, :] = kept[:, b * HD : (b + 1) * HD]
            send_out[b, rows, :] = sent[:, b * HD : (b + 1) * HD]


def backward_kernel(scalars, pre_in, natt_in, inv_in, upstream, normed_t, inv_t, up_t, *refs):
    weights = refs[:HEADS]
    out, grad_mixed, grad_normed = refs[HEADS:]
    mask = score_mask(scalars[0])
    gm = jnp.zeros((SEQ, WIDTH), F32)
    for r in range(HEADS):
        cols = pl.ds(pl.multiple_of(scalars[1 + r] * HD, HD), HD)
        gm = gm + dot(upstream[:, cols], weights[r][:, 4 * HD :], NT)
    grad_mixed[...] = gm
    first = jnp.zeros((SEQ, 1), F32)
    second = jnp.zeros((SEQ, 1), F32)
    for r in range(HEADS):
        cols = pl.ds(pl.multiple_of(scalars[1 + r] * HD, HD), HD)
        gate = pre_in[r, :, :HD]
        g = grad_mixed[:, cols] * (gate * sigmoid(gate))
        first = first + jnp.sum(g, axis=1, keepdims=True)
        second = second + jnp.sum(g * natt_in[r], axis=1, keepdims=True)
    first = first * (1.0 / WIDTH)
    second = second * (1.0 / WIDTH)
    inv = inv_in[:, :1]
    for r in range(HEADS):
        cols = pl.ds(pl.multiple_of(scalars[1 + r] * HD, HD), HD)
        natt = natt_in[r]
        gm_r = grad_mixed[:, cols]
        pre = pre_in[r]
        sig = sigmoid(pre)
        act = pre * sig
        slope = sig + act * (1.0 - sig)
        grad_att = (inv * (gm_r * act[:, :HD] - first - natt * second)).astype(BF)
        val, query, key = (act[:, k * HD : (k + 1) * HD].astype(BF) for k in (1, 2, 3))
        scores = dot(query, key, NT) * SCALE
        sig_s = sigmoid(scores)
        act_s = scores * sig_s
        attn = (act_s * mask).astype(BF)
        slope_s = (sig_s + act_s * (1.0 - sig_s)) * (mask * SCALE)
        grad_scores = (dot(grad_att, val, NT) * slope_s).astype(BF)
        grad_val = dot(attn, grad_att, TN)
        grad_query = dot(grad_scores, key)
        grad_key = dot(grad_scores, query, TN)
        grad_act = jnp.concatenate([gm_r * natt, grad_val, grad_query, grad_key], axis=1)
        grad_pre = (grad_act * slope).astype(BF)
        term = dot(weights[r][:, : 4 * HD], grad_pre, NT)
        if r == 0:
            grad_normed[...] = term
        else:
            grad_normed[...] += term
    gn = grad_normed[...]
    nt = normed_t[...]
    mean_1 = jnp.mean(gn, axis=0, keepdims=True)
    mean_2 = jnp.mean(gn * nt, axis=0, keepdims=True)
    rows = inv_t[...] * (gn - mean_1 - nt * mean_2) + up_t[...].astype(F32)
    out[...] = rows.astype(BF)


HI, LO = 32, 256
BLOCK = 4


def table_kernel(ids, rows, out, acc):
    senders = rows.shape[0]

    def step(i, _):
        left, right = [], []
        for k in range(BLOCK):
            item = ids[i * BLOCK + k]
            hi, lo = item // LO, item % LO
            hot_hi = (lax.broadcasted_iota(jnp.int32, (HI, SEQ), 0) == hi).astype(F32).astype(BF)
            hot_lo = (lax.broadcasted_iota(jnp.int32, (LO, SEQ), 0) == lo).astype(F32).astype(BF)
            part = rows[i * BLOCK + k]
            left.append(
                jnp.concatenate([hot_hi[h : h + 1, :] * part for h in range(HI)], axis=0)
            )
            right.append(hot_lo)
        acc[...] += dot(jnp.concatenate(left, axis=1), jnp.concatenate(right, axis=1), NT)
        return 0

    acc[...] = jnp.zeros_like(acc)
    lax.fori_loop(0, senders // BLOCK, step, 0)
    for h in range(HI):
        out[:, h * LO : (h + 1) * LO] = acc[h * 32 : (h + 1) * 32, :]


VMEM = pl.BlockSpec(memory_space=pltpu.VMEM)
SMEM = pl.BlockSpec(memory_space=pltpu.SMEM)
LIMIT = 56 * 1024 * 1024


def shape(dims, dtype):
    return jax.ShapeDtypeStruct(dims, dtype)


def forward(scalars, normed, keep_up, send_up, weights):
    return pl.pallas_call(
        forward_kernel,
        out_shape=[
            shape((HEADS, SEQ, 4 * HD), F32),
            shape((HEADS, SEQ, HD), F32),
            shape((SEQ, HD), F32),
            shape((4, WIDTH, HD), BF),
            shape((4, WIDTH, HD), BF),
        ],
        in_specs=[SMEM] + [VMEM] * (3 + HEADS),
        out_specs=[VMEM] * 5,
        scratch_shapes=[pltpu.VMEM((HEADS, SEQ, HD), BF)],
        compiler_params=pltpu.CompilerParams(vmem_limit_bytes=LIMIT),
        name="forward",
    )(scalars, normed, keep_up, send_up, *weights)


def backward(scalars, pre, natt, inv, upstream, normed_t, inv_t, up_t, weights):
    return pl.pallas_call(
        backward_kernel,
        out_shape=shape((WIDTH, SEQ), BF),
        in_specs=[SMEM] + [VMEM] * (7 + HEADS),
        out_specs=VMEM,
        scratch_shapes=[pltpu.VMEM((SEQ, WIDTH), F32), pltpu.VMEM((WIDTH, SEQ), F32)],
        compiler_params=pltpu.CompilerParams(vmem_limit_bytes=LIMIT),
        name="backward",
    )(scalars, pre, natt, inv, upstream, normed_t, inv_t, up_t, *weights)


def table_sum(ids, rows):
    return pl.pallas_call(
        table_kernel,
        out_shape=shape((32, ITEMS), F32),
        in_specs=[VMEM, VMEM],
        out_specs=VMEM,
        scratch_shapes=[pltpu.VMEM((HI * 32, LO), F32)],
        compiler_params=pltpu.CompilerParams(vmem_limit_bytes=LIMIT),
        name="table",
    )(ids, rows)


def shift(value, axis, size, by):
    return lax.ppermute(value, axis, [(i, (i + by) % size) for i in range(size)])


def spread(value, axes, count):
    many = jnp.broadcast_to(value[None], (count,) + value.shape)
    return lax.all_to_all(many, axes, 0, 0, tiled=True)


def gather_weights(uvqk, out_w):
    x, c = lax.axis_index("x"), lax.axis_index("c")
    me = x * 2 + c
    mine = lax.dynamic_slice_in_dim(uvqk.reshape(32, 4, HEADS, HD), me, 1, 2).reshape(32, 4 * HD)
    mine_out = lax.dynamic_slice_in_dim(out_w, me * HD, HD, 1)
    own = spread(jnp.concatenate([mine, mine_out], axis=1), COL, 32).reshape(WIDTH, 5 * HD)
    from_left = shift(own, "x", 4, 1)
    from_right = shift(own, "x", 4, -1)
    half = WIDTH // 2
    far_a = shift(from_left[:half], "x", 4, 1)
    far_b = shift(from_right[half:], "x", 4, -1)
    far = jnp.concatenate([far_a, far_b], axis=0)
    blocks = [own, from_left, from_right, far]
    swapped = [shift(b, "c", 2, 1) for b in blocks]
    xs = [x, (x + 3) % 4, (x + 1) % 4, (x + 2) % 4]
    heads = [xx * 2 + c for xx in xs] + [xx * 2 + 1 - c for xx in xs]
    return blocks + swapped, heads


def centre(values):
    mean_val = jnp.mean(values, axis=-1, keepdims=True)
    shifted = values - mean_val
    scale_inv = lax.rsqrt(jnp.mean(shifted * shifted, axis=-1, keepdims=True) + EPSILON)
    return (shifted * scale_inv, scale_inv)


def per_device(events, item_ids, lengths, uvqk_weight, out_weight, cotangent):
    c = lax.axis_index("c")
    weights, heads = gather_weights(uvqk_weight, out_weight)
    ids = spread(item_ids, COL, 32)

    length = lengths[0]
    scalars = jnp.stack([length] + heads).astype(jnp.int32)
    normed, inv_in = centre(events[0].astype(F32))
    live = lax.broadcasted_iota(jnp.int32, (SEQ, 1), 0) < length
    upstream = jnp.where(live, cotangent[0], jnp.zeros((), BF))
    split = upstream.reshape(SEQ, 4, 2, HD)
    keep_up = lax.dynamic_slice_in_dim(split, c, 1, 2).reshape(SEQ, 4 * HD)
    send_up = lax.dynamic_slice_in_dim(split, 1 - c, 1, 2).reshape(SEQ, 4 * HD)

    pre, natt, inv_att, kept, sent = forward(
        scalars, normed.astype(BF), keep_up, send_up, weights
    )
    part = (kept.astype(F32) + shift(sent, "c", 2, 1).astype(F32)).astype(BF)
    part = lax.all_to_all(part, "x", 0, 0, tiled=True)
    part = jnp.sum(part.astype(F32), axis=0).astype(BF)

    rows_t = backward(
        scalars, pre, natt, inv_att, upstream, normed.T, inv_in.T, upstream.T, weights
    )
    received = lax.all_to_all(rows_t.reshape(32, 32, SEQ), COL, 0, 0, tiled=True)

    part = lax.all_to_all(part.reshape(32, 32, HD), COL, 0, 0, tiled=True)
    part = jnp.sum(part.astype(F32), axis=0)
    part = spread(part, GRP, 16)
    summed = jnp.sum(part.reshape(2, 8, 32, HD), axis=0)
    summed = jnp.swapaxes(summed, 0, 1).reshape(32, WIDTH)

    table = table_sum(ids.reshape(32, 1, SEQ), received)
    return (table.T[None], summed)


def solution(mesh):
    fine = Mesh(mesh.devices.reshape(SIZES), AXES)
    every = COL + GRP
    return jax.shard_map(
        per_device,
        mesh=fine,
        in_specs=(
            P(every, None, None),
            P(every, None),
            P(every),
            P(COL, None),
            P(COL, None),
            P(every, None, None),
        ),
        out_specs=(P(GRP, None, COL), P(COL, None)),
        check_vma=False,
    )
```

time: 734 us -> 244 us (0.33)
  waiting for transfers between devices: 538 us -> 52.4 us
  starting transfers between devices: 7.29 us -> 62.5 us
  other arithmetic: 52.5 us -> 6.35 us
  matrix products: 36.2 us -> 0 us
  Pallas kernels: 0 us -> 35.4 us
  between operations: 14.7 us -> 1.63 us
    all_gather x2 -> x0, waiting for transfers between devices: 314 us -> none  [the longest x1 196 us: per_device(): lax.all_gather(uvqk_weight, 'col', axis=0, tiled=True)]
    psum x1 -> x0, waiting for transfers between devices: 153 us -> none  [per_device(): summed = lax.psum(partial_grad, 'grp')]
    reduce_scatter x1 -> x0, waiting for transfers between devices: 70 us -> none  [per_device(): lax.psum_scatter(lax.dot_general(mixed_b, upstream, (((0,), (0,)), ((), (...]
    all_gather x1 -> x0, blocking collectives: 68 us -> none  [per_device(): group_ids = lax.all_gather(item_ids, 'col', axis=0, tiled=True)]
    all_to_all x0 -> x2, blocking collectives: none -> 66.6 us  [the longest x1 47.4 us: spread(): return lax.all_to_all(many, axes, 0, 0, tiled=True)]
    scatter-add x1 -> x0, other arithmetic: 46.5 us -> none  [per_device(): jax.ops.segment_sum(received.astype(jnp.float32), group_ids.reshape(-1),...]
    dot_general x10 -> x0, matrix products: 36.2 us -> none  [the longest x1 10.7 us: history_grads(): jnp.dot(grad_pre, full_in.T, preferred_element_type=jnp.float32)]
    pallas_call x0 -> x3, Pallas kernels: none -> 35.4 us  [the longest x1 15.2 us: backward(): pl.pallas_call(backward_kernel, out_shape=shape((WIDTH, SEQ), BF), in_spe...]
  transfers between devices with their start and end apart: 5 -> 13, of which waited for: 4 -> 5; matrix products, arithmetic and copies ran while one was open for 14% -> 8% of each run, Pallas kernels for 0% -> 10%
where the time goes in v1:
time: 244 us; the launch traced here: 243 us
  blocking collectives  66.6 us (27%)
  starting transfers between devices  62.5 us (26%)
  waiting for transfers between devices  52.4 us (21%)
  Pallas kernels  35.4 us (15%)
  local copies, waits for them, and re-layouts  18.1 us (7%)
  other arithmetic  6.35 us (3%)
    all_to_all x1, blocking collectives, spread(): return lax.all_to_all(many, axes, 0, 0, tiled=True)  47.4 us
    ppermute x9, starting transfers between devices, shift(): lax.ppermute(value, axis, [(i, (i + by) % size) for i in range(size)])  28.6 us
    ppermute x9, waiting for transfers between devices, shift(): lax.ppermute(value, axis, [(i, (i + by) % size) for i in range(size)])  27 us
    all_to_all x2, starting transfers between devices, spread(): return lax.all_to_all(many, axes, 0, 0, tiled=True)  20.6 us
    all_to_all x1, blocking collectives, per_device(): part = lax.all_to_all(part, 'x', 0, 0, tiled=True)  19.3 us
    pallas_call x1, Pallas kernels, backward(): pl.pallas_call(backward_kernel, out_shape=shape((WIDTH, SEQ), BF), in_spe...  15.2 us
    all_to_all x1, waiting for transfers between devices, per_device(): lax.all_to_all(rows_t.reshape(32, 32, SEQ), COL, 0, 0, tiled=True)  14.2 us
    pallas_call x1, Pallas kernels, forward(): pl.pallas_call(forward_kernel, out_shape=[shape((HEADS, SEQ, 4 * HD), F32...  12.1 us
  transfers between devices with their start and end apart: 13, of which 5 were waited for; matrix products, arithmetic and copies ran while one was open for 8% of the time, Pallas kernels for 10%

profile of v1, /device:TPU:1, one launch (start us, length us, event | category | flops | bytes accessed | tf_op | source)
XLA Modules:
  0.0 243.1 jit_solution(4910406487269543878)
XLA Ops:
  0.6 0.0 copy-start
  0.7 1.0 copy.36
  1.7 0.2 dynamic-slice_reduce_fusion
  1.9 0.0 copy-done
  2.0 0.1 broadcast_in_dim.45
  2.1 47.4 %all_to_all.30 = bf16[32,32,640]{2,1,0:T(8,128)(2,1)S(1)} all-to-all(bf16[32,32,640]{2,1,0:T(8,128)(2,1)S(1)} %broadcast_in_dim.45), channel_id=1, replica_groups=mesh['y'=8,'zl'=4,'zh'=2,'x'=4,'c'=2] {'y','zl'}, dimensions={0} | all-to-all | bytes 2621440 | tf_op jit(solution)/shard_map/all_to_all | solution.py:225
  49.4 3.1 %collective-permute-start = (bf16[1024,640]{1,0:T(8,128)(2,1)S(1)}, bf16[1024,640]{1,0:T(8,128)(2,1)S(1)}, u32[]{:S(2)}, u32[]{:S(2)}) collective-permute-start(bf16[1024,640]{1,0:T(8,128)(2,1)S(1)} %bitcast.64), channel_id=1, source_target_pairs={{0,2},{2,4},{4,6},{6,0},{1,3},{3,5},{5,7},{7,1},{8,10},{10,12},{12... | collective-permute-start | bytes 3932168 | tf_op jit(solution)/shard_map/ppermute | solution.py:220
  52.6 3.4 %collective-permute-start.1 = (bf16[1024,640]{1,0:T(8,128)(2,1)S(1)}, bf16[1024,640]{1,0:T(8,128)(2,1)S(1)}, u32[]{:S(2)}, u32[]{:S(2)}) collective-permute-start(bf16[1024,640]{1,0:T(8,128)(2,1)S(1)} %bitcast.65), channel_id=1, source_target_pairs={{0,6},{2,0},{4,2},{6,4},{1,7},{3,1},{5,3},{7,5},{8,14},{10,8},{12,... | collective-permute-start | bytes 3932168 | tf_op jit(solution)/shard_map/ppermute | solution.py:220
  55.9 24.2 %collective-permute-done.refs_1_ = bf16[1024,640]{1,0:T(8,128)(2,1)S(1)} collective-permute-done((bf16[1024,640]{1,0:T(8,128)(2,1)S(1)}, bf16[1024,640]{1,0:T(8,128)(2,1)S(1)}, u32[]{:S(2)}, u32[]{:S(2)}) %collective-permute-start) | collective-permute-done | bytes 1310752 | tf_op jit(solution)/shard_map/ppermute | solution.py:220
  80.1 1.0 slice.8
  81.1 1.9 collective-permute-start.2
  83.0 0.0 collective-permute-done.1.refs_2_
  83.0 0.0 copy-start.3
  83.1 1.0 slice.9
  84.1 0.3 copy-done.3
  84.4 4.6 %collective-permute-start.3 = (bf16[512,640]{1,0:T(8,128)(2,1)}, bf16[512,640]{1,0:T(8,128)(2,1)}, u32[]{:S(2)}, u32[]{:S(2)}) collective-permute-start(bf16[512,640]{1,0:T(8,128)(2,1)} %slice.9), channel_id=1, source_target_pairs={{0,6},{2,0},{4,2},{6,4},{1,7},{3,1},{5,3},{7,5},{8,14},{10,8},{12,... | collective-permute-start | bytes 1966088 | tf_op jit(solution)/shard_map/ppermute | solution.py:220
  88.9 1.2 copy.25
  90.2 0.2 convert_reduce_fusion
  90.4 6.1 %collective-permute-start.4 = (bf16[1024,640]{1,0:T(8,128)(2,1)S(1)}, bf16[1024,640]{1,0:T(8,128)(2,1)}, u32[]{:S(2)}, u32[]{:S(2)}) collective-permute-start(bf16[1024,640]{1,0:T(8,128)(2,1)S(1)} %bitcast.66), channel_id=1, source_target_pairs={{0,1},{1,0},{2,3},{3,2},{4,5},{5,4},{6,7},{7,6},{8,9},{9,8},{10,11... | collective-permute-start | bytes 3932168 | tf_op jit(solution)/shard_map/ppermute | solution.py:220
  96.4 1.9 collective-permute-start.5
  98.4 2.4 collective-permute-start.6
  100.8 0.0 collective-permute-done.2
  100.8 2.0 constant_dynamic-update-slice_fusion.1
  102.8 0.0 collective-permute-done.3
  102.8 2.0 constant_dynamic-update-slice_fusion.refs_3_
  104.8 3.3 %collective-permute-start.7 = (bf16[1024,640]{1,0:T(8,128)(2,1)}, bf16[1024,640]{1,0:T(8,128)(2,1)}, u32[]{:S(2)}, u32[]{:S(2)}) collective-permute-start(bf16[1024,640]{1,0:T(8,128)(2,1)} %constant_dynamic-update-slice_fusion.refs_3_), channel_id=1, source_target_pairs={{0,1},{1,0},{2,3},{3,2},{4,5},{5,4},{6,7},{7,6},{8,9},{9,8},{10,11... | collective-permute-start | bytes 3932168 | tf_op jit(solution)/shard_map/ppermute | solution.py:220
  108.1 0.2 fusion.5
  108.9 2.2 squeeze.10
  111.1 1.3 fusion.3
  112.4 2.1 copy.28.normed
  114.6 0.6 stack.35.scalars
  115.2 1.3 copy_select_fusion
  116.5 0.2 constant_dynamic-slice_fusion.1
  116.7 0.9 copy_bitcast_fusion
  117.6 0.0 collective-permute-done.4.refs_4_
  117.6 0.0 collective-permute-done.5.refs_5_
  117.6 0.0 collective-permute-done.6.refs_6_
  117.6 0.0 collective-permute-done.7.refs_7_
  117.6 12.1 %forward.1 = (f32[8,256,512]{2,1,0:T(8,128)}, f32[8,256,128]{2,1,0:T(8,128)}, f32[256,128]{1,0:T(8,128)}, bf16[4,1024,128]{2,1,0:T(8,128)(2,1)}, bf16[4,1024,128]{2,1,0:T(8,128)(2,1)}) custom-call(s32[9]{0:T(128)} %stack.35.scalars, bf16[256,1024]{1,0:T(8,128)(2,1)} %copy.28.normed, bf16[256,512]{1,0:T(8,128)(2,1)} %get-tuple-element.17.keep_up, ...), custom_call_target="tpu_custom_call" | custom-call | tf_op jit(solution)/shard_map/forward/pallas_call | solution.py:178
  129.7 1.9 collective-permute-start.8
  131.6 2.8 %collective-permute-done.8 = bf16[4,1024,128]{2,1,0:T(8,128)(2,1)S(1)} collective-permute-done((bf16[4,1024,128]{2,1,0:T(8,128)(2,1)}, bf16[4,1024,128]{2,1,0:T(8,128)(2,1)S(1)}, u32[]{:S(2)}, u32[]{:S(2)}) %collective-permute-start.8) | collective-permute-done | bytes 1048608 | tf_op jit(solution)/shard_map/ppermute | solution.py:220
  134.4 1.5 add_convert_fusion
  135.9 0.0 copy-start.9
  136.0 19.3 %all_to_all.31 = bf16[4,1024,128]{2,1,0:T(8,128)(2,1)S(1)} all-to-all(bf16[4,1024,128]{2,1,0:T(8,128)(2,1)S(1)} %add_convert_fusion), channel_id=1, replica_groups=mesh['y'=8,'zl'=4,'zh'=2,'x'=4,'c'=2] {'x'}, dimensions={0} | all-to-all | bytes 2097152 | tf_op jit(solution)/shard_map/all_to_all | solution.py:272
  155.2 0.0 copy-done.9
  155.2 0.6 broadcast_in_dim.42
  155.8 7.0 %all-to-all-start = ((s32[32,1,256]{2,1,0:T(1,128)}), s32[32,1,256]{2,1,0:T(1,128)S(1)}, u32[]{:S(2)}, u32[]{:S(2)}) async-start(s32[32,1,256]{2,1,0:T(1,128)} %broadcast_in_dim.42), calls=%async_computation | async-start | bytes 65536 | tf_op jit(solution)/shard_map/all_to_all | solution.py:225
  162.9 0.9 reduce_sum.50
  163.8 8.2 %all-to-all-done.ids = s32[32,1,256]{2,1,0:T(1,128)S(1)} async-done(((s32[32,1,256]{2,1,0:T(1,128)}), s32[32,1,256]{2,1,0:T(1,128)S(1)}, u32[]{:S(2)}, u32[]{:S(2)}) %all-to-all-start) | async-done | bytes 32800 | tf_op jit(solution)/shard_map/all_to_all | solution.py:225
  172.0 4.1 %all-to-all-start.4 = ((bf16[32,32,128]{2,1,0:T(8,128)(2,1)}), bf16[32,32,128]{2,1,0:T(8,128)(2,1)S(1)}, u32[]{:S(2)}, u32[]{:S(2)}) async-start(bf16[32,32,128]{2,1,0:T(8,128)(2,1)} %bitcast.19), calls=%async_computation.4 | async-start | bytes 524288 | tf_op jit(solution)/shard_map/all_to_all | solution.py:280
  176.1 0.0 copy-done.5
  176.1 0.2 copy.29
  176.4 1.0 copy.30.upstream
  177.4 0.8 fusion.6.up_t
  178.2 15.2 %backward.1 = bf16[1024,256]{1,0:T(8,128)(2,1)} custom-call(s32[9]{0:T(128)} %stack.35.scalars, f32[8,256,512]{2,1,0:T(8,128)} %get-tuple-element.7.pre_in, f32[8,256,128]{2,1,0:T(8,128)} %get-tuple-element.8.natt_in, f32[256,128]{1,0:T(8,128)} %get-tuple-element.9.inv_in, bf16[256,1024]{1,0:T(8,128)(2,1)} %copy.30.upstream, ...), custom_call_target="tpu_custom_call" | custom-call | tf_op jit(solution)/shard_map/backward/pallas_call | solution.py:196
  193.4 0.0 all-to-all-done.4
  193.4 9.3 %all-to-all-start.2 = ((bf16[32,32,256]{2,1,0:T(8,128)(2,1)}), bf16[32,32,256]{2,1,0:T(8,128)(2,1)S(1)}, u32[]{:S(2)}, u32[]{:S(2)}) async-start(bf16[32,32,256]{2,1,0:T(8,128)(2,1)} %bitcast.69), calls=%async_computation.2 | async-start | bytes 1048576 | tf_op jit(solution)/shard_map/all_to_all | solution.py:278
  202.8 14.2 %all-to-all-done.2.rows = bf16[32,32,256]{2,1,0:T(8,128)(2,1)S(1)} async-done(((bf16[32,32,256]{2,1,0:T(8,128)(2,1)}), bf16[32,32,256]{2,1,0:T(8,128)(2,1)S(1)}, u32[]{:S(2)}, u32[]{:S(2)}) %all-to-all-start.2) | async-done | bytes 524320 | tf_op jit(solution)/shard_map/all_to_all | solution.py:278
  217.0 0.8 broadcast_in_dim.49
  217.8 13.5 %all-to-all-start.5 = ((f32[16,32,128]{2,1,0:T(8,128)}), f32[16,32,128]{2,1,0:T(8,128)S(1)}, u32[]{:S(2)}, u32[]{:S(2)}) async-start(f32[16,32,128]{2,1,0:T(8,128)} %broadcast_in_dim.49), calls=%async_computation.5 | async-start | bytes 524288 | tf_op jit(solution)/shard_map/all_to_all | solution.py:225
  231.3 0.0 copy-done.4
  231.3 8.2 %table.1 = f32[32,8192]{1,0:T(8,128)} custom-call(s32[32,1,256]{2,1,0:T(1,128)} %copy-done.7, bf16[32,32,256]{2,1,0:T(8,128)(2,1)} %copy-done.4), custom_call_target="tpu_custom_call" | custom-call | tf_op jit(solution)/shard_map/table/pallas_call | solution.py:208
  239.5 2.9 %all-to-all-done.5 = f32[16,32,128]{2,1,0:T(8,128)S(1)} async-done(((f32[16,32,128]{2,1,0:T(8,128)}), f32[16,32,128]{2,1,0:T(8,128)S(1)}, u32[]{:S(2)}, u32[]{:S(2)}) %all-to-all-start.5) | async-done | bytes 262176 | tf_op jit(solution)/shard_map/all_to_all | solution.py:225
  242.4 0.7 copy_bitcast_fusion.2
  (21 shorter events, 0.2 us)
Async XLA Ops:
  0.6 1.3 copy-start
  49.4 40.9 %copy-start.1 = (bf16[32,32,640]{2,1,0:T(8,128)(2,1)}, bf16[32,32,640]{2,1,0:T(8,128)(2,1)S(1)}, u32[]{:S(2)}) copy-start(bf16[32,32,640]{2,1,0:T(8,128)(2,1)S(1)} %all_to_all.30) | copy-start | bytes 3932164
  49.4 30.7 %collective-permute-start = (bf16[1024,640]{1,0:T(8,128)(2,1)S(1)}, bf16[1024,640]{1,0:T(8,128)(2,1)S(1)}, u32[]{:S(2)}, u32[]{:S(2)}) collective-permute-start(bf16[1024,640]{1,0:T(8,128)(2,1)S(1)} %bitcast.64), channel_id=1, source_target_pairs={{0,2},{2,4},{4,6},{6,0},{1,3},{3,5},{5,7},{7,1},{8,10},{10,12},{12... | collective-permute-start | bytes 3932168 | tf_op jit(solution)/shard_map/ppermute | solution.py:220
  52.6 30.5 %collective-permute-start.1 = (bf16[1024,640]{1,0:T(8,128)(2,1)S(1)}, bf16[1024,640]{1,0:T(8,128)(2,1)S(1)}, u32[]{:S(2)}, u32[]{:S(2)}) collective-permute-start(bf16[1024,640]{1,0:T(8,128)(2,1)S(1)} %bitcast.65), channel_id=1, source_target_pairs={{0,6},{2,0},{4,2},{6,4},{1,7},{3,1},{5,3},{7,5},{8,14},{10,8},{12,... | collective-permute-start | bytes 3932168 | tf_op jit(solution)/shard_map/ppermute | solution.py:220
  80.1 16.3 %copy-start.2 = (bf16[1024,640]{1,0:T(8,128)(2,1)}, bf16[1024,640]{1,0:T(8,128)(2,1)S(1)}, u32[]{:S(2)}) copy-start(bf16[1024,640]{1,0:T(8,128)(2,1)S(1)} %collective-permute-done.refs_1_) | copy-start | bytes 3932164
  81.1 19.7 %collective-permute-start.2 = (bf16[512,640]{1,0:T(8,128)(2,1)}, bf16[512,640]{1,0:T(8,128)(2,1)}, u32[]{:S(2)}, u32[]{:S(2)}) collective-permute-start(bf16[512,640]{1,0:T(8,128)(2,1)} %slice.8), channel_id=1, source_target_pairs={{0,2},{2,4},{4,6},{6,0},{1,3},{3,5},{5,7},{7,1},{8,10},{10,12},{12... | collective-permute-start | bytes 1966088 | tf_op jit(solution)/shard_map/ppermute | solution.py:220
  83.0 1.3 copy-start.3
  84.4 18.4 %collective-permute-start.3 = (bf16[512,640]{1,0:T(8,128)(2,1)}, bf16[512,640]{1,0:T(8,128)(2,1)}, u32[]{:S(2)}, u32[]{:S(2)}) collective-permute-start(bf16[512,640]{1,0:T(8,128)(2,1)} %slice.9), channel_id=1, source_target_pairs={{0,6},{2,0},{4,2},{6,4},{1,7},{3,1},{5,3},{7,5},{8,14},{10,8},{12,... | collective-permute-start | bytes 1966088 | tf_op jit(solution)/shard_map/ppermute | solution.py:220
  90.4 27.2 %collective-permute-start.4 = (bf16[1024,640]{1,0:T(8,128)(2,1)S(1)}, bf16[1024,640]{1,0:T(8,128)(2,1)}, u32[]{:S(2)}, u32[]{:S(2)}) collective-permute-start(bf16[1024,640]{1,0:T(8,128)(2,1)S(1)} %bitcast.66), channel_id=1, source_target_pairs={{0,1},{1,0},{2,3},{3,2},{4,5},{5,4},{6,7},{7,6},{8,9},{9,8},{10,11... | collective-permute-start | bytes 3932168 | tf_op jit(solution)/shard_map/ppermute | solution.py:220
  96.4 21.2 %collective-permute-start.5 = (bf16[1024,640]{1,0:T(8,128)(2,1)S(1)}, bf16[1024,640]{1,0:T(8,128)(2,1)}, u32[]{:S(2)}, u32[]{:S(2)}) collective-permute-start(bf16[1024,640]{1,0:T(8,128)(2,1)S(1)} %collective-permute-done.refs_1_), channel_id=1, source_target_pairs={{0,1},{1,0},{2,3},{3,2},{4,5},{5,4},{6,7},{7,6},{8,9},{9,8},{10,11... | collective-permute-start | bytes 3932168 | tf_op jit(solution)/shard_map/ppermute | solution.py:220
  98.4 19.2 %collective-permute-start.6 = (bf16[1024,640]{1,0:T(8,128)(2,1)}, bf16[1024,640]{1,0:T(8,128)(2,1)}, u32[]{:S(2)}, u32[]{:S(2)}) collective-permute-start(bf16[1024,640]{1,0:T(8,128)(2,1)} %copy-done.3), channel_id=1, source_target_pairs={{0,1},{1,0},{2,3},{3,2},{4,5},{5,4},{6,7},{7,6},{8,9},{9,8},{10,11... | collective-permute-start | bytes 3932168 | tf_op jit(solution)/shard_map/ppermute | solution.py:220
  104.8 12.9 %collective-permute-start.7 = (bf16[1024,640]{1,0:T(8,128)(2,1)}, bf16[1024,640]{1,0:T(8,128)(2,1)}, u32[]{:S(2)}, u32[]{:S(2)}) collective-permute-start(bf16[1024,640]{1,0:T(8,128)(2,1)} %constant_dynamic-update-slice_fusion.refs_3_), channel_id=1, source_target_pairs={{0,1},{1,0},{2,3},{3,2},{4,5},{5,4},{6,7},{7,6},{8,9},{9,8},{10,11... | collective-permute-start | bytes 3932168 | tf_op jit(solution)/shard_map/ppermute | solution.py:220
  111.1 3.4 %copy-start.8 = (f32[256]{0:T(256)}, f32[256]{0:T(256)S(1)}, u32[]{:S(2)}) copy-start(f32[256]{0:T(256)S(1)} %add_rsqrt_fusion) | copy-start | bytes 3076
  112.4 2.8 %copy-start.6 = (bf16[256,4,2,128]{3,2,1,0:T(2,128)(2,1)S(1)}, bf16[256,4,2,128]{3,2,1,0:T(2,128)(2,1)}, u32[]{:S(2)}) copy-start(bf16[256,4,2,128]{3,2,1,0:T(2,128)(2,1)} %squeeze.10) | copy-start | bytes 1572868
  129.7 4.8 %collective-permute-start.8 = (bf16[4,1024,128]{2,1,0:T(8,128)(2,1)}, bf16[4,1024,128]{2,1,0:T(8,128)(2,1)S(1)}, u32[]{:S(2)}, u32[]{:S(2)}) collective-permute-start(bf16[4,1024,128]{2,1,0:T(8,128)(2,1)} %get-tuple-element.11), channel_id=1, source_target_pairs={{0,1},{1,0},{2,3},{3,2},{4,5},{5,4},{6,7},{7,6},{8,9},{9,8},{10,11... | collective-permute-start | bytes 3145736 | tf_op jit(solution)/shard_map/ppermute | solution.py:220
  135.9 19.3 %copy-start.9 = (s32[1,256]{1,0:T(1,128)S(1)}, s32[1,256]{1,0:T(1,128)}, u32[]{:S(2)}) copy-start(s32[1,256]{1,0:T(1,128)} %param.7) | copy-start | bytes 3076
  155.2 20.9 %copy-start.5 = (bf16[1,256,1024]{2,1,0:T(8,128)(2,1)S(1)}, bf16[1,256,1024]{2,1,0:T(8,128)(2,1)}, u32[]{:S(2)}) copy-start(bf16[1,256,1024]{2,1,0:T(8,128)(2,1)} %param.11) | copy-start | bytes 1572868
  155.8 16.2 %all-to-all-start = ((s32[32,1,256]{2,1,0:T(1,128)}), s32[32,1,256]{2,1,0:T(1,128)S(1)}, u32[]{:S(2)}, u32[]{:S(2)}) async-start(s32[32,1,256]{2,1,0:T(1,128)} %broadcast_in_dim.42), calls=%async_computation | async-start | bytes 65536 | tf_op jit(solution)/shard_map/all_to_all | solution.py:225
  172.0 4.3 %copy-start.7 = (s32[32,1,256]{2,1,0:T(1,128)}, s32[32,1,256]{2,1,0:T(1,128)S(1)}, u32[]{:S(2)}) copy-start(s32[32,1,256]{2,1,0:T(1,128)S(1)} %all-to-all-done.ids) | copy-start | bytes 98308
  172.0 21.4 %all-to-all-start.4 = ((bf16[32,32,128]{2,1,0:T(8,128)(2,1)}), bf16[32,32,128]{2,1,0:T(8,128)(2,1)S(1)}, u32[]{:S(2)}, u32[]{:S(2)}) async-start(bf16[32,32,128]{2,1,0:T(8,128)(2,1)} %bitcast.19), calls=%async_computation.4 | async-start | bytes 524288 | tf_op jit(solution)/shard_map/all_to_all | solution.py:280
  193.4 23.6 %all-to-all-start.2 = ((bf16[32,32,256]{2,1,0:T(8,128)(2,1)}), bf16[32,32,256]{2,1,0:T(8,128)(2,1)S(1)}, u32[]{:S(2)}, u32[]{:S(2)}) async-start(bf16[32,32,256]{2,1,0:T(8,128)(2,1)} %bitcast.69), calls=%async_computation.2 | async-start | bytes 1048576 | tf_op jit(solution)/shard_map/all_to_all | solution.py:278
  217.0 14.3 %copy-start.4 = (bf16[32,32,256]{2,1,0:T(8,128)(2,1)}, bf16[32,32,256]{2,1,0:T(8,128)(2,1)S(1)}, u32[]{:S(2)}) copy-start(bf16[32,32,256]{2,1,0:T(8,128)(2,1)S(1)} %all-to-all-done.2.rows) | copy-start | bytes 1572868
  217.8 24.6 %all-to-all-start.5 = ((f32[16,32,128]{2,1,0:T(8,128)}), f32[16,32,128]{2,1,0:T(8,128)S(1)}, u32[]{:S(2)}, u32[]{:S(2)}) async-start(f32[16,32,128]{2,1,0:T(8,128)} %broadcast_in_dim.49), calls=%async_computation.5 | async-start | bytes 524288 | tf_op jit(solution)/shard_map/all_to_all | solution.py:225

commit v2 on v1

v2 whole, which is shorter than its diff:
```python
import functools

import jax
import jax.numpy as jnp
from jax import lax
from jax.experimental import pallas as pl
from jax.experimental.pallas import tpu as pltpu
from jax.sharding import Mesh
from jax.sharding import PartitionSpec as P

HEADS = 8
ITEMS = 8192
SEQ = 256
WIDTH = 1024
HD = 128
EPSILON = 1e-05
BF = jnp.bfloat16
F32 = jnp.float32

AXES = ("y", "zl", "zh", "x", "c")
COL = ("y", "zl")
GRP = ("zh", "x", "c")
SIZES = (8, 4, 2, 4, 2)

NT = (((1,), (1,)), ((), ()))
TN = (((0,), (0,)), ((), ()))
NN = (((1,), (0,)), ((), ()))


def dot(a, b, dims=NN):
    return lax.dot_general(a, b, dims, preferred_element_type=F32)


def sigmoid(v):
    return 0.5 * jnp.tanh(0.5 * v) + 0.5


def score_mask(length):
    rows = lax.broadcasted_iota(jnp.int32, (SEQ, SEQ), 0)
    cols = lax.broadcasted_iota(jnp.int32, (SEQ, SEQ), 1)
    inv_len = 1.0 / jnp.full((1, 1), length, jnp.int32).astype(F32)
    return jnp.where((rows >= cols) & (rows < length), inv_len, 0.0)


SCALE = HD**-0.5


COLS = HEADS * 256
OUT = 512
PAIRS = 4
PAIR = 512


ORDER = (0, 1, -1, -2)


def block_copies(scalars, buffers, part, sems, at, first, size):
    zl, c, sz = scalars[1], scalars[2], scalars[3]
    copies = []
    for core in range(2):
        half, sign = (c, sz) if core == 0 else (1 - c, -sz)
        own, near, far = buffers[core * 3 : core * 3 + 3]
        cols = slice(first, first + size)
        blocks = [own.at[:, :, cols], near.at[:, :, cols]]
        blocks += [far.at[k, :, :, at : at + size] for k in range(2)]
        for block, by in zip(blocks, ORDER):
            dst = part.at[half, :, lax.rem(zl + 8 + by * sign, 4), :, at : at + size]
            copies.append(pltpu.make_async_copy(block, dst, sems.at[len(copies)]))
    return copies


def weight_copies(scalars, buffers, weights, sems):
    return [
        block_copies(scalars, buffers, weights, sems.at[n], n * PAIR, n * PAIR, PAIR)
        for n in range(PAIRS)
    ]


def start(copies):
    for copy in copies:
        copy.start()


def wait(copies):
    for copy in copies:
        copy.wait()


def columns(weights, half, head):
    return weights[half, :, :, :, head * 256 : (head + 1) * 256].reshape(WIDTH, 256)


def row_mean(value):
    return jnp.sum(value, axis=1, keepdims=True) * (1.0 / WIDTH)


def forward_kernel(scalars, normed, *refs):
    buffers = refs[:6]
    pre_out, gate_out, natt_out, inv_out, mixed_out, pre, weights, sems, pre_sems = refs[6:]
    copies = weight_copies(scalars, buffers, weights, sems)
    for pair in copies:
        start(pair)
    mask = score_mask(scalars[0])
    total = jnp.zeros((SEQ, HD), F32)
    for h in range(HEADS):
        if h % 2 == 0:
            wait(copies[h // 2])
        pre_a = dot(normed[...], columns(weights, 0, h))
        pre_b = dot(normed[...], columns(weights, 1, h))
        pre[h, :, :256] = pre_a
        pre[h, :, 256:] = pre_b
        pltpu.make_async_copy(pre.at[h], pre_out.at[h], pre_sems.at[h]).start()
        act_a = pre_a * sigmoid(pre_a)
        act_b = (pre_b * sigmoid(pre_b)).astype(BF)
        gate_out[h] = act_a[:, :HD]
        scores = dot(act_b[:, :HD], act_b[:, HD:], NT) * SCALE
        attn = (scores * sigmoid(scores) * mask).astype(BF)
        att = dot(attn, act_a[:, HD:].astype(BF))
        natt_out[h] = att
        total = total + att
    mean = row_mean(total)
    square = jnp.zeros((SEQ, HD), F32)
    for h in range(HEADS):
        shifted = natt_out[h] - mean
        square = square + shifted * shifted
    inv = lax.rsqrt(row_mean(square) + EPSILON)
    inv_out[...] = jnp.broadcast_to(inv, (SEQ, HD))
    for h in range(HEADS):
        natt = (natt_out[h] - mean) * inv
        natt_out[h] = natt
        mixed_out[h * HD : (h + 1) * HD, :] = (natt * gate_out[h]).T.astype(BF)
    for h in range(HEADS):
        pltpu.make_async_copy(pre.at[h], pre_out.at[h], pre_sems.at[h]).wait()


def weight_kernel(mixed_t, other_mixed_t, up, other_up, out):
    total = dot(mixed_t[...], up[...]) + dot(other_mixed_t[...], other_up[...])
    total = total.astype(BF).reshape(32, 32, 4 * HD)
    for b in range(4):
        for k in range(2):
            part = total[:, k * 16 : (k + 1) * 16, b * HD : (b + 1) * HD]
            out[b, :, :, k * HD : (k + 1) * HD] = part


def backward_kernel(
    scalars, gate_in, natt_in, inv_in, upstream, normed_t, inv_t, up_t, pre_in, *refs
):
    out, weights, out_w, pre, grad_mixed, grad_pre, grad_normed, sems, out_sems, pre_sems = refs[8:]
    out_buffers = [*refs[0:2], refs[6], *refs[3:5], refs[7]]
    out_moves = block_copies(scalars, out_buffers, out_w, out_sems, 0, COLS, OUT)
    moves = weight_copies(scalars, refs[:6], weights, sems)
    pre_moves = [
        pltpu.make_async_copy(pre_in.at[h], pre.at[h], pre_sems.at[h]) for h in range(HEADS)
    ]
    start(out_moves)
    start(pre_moves)
    for pair in moves:
        start(pair)
    mask = score_mask(scalars[0])
    wait(out_moves)
    gm = dot(upstream[:, :OUT], out_w[0].reshape(WIDTH, OUT), NT)
    gm = gm + dot(upstream[:, OUT:], out_w[1].reshape(WIDTH, OUT), NT)
    grad_mixed[...] = gm
    first = jnp.zeros((SEQ, HD), F32)
    second = jnp.zeros((SEQ, HD), F32)
    for h in range(HEADS):
        g = grad_mixed[:, h * HD : (h + 1) * HD] * gate_in[h]
        first = first + g
        second = second + g * natt_in[h]
    first, second = row_mean(first), row_mean(second)
    inv = inv_in[:, :1]
    for h in range(HEADS):
        wait(pre_moves[h : h + 1])
        natt = natt_in[h]
        gm_h = grad_mixed[:, h * HD : (h + 1) * HD]
        pre_h = pre[h]
        sig = sigmoid(pre_h)
        act = pre_h * sig
        slope = sig + act * (1.0 - sig)
        grad_att = (inv * (gm_h * act[:, :HD] - first - natt * second)).astype(BF)
        val, query, key = (act[:, k * HD : (k + 1) * HD].astype(BF) for k in (1, 2, 3))
        scores = dot(query, key, NT) * SCALE
        sig_s = sigmoid(scores)
        act_s = scores * sig_s
        attn = (act_s * mask).astype(BF)
        slope_s = (sig_s + act_s * (1.0 - sig_s)) * (mask * SCALE)
        grad_scores = (dot(grad_att, val, NT) * slope_s).astype(BF)
        parts = [
            gm_h * natt,
            dot(attn, grad_att, TN),
            dot(grad_scores, key),
            dot(grad_scores, query, TN),
        ]
        for k in range(4):
            part = parts[k] * slope[:, k * HD : (k + 1) * HD]
            at = h * 256 + k % 2 * HD
            grad_pre[k // 2, :, at : at + HD] = part.astype(BF)
    for pair in moves:
        wait(pair)
    mean_1 = jnp.zeros((1, SEQ), F32)
    mean_2 = jnp.zeros((1, SEQ), F32)
    for m in range(4):
        rows = slice(m * 256, (m + 1) * 256)
        left, right = (weights[k, 2 * m : 2 * m + 2].reshape(256, COLS) for k in range(2))
        gn = dot(left, grad_pre[0], NT) + dot(right, grad_pre[1], NT)
        grad_normed[rows, :] = gn
        mean_1 = mean_1 + jnp.sum(gn, axis=0, keepdims=True)
        mean_2 = mean_2 + jnp.sum(gn * normed_t[rows, :], axis=0, keepdims=True)
    mean_1, mean_2 = mean_1 * (1.0 / WIDTH), mean_2 * (1.0 / WIDTH)
    for m in range(4):
        rows = slice(m * 256, (m + 1) * 256)
        grad = inv_t[...] * (grad_normed[rows, :] - mean_1 - normed_t[rows, :] * mean_2)
        out[rows, :] = (grad + up_t[rows, :].astype(F32)).astype(BF)


HI, LO = 32, 256
BLOCK = 4


def table_kernel(ids, rows, out, acc):
    senders = rows.shape[0]

    def step(i, _):
        left, right = [], []
        for k in range(BLOCK):
            n = i * BLOCK + k
            hi, lo = ids[n, 0:1, :], ids[n, 1:2, :]
            hot_hi = (lax.broadcasted_iota(jnp.int32, (HI, SEQ), 0) == hi).astype(F32).astype(BF)
            hot_lo = (lax.broadcasted_iota(jnp.int32, (LO, SEQ), 0) == lo).astype(F32).astype(BF)
            part = rows[n, :32, :]
            left.append(
                jnp.concatenate([hot_hi[h : h + 1, :] * part for h in range(HI)], axis=0)
            )
            right.append(hot_lo)
        acc[...] += dot(jnp.concatenate(left, axis=1), jnp.concatenate(right, axis=1), NT)
        return 0

    acc[...] = jnp.zeros_like(acc)
    lax.fori_loop(0, senders // BLOCK, step, 0)
    for h in range(HI):
        out[:, h * LO : (h + 1) * LO] = acc[h * 32 : (h + 1) * 32, :]


VMEM = pl.BlockSpec(memory_space=pltpu.VMEM)
SMEM = pl.BlockSpec(memory_space=pltpu.SMEM)
HBM = pl.BlockSpec(memory_space=pl.ANY)
LIMIT = 56 * 1024 * 1024
PARAMS = pltpu.CompilerParams(vmem_limit_bytes=LIMIT)
COST = pl.CostEstimate(flops=1024, bytes_accessed=1024, transcendentals=0)
WEIGHT_SCRATCH = pltpu.VMEM((2, 8, 4, 32, COLS), BF)
OUT_SCRATCH = pltpu.VMEM((2, 8, 4, 32, OUT), BF)
PRE_SCRATCH = pltpu.VMEM((HEADS, SEQ, 4 * HD), F32)


def shape(dims, dtype):
    return jax.ShapeDtypeStruct(dims, dtype)


def sems(count):
    return pltpu.SemaphoreType.DMA((count,))


def forward(scalars, normed, buffers):
    return pl.pallas_call(
        forward_kernel,
        out_shape=[
            shape((HEADS, SEQ, 4 * HD), F32),
            shape((HEADS, SEQ, HD), F32),
            shape((HEADS, SEQ, HD), F32),
            shape((SEQ, HD), F32),
            shape((WIDTH, SEQ), BF),
        ],
        in_specs=[SMEM, VMEM] + [HBM] * 6,
        out_specs=[HBM] + [VMEM] * 4,
        scratch_shapes=[PRE_SCRATCH, WEIGHT_SCRATCH, pltpu.SemaphoreType.DMA((PAIRS, 8)), sems(HEADS)],
        compiler_params=PARAMS,
        cost_estimate=COST,
        name="forward",
    )(scalars, normed, *buffers)


def weight_term(mixed, other_mixed, up, other_up):
    return pl.pallas_call(
        weight_kernel,
        out_shape=shape((4, 32, 16, 2 * HD), BF),
        in_specs=[VMEM] * 4,
        out_specs=VMEM,
        compiler_params=PARAMS,
        cost_estimate=COST,
        name="weight_term",
    )(mixed, other_mixed, up, other_up)


def backward(scalars, gate, natt, inv, upstream, normed_t, inv_t, up_t, pre, buffers):
    return pl.pallas_call(
        backward_kernel,
        out_shape=shape((WIDTH, SEQ), BF),
        in_specs=[SMEM] + [VMEM] * 7 + [HBM] * 9,
        out_specs=VMEM,
        scratch_shapes=[
            WEIGHT_SCRATCH,
            OUT_SCRATCH,
            PRE_SCRATCH,
            pltpu.VMEM((SEQ, WIDTH), F32),
            pltpu.VMEM((2, SEQ, COLS), BF),
            pltpu.VMEM((WIDTH, SEQ), F32),
            pltpu.SemaphoreType.DMA((PAIRS, 8)),
            sems(8),
            sems(HEADS),
        ],
        compiler_params=PARAMS,
        cost_estimate=COST,
        name="backward",
    )(scalars, gate, natt, inv, upstream, normed_t, inv_t, up_t, pre, *buffers)


def table_sum(ids, rows):
    return pl.pallas_call(
        table_kernel,
        out_shape=shape((32, ITEMS), F32),
        in_specs=[VMEM, VMEM],
        out_specs=VMEM,
        scratch_shapes=[pltpu.VMEM((HI * 32, LO), F32)],
        compiler_params=PARAMS,
        cost_estimate=COST,
        name="table",
    )(ids, rows)


def to_z(value, step):
    def index(z, c):
        return (z % 4) * 4 + z // 4 * 2 + c

    pairs = [
        (index(z, c), index((z + (1 - 2 * ((z + c + step) % 2))) % 8, c))
        for z in range(8)
        for c in range(2)
    ]
    return lax.ppermute(value, ("zl", "zh", "c"), pairs)


def swap(value):
    return lax.ppermute(value, "c", [(0, 1), (1, 0)])


def spread(value, axes, count):
    many = jnp.broadcast_to(value[None], (count,) + value.shape)
    return lax.all_to_all(many, axes, 0, 0, tiled=True)


def tie(*values):
    return lax.optimization_barrier(values)


def centre(values):
    mean_val = jnp.mean(values, axis=-1, keepdims=True)
    shifted = values - mean_val
    scale_inv = lax.rsqrt(jnp.mean(shifted * shifted, axis=-1, keepdims=True) + EPSILON)
    return (shifted * scale_inv, scale_inv)


def per_device(events, item_ids, lengths, uvqk_weight, out_weight, cotangent):
    zl, c = lax.axis_index("zl"), lax.axis_index("c")
    length = lengths[0]
    scalars = jnp.stack([length, zl, c, 1 - 2 * lax.rem(zl + c, 2)]).astype(jnp.int32)

    kinds = lax.dynamic_slice_in_dim(uvqk_weight.reshape(32, 4, HEADS, HD), 2 * c, 2, 1)
    kinds = jnp.swapaxes(kinds, 1, 2).reshape(32, COLS)
    out_w = lax.dynamic_slice_in_dim(out_weight, c * OUT, OUT, 1)
    own = spread(jnp.concatenate([kinds, out_w], axis=1), "y", 8)

    normed, inv_in = centre(events[0].astype(F32))
    live = lax.broadcasted_iota(jnp.int32, (SEQ, 1), 0) < length
    upstream = jnp.where(live, cotangent[0], jnp.zeros((), BF))
    split = upstream.reshape(SEQ, 4, 2, HD)
    half_up = lax.dynamic_slice_in_dim(split, c, 1, 2).reshape(SEQ, 4 * HD)
    send_up = lax.dynamic_slice_in_dim(split, 1 - c, 1, 2).reshape(SEQ, 4 * HD)
    normed_b, normed_t, up_t = normed.astype(BF), normed.T, upstream.T
    own, normed_b, normed_t, up_t, half_up, send_up = tie(
        own, normed_b, normed_t, up_t, half_up, send_up
    )

    near = to_z(own, 0)
    own_swapped = swap(own)
    near, own_swapped, send_up = tie(near, own_swapped, send_up)
    far = to_z(jnp.stack([own[:, :, :COLS], near[:, :, :COLS]]), 1)
    near_swapped, other_up = swap(near), swap(send_up)
    out_w = jnp.stack([own[:, :, COLS:], near[:, :, COLS:]])
    far, near_swapped, out_w, other_up = tie(far, near_swapped, out_w, other_up)
    buffers = [own, near, far, own_swapped, near_swapped, swap(far)]
    out_far = to_z(out_w, 1)
    pre, gate, natt, inv_att, mixed_t = forward(scalars, normed_b, buffers)
    mixed_t, out_far = tie(mixed_t, out_far)
    out_w = [out_far, swap(out_far)]
    part = weight_term(mixed_t, swap(mixed_t), half_up, other_up)
    part, natt = tie(part, natt)
    part = lax.all_to_all(part, "x", 0, 0, tiled=True)
    rows_t = backward(
        scalars, gate, natt, inv_att, upstream, normed_t, inv_in.T, up_t, pre, buffers + out_w
    )
    part, rows_t = tie(part, rows_t)
    part = jnp.sum(part.astype(F32), axis=0).astype(BF)
    digits = jnp.concatenate([item_ids // LO, item_ids % LO, jnp.zeros((6, SEQ), jnp.int32)])
    digits = jnp.broadcast_to(digits.astype(BF)[None], (32, 8, SEQ))
    both = jnp.concatenate([rows_t.reshape(32, 32, SEQ), part, digits], axis=1)
    both = lax.all_to_all(both, COL, 0, 0, tiled=True)
    part = jnp.sum(both[:, 32:48].astype(F32), axis=0)
    ids = both[:, 48:].astype(jnp.int32)
    part, both, ids = tie(part, both, ids)
    part = spread(jnp.concatenate([part[:, :HD], part[:, HD:]]), GRP, 16)
    table = table_sum(ids, both)
    summed = jnp.sum(part.reshape(2, 8, 32, HD), axis=0)
    summed = jnp.swapaxes(summed, 0, 1).reshape(32, WIDTH)
    return (table.T[None], summed)


def solution(mesh):
    fine = Mesh(mesh.devices.reshape(SIZES), AXES)
    every = COL + GRP
    return jax.shard_map(
        per_device,
        mesh=fine,
        in_specs=(
            P(every, None, None),
            P(every, None),
            P(every),
            P(COL, None),
            P(COL, None),
            P(every, None, None),
        ),
        out_specs=(P(GRP, None, COL), P(COL, None)),
        check_vma=False,
    )
```

time: 244 us -> 207 us (0.85)
  blocking collectives: 66.6 us -> 27.9 us
  waiting for transfers between devices: 52.4 us -> 62.8 us
  starting transfers between devices: 62.5 us -> 55.6 us
  local copies, waits for them, and re-layouts: 18.1 us -> 13.2 us
    all_to_all x2 -> x1, blocking collectives: 66.6 us -> 27.9 us  [per_device(): both = lax.all_to_all(both, COL, 0, 0, tiled=True)]
    all_to_all x2, waiting for transfers between devices: 11.1 us -> 31.4 us  [spread(): return lax.all_to_all(many, axes, 0, 0, tiled=True)]
    all_to_all x2 -> x1, waiting for transfers between devices: 14.2 us -> 0.01 us  [per_device(): part = lax.all_to_all(part, 'x', 0, 0, tiled=True)]
    all_to_all x2 -> x1, starting transfers between devices: 13.4 us -> 4.15 us  [per_device(): part = lax.all_to_all(part, 'x', 0, 0, tiled=True)]
    ppermute x9, starting transfers between devices: 28.6 us -> 35.3 us  [the longest x6 20.7 us: swap(): return lax.ppermute(value, 'c', [(0, 1), (1, 0)])]
    all_to_all x2, starting transfers between devices: 20.6 us -> 16.2 us  [spread(): return lax.all_to_all(many, axes, 0, 0, tiled=True)]
    ppermute x9, waiting for transfers between devices: 27 us -> 31.4 us  [the longest x3 28.2 us: to_z(): return lax.ppermute(value, ('zl', 'zh', 'c'), pairs)]
    pallas_call x0 -> x1, Pallas kernels: none -> 3.02 us  [weight_term(): pl.pallas_call(weight_kernel, out_shape=shape((4, 32, 16, 2 * HD), BF), i...]
  transfers between devices with their start and end apart: 13 -> 12, of which waited for: 5 -> 8; matrix products, arithmetic and copies ran while one was open for 8% -> 5% of each run, Pallas kernels for 10% -> 16%
where the time goes in v2:
time: 207 us; the launch traced here: 205 us
  waiting for transfers between devices  62.8 us (30%)
  starting transfers between devices  55.6 us (27%)
  Pallas kernels  36.5 us (18%)
  blocking collectives  27.9 us (13%)
  local copies, waits for them, and re-layouts  13.2 us (6%)
  other arithmetic  7.68 us (4%)
    all_to_all x2, waiting for transfers between devices, spread(): return lax.all_to_all(many, axes, 0, 0, tiled=True)  31.4 us
    ppermute x3, waiting for transfers between devices, to_z(): return lax.ppermute(value, ('zl', 'zh', 'c'), pairs)  28.2 us
    all_to_all x1, blocking collectives, per_device(): both = lax.all_to_all(both, COL, 0, 0, tiled=True)  27.9 us
    ppermute x6, starting transfers between devices, swap(): return lax.ppermute(value, 'c', [(0, 1), (1, 0)])  20.7 us
    all_to_all x2, starting transfers between devices, spread(): return lax.all_to_all(many, axes, 0, 0, tiled=True)  16.2 us
    ppermute x3, starting transfers between devices, to_z(): return lax.ppermute(value, ('zl', 'zh', 'c'), pairs)  14.6 us
    pallas_call x1, Pallas kernels, backward(): pl.pallas_call(backward_kernel, out_shape=shape((WIDTH, SEQ), BF), in_spe...  14.5 us
    pallas_call x1, Pallas kernels, forward(): pl.pallas_call(forward_kernel, out_shape=[shape((HEADS, SEQ, 4 * HD), F32...  10.6 us
  transfers between devices with their start and end apart: 12, of which 8 were waited for; matrix products, arithmetic and copies ran while one was open for 5% of the time, Pallas kernels for 16%

profile of v2, /device:TPU:1, one launch (start us, length us, event | category | flops | bytes accessed | tf_op | source)
XLA Modules:
  0.0 205.4 jit_solution(9090677301846599070)
XLA Ops:
  0.6 0.0 copy-start
  0.7 1.0 copy.28
  1.7 0.1 copy.20
  1.8 0.1 reshape.90
  2.0 0.0 copy-start.7
  2.0 1.2 broadcast_in_dim.42
  3.2 7.8 %all-to-all-start = ((bf16[8,32,2560]{2,1,0:T(8,128)(2,1)}), bf16[8,32,2560]{2,1,0:T(8,128)(2,1)S(1)}, u32[]{:S(2)}, u32[]{:S(2)}) async-start(bf16[8,32,2560]{2,1,0:T(8,128)(2,1)} %broadcast_in_dim.42), calls=%async_computation | async-start | bytes 2621440 | tf_op jit(solution)/shard_map/all_to_all | solution.py:348
  10.9 0.4 squeeze.11
  11.3 0.2 copy.22
  12.2 0.2 copy.21
  12.4 1.4 copy_select_fusion
  13.8 0.2 constant_dynamic-slice_fusion
  14.0 0.2 convert_reduce_fusion
  14.2 0.2 fusion.5
  14.4 0.8 copy_bitcast_fusion
  15.1 0.8 fusion.9.up_t
  16.0 1.1 fusion.3
  17.1 28.7 %all-to-all-done.refs_0_ = bf16[8,32,2560]{2,1,0:T(8,128)(2,1)S(1)} async-done(((bf16[8,32,2560]{2,1,0:T(8,128)(2,1)}), bf16[8,32,2560]{2,1,0:T(8,128)(2,1)S(1)}, u32[]{:S(2)}, u32[]{:S(2)}) %all-to-all-start) | async-done | bytes 1310752 | tf_op jit(solution)/shard_map/all_to_all | solution.py:348
  45.8 10.7 %collective-permute-start = (bf16[8,32,2560]{2,1,0:T(8,128)(2,1)S(1)}, bf16[8,32,2560]{2,1,0:T(8,128)(2,1)S(1)}, u32[]{:S(2)}, u32[]{:S(2)}) collective-permute-start(bf16[8,32,2560]{2,1,0:T(8,128)(2,1)S(1)} %all-to-all-done.refs_0_), channel_id=1, source_target_pairs={{0,16},{1,57},{16,0},{17,33},{32,48},{33,17},{48,32},{49,9},{8,24}... | collective-permute-start | bytes 3932168 | tf_op jit(solution)/shard_map/ppermute | solution.py:339
  56.5 1.9 collective-permute-start.1
  58.4 0.1 slice_bitcast_fusion.1
  58.6 12.9 %collective-permute-done.refs_1_ = bf16[8,32,2560]{2,1,0:T(8,128)(2,1)S(1)} collective-permute-done((bf16[8,32,2560]{2,1,0:T(8,128)(2,1)S(1)}, bf16[8,32,2560]{2,1,0:T(8,128)(2,1)S(1)}, u32[]{:S(2)}, u32[]{:S(2)}) %collective-permute-start) | collective-permute-done | bytes 1310752 | tf_op jit(solution)/shard_map/ppermute | solution.py:339
  71.5 0.0 collective-permute-done.1.refs_3_
  71.5 1.1 copy-done.5
  72.6 0.1 slice_bitcast_fusion
  72.7 0.2 pad_maximum_fusion
  72.9 1.9 collective-permute-start.2
  74.8 5.3 %collective-permute-start.3 = (bf16[8,32,2560]{2,1,0:T(8,128)(2,1)S(1)}, bf16[8,32,2560]{2,1,0:T(8,128)(2,1)S(1)}, u32[]{:S(2)}, u32[]{:S(2)}) collective-permute-start(bf16[8,32,2560]{2,1,0:T(8,128)(2,1)S(1)} %collective-permute-done.refs_1_), channel_id=1, source_target_pairs={{0,1},{1,0},{2,3},{3,2},{4,5},{5,4},{6,7},{7,6},{8,9},{9,8},{10,11... | collective-permute-start | bytes 3932168 | tf_op jit(solution)/shard_map/ppermute | solution.py:343
  80.2 1.9 collective-permute-start.4
  82.1 0.8 pad_maximum_fusion.2
  83.0 0.6 collective-permute-done.4.other_up
  83.6 0.0 collective-permute-done.3.refs_4_
  83.6 1.2 copy-done.6
  84.8 15.3 %collective-permute-done.2.refs_2_ = bf16[2,8,32,2048]{3,2,1,0:T(8,128)(2,1)} collective-permute-done((bf16[2,8,32,2048]{3,2,1,0:T(8,128)(2,1)S(1)}, bf16[2,8,32,2048]{3,2,1,0:T(8,128)(2,1)}, u32[]{:S(2)}, u32[]{:S(2)}) %collective-permute-start.2) | collective-permute-done | bytes 2097184 | tf_op jit(solution)/shard_map/ppermute | solution.py:339
  100.1 4.1 %collective-permute-start.5 = (bf16[2,8,32,2048]{3,2,1,0:T(8,128)(2,1)}, bf16[2,8,32,2048]{3,2,1,0:T(8,128)(2,1)S(1)}, u32[]{:S(2)}, u32[]{:S(2)}) collective-permute-start(bf16[2,8,32,2048]{3,2,1,0:T(8,128)(2,1)} %collective-permute-done.2.refs_2_), channel_id=1, source_target_pairs={{0,1},{1,0},{2,3},{3,2},{4,5},{5,4},{6,7},{7,6},{8,9},{9,8},{10,11... | collective-permute-start | bytes 6291464 | tf_op jit(solution)/shard_map/ppermute | solution.py:343
  104.2 1.9 collective-permute-start.6
  106.2 0.6 pad_add_fusion.scalars
  106.7 1.0 copy.24.normed
  107.8 0.4 collective-permute-done.5.refs_5_
  108.2 1.4 copy-done.3
  109.5 10.6 %forward.1 = (f32[8,256,512]{2,1,0:T(8,128)}, f32[8,256,128]{2,1,0:T(8,128)}, f32[8,256,128]{2,1,0:T(8,128)}, f32[256,128]{1,0:T(8,128)}, bf16[1024,256]{1,0:T(8,128)(2,1)}) custom-call(s32[4]{0:T(128)} %pad_add_fusion.scalars, bf16[256,1024]{1,0:T(8,128)(2,1)} %copy.24.normed, bf16[8,32,2560]{2,1,0:T(8,128)(2,1)} %copy-done.1, ...), custom_call_target="tpu_custom_call" | custom-call | flops 1024 | bytes 1024 | tf_op jit(solution)/shard_map/forward/pallas_call | solution.py:264
  120.2 0.0 collective-permute-done.6.refs_6_
  120.2 4.7 %collective-permute-start.7 = (bf16[1024,256]{1,0:T(8,128)(2,1)}, bf16[1024,256]{1,0:T(8,128)(2,1)S(1)}, u32[]{:S(2)}, u32[]{:S(2)}) collective-permute-start(bf16[1024,256]{1,0:T(8,128)(2,1)} %get-tuple-element.39.mixed_t), channel_id=1, source_target_pairs={{0,1},{1,0},{2,3},{3,2},{4,5},{5,4},{6,7},{7,6},{8,9},{9,8},{10,11... | collective-permute-start | bytes 1572872 | tf_op jit(solution)/shard_map/ppermute | solution.py:343
  124.9 1.7 collective-permute-done.7.other_mixed_t
  126.7 0.8 copy-done.9
  127.5 3.0 %weight_term.1 = bf16[4,32,16,256]{3,2,1,0:T(8,128)(2,1)} custom-call(bf16[1024,256]{1,0:T(8,128)(2,1)} %get-tuple-element.39.mixed_t, bf16[1024,256]{1,0:T(8,128)(2,1)} %copy-done.9, bf16[256,512]{1,0:T(8,128)(2,1)} %get-tuple-element.40.up, bf16[256,512]{1,0:T(8,128)(2,1)} %copy-done.11), custom_call_target="tpu_custom_call" | custom-call | flops 1024 | bytes 1024 | tf_op jit(solution)/shard_map/weight_term/pallas_call | solution.py:283
  130.5 4.2 %all-to-all-start.1 = ((bf16[4,32,16,256]{3,2,1,0:T(8,128)(2,1)}), bf16[4,32,16,256]{3,2,1,0:T(8,128)(2,1)S(1)}, u32[]{:S(2)}, u32[]{:S(2)}) async-start(bf16[4,32,16,256]{3,2,1,0:T(8,128)(2,1)} %weight_term.1), calls=%async_computation.1 | async-start | bytes 2097152 | tf_op jit(solution)/shard_map/all_to_all | solution.py:397
  134.7 2.7 %collective-permute-start.8 = (bf16[2,8,32,512]{3,2,1,0:T(8,128)(2,1)}, bf16[2,8,32,512]{3,2,1,0:T(8,128)(2,1)S(1)}, u32[]{:S(2)}, u32[]{:S(2)}) collective-permute-start(bf16[2,8,32,512]{3,2,1,0:T(8,128)(2,1)} %collective-permute-done.6.refs_6_), channel_id=1, source_target_pairs={{0,1},{1,0},{2,3},{3,2},{4,5},{5,4},{6,7},{7,6},{8,9},{9,8},{10,11... | collective-permute-start | bytes 1572872 | tf_op jit(solution)/shard_map/ppermute | solution.py:343
  137.5 1.0 copy.25.upstream
  138.5 0.1 pad.7.clone
  138.6 0.1 maximum_maximum_fusion
  138.6 0.3 collective-permute-done.8.refs_7_
  139.0 0.8 copy-done.8
  139.8 14.5 %backward.1 = bf16[1024,256]{1,0:T(8,128)(2,1)} custom-call(s32[4]{0:T(128)} %pad_add_fusion.scalars, f32[8,256,128]{2,1,0:T(8,128)} %get-tuple-element.44.gate_in, f32[8,256,128]{2,1,0:T(8,128)} %get-tuple-element.45.natt_in, f32[256,128]{1,0:T(8,128)} %get-tuple-element.46.inv_in, bf16[256,1024]{1,0:T(8,128)(2,1)} %copy.25.upstream, ...), custom_call_target="tpu_custom_call" | custom-call | flops 1024 | bytes 1024 | tf_op jit(solution)/shard_map/backward/pallas_call | solution.py:295
  154.3 0.0 all-to-all-done.1
  154.3 0.2 reduce_sum.50
  154.5 1.1 pad_maximum_fusion.1
  155.6 27.9 %all_to_all.20.rows = bf16[32,56,256]{2,1,0:T(8,128)(2,1)S(1)} all-to-all(bf16[32,56,256]{2,1,0:T(8,128)(2,1)S(1)} %pad_maximum_fusion.1), channel_id=1, replica_groups=mesh['y'=8,'zl'=4,'zh'=2,'x'=4,'c'=2] {'y','zl'}, dimensions={0} | all-to-all | bytes 1835008 | tf_op jit(solution)/shard_map/all_to_all | solution.py:406
  183.6 0.8 slice_convert_fusion.ids
  184.5 0.7 broadcast_in_dim.50
  185.2 8.4 %all-to-all-start.3 = ((f32[16,32,128]{2,1,0:T(8,128)}), f32[16,32,128]{2,1,0:T(8,128)S(1)}, u32[]{:S(2)}, u32[]{:S(2)}) async-start(f32[16,32,128]{2,1,0:T(8,128)} %broadcast_in_dim.50), calls=%async_computation.3 | async-start | bytes 524288 | tf_op jit(solution)/shard_map/all_to_all | solution.py:348
  193.6 8.4 %table.1 = f32[32,8192]{1,0:T(8,128)} custom-call(s32[32,8,256]{2,1,0:T(8,128)} %slice_convert_fusion.ids, bf16[32,56,256]{2,1,0:T(8,128)(2,1)} %copy-done.4), custom_call_target="tpu_custom_call" | custom-call | flops 1024 | bytes 1024 | tf_op jit(solution)/shard_map/table/pallas_call | solution.py:318
  202.0 2.7 %all-to-all-done.3 = f32[16,32,128]{2,1,0:T(8,128)S(1)} async-done(((f32[16,32,128]{2,1,0:T(8,128)}), f32[16,32,128]{2,1,0:T(8,128)S(1)}, u32[]{:S(2)}, u32[]{:S(2)}) %all-to-all-start.3) | async-done | bytes 262176 | tf_op jit(solution)/shard_map/all_to_all | solution.py:348
  204.7 0.7 copy_bitcast_fusion.2
  (38 shorter events, 0.3 us)
Async XLA Ops:
  0.6 1.3 copy-start
  2.0 9.0 %copy-start.7 = (bf16[1,256,1024]{2,1,0:T(8,128)(2,1)S(1)}, bf16[1,256,1024]{2,1,0:T(8,128)(2,1)}, u32[]{:S(2)}) copy-start(bf16[1,256,1024]{2,1,0:T(8,128)(2,1)} %param.11) | copy-start | bytes 1572868
  3.2 9.0 %copy-start.10 = (bf16[1,256,1024]{2,1,0:T(8,128)(2,1)S(1)}, bf16[1,256,1024]{2,1,0:T(8,128)(2,1)}, u32[]{:S(2)}) copy-start(bf16[1,256,1024]{2,1,0:T(8,128)(2,1)} %param.6) | copy-start | bytes 1572868
  3.2 42.6 %all-to-all-start = ((bf16[8,32,2560]{2,1,0:T(8,128)(2,1)}), bf16[8,32,2560]{2,1,0:T(8,128)(2,1)S(1)}, u32[]{:S(2)}, u32[]{:S(2)}) async-start(bf16[8,32,2560]{2,1,0:T(8,128)(2,1)} %broadcast_in_dim.42), calls=%async_computation | async-start | bytes 2621440 | tf_op jit(solution)/shard_map/all_to_all | solution.py:348
  14.4 2.7 %copy-start.12 = (f32[256]{0:T(256)}, f32[256]{0:T(256)S(1)}, u32[]{:S(2)}) copy-start(f32[256]{0:T(256)S(1)} %add_rsqrt_fusion) | copy-start | bytes 3076
  45.7 34.4 %copy-start.1 = (bf16[8,32,2560]{2,1,0:T(8,128)(2,1)}, bf16[8,32,2560]{2,1,0:T(8,128)(2,1)S(1)}, u32[]{:S(2)}) copy-start(bf16[8,32,2560]{2,1,0:T(8,128)(2,1)S(1)} %all-to-all-done.refs_0_) | copy-start | bytes 3932164
  45.8 25.7 %collective-permute-start = (bf16[8,32,2560]{2,1,0:T(8,128)(2,1)S(1)}, bf16[8,32,2560]{2,1,0:T(8,128)(2,1)S(1)}, u32[]{:S(2)}, u32[]{:S(2)}) collective-permute-start(bf16[8,32,2560]{2,1,0:T(8,128)(2,1)S(1)} %all-to-all-done.refs_0_), channel_id=1, source_target_pairs={{0,16},{1,57},{16,0},{17,33},{32,48},{33,17},{48,32},{49,9},{8,24}... | collective-permute-start | bytes 3932168 | tf_op jit(solution)/shard_map/ppermute | solution.py:339
  56.5 15.0 %collective-permute-start.1 = (bf16[8,32,2560]{2,1,0:T(8,128)(2,1)S(1)}, bf16[8,32,2560]{2,1,0:T(8,128)(2,1)S(1)}, u32[]{:S(2)}, u32[]{:S(2)}) collective-permute-start(bf16[8,32,2560]{2,1,0:T(8,128)(2,1)S(1)} %all-to-all-done.refs_0_), channel_id=1, source_target_pairs={{0,1},{1,0},{2,3},{3,2},{4,5},{5,4},{6,7},{7,6},{8,9},{9,8},{10,11... | collective-permute-start | bytes 3932168 | tf_op jit(solution)/shard_map/ppermute | solution.py:343
  71.5 10.6 %copy-start.2 = (bf16[8,32,2560]{2,1,0:T(8,128)(2,1)}, bf16[8,32,2560]{2,1,0:T(8,128)(2,1)S(1)}, u32[]{:S(2)}) copy-start(bf16[8,32,2560]{2,1,0:T(8,128)(2,1)S(1)} %collective-permute-done.refs_1_) | copy-start | bytes 3932164
  71.5 1.1 copy-start.5
  72.9 27.2 %collective-permute-start.2 = (bf16[2,8,32,2048]{3,2,1,0:T(8,128)(2,1)S(1)}, bf16[2,8,32,2048]{3,2,1,0:T(8,128)(2,1)}, u32[]{:S(2)}, u32[]{:S(2)}) collective-permute-start(bf16[2,8,32,2048]{3,2,1,0:T(8,128)(2,1)S(1)} %pad_maximum_fusion), channel_id=1, source_target_pairs={{0,56},{1,17},{16,32},{17,1},{32,16},{33,49},{48,8},{49,33},{8,48}... | collective-permute-start | bytes 6291464 | tf_op jit(solution)/shard_map/ppermute | solution.py:339
  74.8 8.8 %collective-permute-start.3 = (bf16[8,32,2560]{2,1,0:T(8,128)(2,1)S(1)}, bf16[8,32,2560]{2,1,0:T(8,128)(2,1)S(1)}, u32[]{:S(2)}, u32[]{:S(2)}) collective-permute-start(bf16[8,32,2560]{2,1,0:T(8,128)(2,1)S(1)} %collective-permute-done.refs_1_), channel_id=1, source_target_pairs={{0,1},{1,0},{2,3},{3,2},{4,5},{5,4},{6,7},{7,6},{8,9},{9,8},{10,11... | collective-permute-start | bytes 3932168 | tf_op jit(solution)/shard_map/ppermute | solution.py:343
  80.2 3.4 %collective-permute-start.4 = (bf16[256,512]{1,0:T(8,128)(2,1)S(1)}, bf16[256,512]{1,0:T(8,128)(2,1)S(1)}, u32[]{:S(2)}, u32[]{:S(2)}) collective-permute-start(bf16[256,512]{1,0:T(8,128)(2,1)S(1)} %get-tuple-element.33), channel_id=1, source_target_pairs={{0,1},{1,0},{2,3},{3,2},{4,5},{5,4},{6,7},{7,6},{8,9},{9,8},{10,11... | collective-permute-start | bytes 786440 | tf_op jit(solution)/shard_map/ppermute | solution.py:343
  83.6 36.6 %copy-start.11 = (bf16[256,512]{1,0:T(8,128)(2,1)}, bf16[256,512]{1,0:T(8,128)(2,1)S(1)}, u32[]{:S(2)}) copy-start(bf16[256,512]{1,0:T(8,128)(2,1)S(1)} %collective-permute-done.4.other_up) | copy-start | bytes 786436
  83.6 1.2 copy-start.6
  100.1 8.1 %collective-permute-start.5 = (bf16[2,8,32,2048]{3,2,1,0:T(8,128)(2,1)}, bf16[2,8,32,2048]{3,2,1,0:T(8,128)(2,1)S(1)}, u32[]{:S(2)}, u32[]{:S(2)}) collective-permute-start(bf16[2,8,32,2048]{3,2,1,0:T(8,128)(2,1)} %collective-permute-done.2.refs_2_), channel_id=1, source_target_pairs={{0,1},{1,0},{2,3},{3,2},{4,5},{5,4},{6,7},{7,6},{8,9},{9,8},{10,11... | collective-permute-start | bytes 6291464 | tf_op jit(solution)/shard_map/ppermute | solution.py:343
  104.2 16.0 %collective-permute-start.6 = (bf16[2,8,32,512]{3,2,1,0:T(8,128)(2,1)}, bf16[2,8,32,512]{3,2,1,0:T(8,128)(2,1)}, u32[]{:S(2)}, u32[]{:S(2)}) collective-permute-start(bf16[2,8,32,512]{3,2,1,0:T(8,128)(2,1)} %pad_maximum_fusion.2), channel_id=1, source_target_pairs={{0,56},{1,17},{16,32},{17,1},{32,16},{33,49},{48,8},{49,33},{8,48}... | collective-permute-start | bytes 1572872 | tf_op jit(solution)/shard_map/ppermute | solution.py:339
  108.2 1.4 copy-start.3
  120.2 6.4 %collective-permute-start.7 = (bf16[1024,256]{1,0:T(8,128)(2,1)}, bf16[1024,256]{1,0:T(8,128)(2,1)S(1)}, u32[]{:S(2)}, u32[]{:S(2)}) collective-permute-start(bf16[1024,256]{1,0:T(8,128)(2,1)} %get-tuple-element.39.mixed_t), channel_id=1, source_target_pairs={{0,1},{1,0},{2,3},{3,2},{4,5},{5,4},{6,7},{7,6},{8,9},{9,8},{10,11... | collective-permute-start | bytes 1572872 | tf_op jit(solution)/shard_map/ppermute | solution.py:343
  126.6 0.8 copy-start.9
  130.5 6.9 %copy-start.13 = (s32[1,256]{1,0:T(1,128)S(1)}, s32[1,256]{1,0:T(1,128)}, u32[]{:S(2)}) copy-start(s32[1,256]{1,0:T(1,128)} %param.7) | copy-start | bytes 3076
  130.5 23.8 %all-to-all-start.1 = ((bf16[4,32,16,256]{3,2,1,0:T(8,128)(2,1)}), bf16[4,32,16,256]{3,2,1,0:T(8,128)(2,1)S(1)}, u32[]{:S(2)}, u32[]{:S(2)}) async-start(bf16[4,32,16,256]{3,2,1,0:T(8,128)(2,1)} %weight_term.1), calls=%async_computation.1 | async-start | bytes 2097152 | tf_op jit(solution)/shard_map/all_to_all | solution.py:397
  134.7 4.3 %collective-permute-start.8 = (bf16[2,8,32,512]{3,2,1,0:T(8,128)(2,1)}, bf16[2,8,32,512]{3,2,1,0:T(8,128)(2,1)S(1)}, u32[]{:S(2)}, u32[]{:S(2)}) collective-permute-start(bf16[2,8,32,512]{3,2,1,0:T(8,128)(2,1)} %collective-permute-done.6.refs_6_), channel_id=1, source_target_pairs={{0,1},{1,0},{2,3},{3,2},{4,5},{5,4},{6,7},{7,6},{8,9},{9,8},{10,11... | collective-permute-start | bytes 1572872 | tf_op jit(solution)/shard_map/ppermute | solution.py:343
  139.0 0.8 copy-start.8
  183.6 10.0 %copy-start.4 = (bf16[32,56,256]{2,1,0:T(8,128)(2,1)}, bf16[32,56,256]{2,1,0:T(8,128)(2,1)S(1)}, u32[]{:S(2)}) copy-start(bf16[32,56,256]{2,1,0:T(8,128)(2,1)S(1)} %all_to_all.20.rows) | copy-start | bytes 2752516
  185.2 19.5 %all-to-all-start.3 = ((f32[16,32,128]{2,1,0:T(8,128)}), f32[16,32,128]{2,1,0:T(8,128)S(1)}, u32[]{:S(2)}, u32[]{:S(2)}) async-start(f32[16,32,128]{2,1,0:T(8,128)} %broadcast_in_dim.50), calls=%async_computation.3 | async-start | bytes 524288 | tf_op jit(solution)/shard_map/all_to_all | solution.py:348

commit v3 on v2

--- a/solution.py
+++ b/solution.py
@@ -94,30 +94,56 @@
     return jnp.sum(value, axis=1, keepdims=True) * (1.0 / WIDTH)
 
 
+def prepare_kernel(scalars, events, cotangent, normed, normed_t, inv_t, up, up_t, half_up, send_up):
+    length, c, x = scalars[0], scalars[2], scalars[4]
+    value = events[...].astype(F32)
+    shifted = value - row_mean(value)
+    inv = lax.rsqrt(row_mean(shifted * shifted) + EPSILON)
+    value = shifted * inv
+    normed[...] = value.astype(BF)
+    normed_t[...] = value.T
+    inv_t[...] = jnp.broadcast_to(inv, (SEQ, HD)).T[:8]
+    live = lax.broadcasted_iota(jnp.int32, (SEQ, 1), 0) < length
+    masked = jnp.where(live, cotangent[...].astype(F32), 0.0)
+    up[...] = masked.astype(BF)
+    up_t[...] = masked.T.astype(BF)
+    for b in range(4):
+        first = lax.rem(x + b, 4) * 2
+        for out, half in ((half_up, c), (send_up, 1 - c)):
+            cols = pl.ds(pl.multiple_of((first + half) * HD, HD), HD)
+            out[:, b * HD : (b + 1) * HD] = up[:, cols]
+
+
 def forward_kernel(scalars, normed, *refs):
     buffers = refs[:6]
-    pre_out, gate_out, natt_out, inv_out, mixed_out, pre, weights, sems, pre_sems = refs[6:]
+    pre, gate_out, natt_out, inv_out, mixed_out, weights, sems = refs[6:]
     copies = weight_copies(scalars, buffers, weights, sems)
     for pair in copies:
         start(pair)
     mask = score_mask(scalars[0])
     total = jnp.zeros((SEQ, HD), F32)
-    for h in range(HEADS):
-        if h % 2 == 0:
-            wait(copies[h // 2])
-        pre_a = dot(normed[...], columns(weights, 0, h))
-        pre_b = dot(normed[...], columns(weights, 1, h))
-        pre[h, :, :256] = pre_a
-        pre[h, :, 256:] = pre_b
-        pltpu.make_async_copy(pre.at[h], pre_out.at[h], pre_sems.at[h]).start()
-        act_a = pre_a * sigmoid(pre_a)
-        act_b = (pre_b * sigmoid(pre_b)).astype(BF)
-        gate_out[h] = act_a[:, :HD]
-        scores = dot(act_b[:, :HD], act_b[:, HD:], NT) * SCALE
-        attn = (scores * sigmoid(scores) * mask).astype(BF)
-        att = dot(attn, act_a[:, HD:].astype(BF))
-        natt_out[h] = att
-        total = total + att
+    last = None
+    for h in range(HEADS + 1):
+        now = None
+        if h < HEADS:
+            if h % 2 == 0:
+                wait(copies[h // 2])
+            pre_a = dot(normed[...], columns(weights, 0, h))
+            pre_b = dot(normed[...], columns(weights, 1, h))
+            pre[h, :, :256] = pre_a
+            pre[h, :, 256:] = pre_b
+            act_a = pre_a * sigmoid(pre_a)
+            act_b = (pre_b * sigmoid(pre_b)).astype(BF)
+            gate_out[h] = act_a[:, :HD]
+            now = act_b[:, :HD], act_b[:, HD:], act_a[:, HD:].astype(BF)
+        if h > 0:
+            query, key, val = last
+            scores = dot(query, key, NT) * SCALE
+            attn = (scores * sigmoid(scores) * mask).astype(BF)
+            att = dot(attn, val)
+            natt_out[h - 1] = att
+            total = total + att
+        last = now
     mean = row_mean(total)
     square = jnp.zeros((SEQ, HD), F32)
     for h in range(HEADS):
@@ -129,31 +155,25 @@
         natt = (natt_out[h] - mean) * inv
         natt_out[h] = natt
         mixed_out[h * HD : (h + 1) * HD, :] = (natt * gate_out[h]).T.astype(BF)
-    for h in range(HEADS):
-        pltpu.make_async_copy(pre.at[h], pre_out.at[h], pre_sems.at[h]).wait()
-
-
-def weight_kernel(mixed_t, other_mixed_t, up, other_up, out):
+
+
+def weight_kernel(mixed_t, other_mixed_t, up, other_up, *outs):
     total = dot(mixed_t[...], up[...]) + dot(other_mixed_t[...], other_up[...])
     total = total.astype(BF).reshape(32, 32, 4 * HD)
     for b in range(4):
         for k in range(2):
             part = total[:, k * 16 : (k + 1) * 16, b * HD : (b + 1) * HD]
-            out[b, :, :, k * HD : (k + 1) * HD] = part
+            outs[b][:, :, k * HD : (k + 1) * HD] = part
 
 
 def backward_kernel(
-    scalars, gate_in, natt_in, inv_in, upstream, normed_t, inv_t, up_t, pre_in, *refs
+    scalars, gate_in, natt_in, inv_in, upstream, normed_t, inv_t, up_t, pre, *refs
 ):
-    out, weights, out_w, pre, grad_mixed, grad_pre, grad_normed, sems, out_sems, pre_sems = refs[8:]
+    out, weights, out_w, grad_mixed, grad_pre, grad_normed, sems, out_sems = refs[8:]
     out_buffers = [*refs[0:2], refs[6], *refs[3:5], refs[7]]
     out_moves = block_copies(scalars, out_buffers, out_w, out_sems, 0, COLS, OUT)
     moves = weight_copies(scalars, refs[:6], weights, sems)
-    pre_moves = [
-        pltpu.make_async_copy(pre_in.at[h], pre.at[h], pre_sems.at[h]) for h in range(HEADS)
-    ]
     start(out_moves)
-    start(pre_moves)
     for pair in moves:
         start(pair)
     mask = score_mask(scalars[0])
@@ -169,24 +189,27 @@
         second = second + g * natt_in[h]
     first, second = row_mean(first), row_mean(second)
     inv = inv_in[:, :1]
-    for h in range(HEADS):
-        wait(pre_moves[h : h + 1])
-        natt = natt_in[h]
-        gm_h = grad_mixed[:, h * HD : (h + 1) * HD]
+
+    def products(h):
         pre_h = pre[h]
         sig = sigmoid(pre_h)
         act = pre_h * sig
         slope = sig + act * (1.0 - sig)
-        grad_att = (inv * (gm_h * act[:, :HD] - first - natt * second)).astype(BF)
+        gm_h = grad_mixed[:, h * HD : (h + 1) * HD]
+        grad_att = (inv * (gm_h * act[:, :HD] - first - natt_in[h] * second)).astype(BF)
         val, query, key = (act[:, k * HD : (k + 1) * HD].astype(BF) for k in (1, 2, 3))
         scores = dot(query, key, NT) * SCALE
+        grad_weights = dot(grad_att, val, NT)
+        return slope, grad_att, query, key, scores, grad_weights
+
+    def gradients(h, slope, grad_att, query, key, scores, grad_weights):
         sig_s = sigmoid(scores)
         act_s = scores * sig_s
         attn = (act_s * mask).astype(BF)
         slope_s = (sig_s + act_s * (1.0 - sig_s)) * (mask * SCALE)
-        grad_scores = (dot(grad_att, val, NT) * slope_s).astype(BF)
+        grad_scores = (grad_weights * slope_s).astype(BF)
         parts = [
-            gm_h * natt,
+            grad_mixed[:, h * HD : (h + 1) * HD] * natt_in[h],
             dot(attn, grad_att, TN),
             dot(grad_scores, key),
             dot(grad_scores, query, TN),
@@ -195,6 +218,12 @@
             part = parts[k] * slope[:, k * HD : (k + 1) * HD]
             at = h * 256 + k % 2 * HD
             grad_pre[k // 2, :, at : at + HD] = part.astype(BF)
+
+    last = products(0)
+    for h in range(HEADS):
+        following = products(h + 1) if h + 1 < HEADS else None
+        gradients(h, *last)
+        last = following
     for pair in moves:
         wait(pair)
     mean_1 = jnp.zeros((1, SEQ), F32)
@@ -207,14 +236,15 @@
         mean_1 = mean_1 + jnp.sum(gn, axis=0, keepdims=True)
         mean_2 = mean_2 + jnp.sum(gn * normed_t[rows, :], axis=0, keepdims=True)
     mean_1, mean_2 = mean_1 * (1.0 / WIDTH), mean_2 * (1.0 / WIDTH)
+    inv_row = inv_t[:1]
     for m in range(4):
         rows = slice(m * 256, (m + 1) * 256)
-        grad = inv_t[...] * (grad_normed[rows, :] - mean_1 - normed_t[rows, :] * mean_2)
+        grad = inv_row * (grad_normed[rows, :] - mean_1 - normed_t[rows, :] * mean_2)
         out[rows, :] = (grad + up_t[rows, :].astype(F32)).astype(BF)
 
 
 HI, LO = 32, 256
-BLOCK = 4
+BLOCK = 8
 
 
 def table_kernel(ids, rows, out, acc):
@@ -224,14 +254,13 @@
         left, right = [], []
         for k in range(BLOCK):
             n = i * BLOCK + k
-            hi, lo = ids[n, 0:1, :], ids[n, 1:2, :]
-            hot_hi = (lax.broadcasted_iota(jnp.int32, (HI, SEQ), 0) == hi).astype(F32).astype(BF)
-            hot_lo = (lax.broadcasted_iota(jnp.int32, (LO, SEQ), 0) == lo).astype(F32).astype(BF)
+            hi = jnp.broadcast_to(ids[n, 0:1, :].astype(BF), (32, SEQ))
+            lo = ids[n, 1:2, :]
             part = rows[n, :32, :]
             left.append(
-                jnp.concatenate([hot_hi[h : h + 1, :] * part for h in range(HI)], axis=0)
+                jnp.concatenate([jnp.where(hi == h, part, jnp.zeros((), BF)) for h in range(HI)], axis=0)
             )
-            right.append(hot_lo)
+            right.append((lax.broadcasted_iota(jnp.int32, (LO, SEQ), 0) == lo).astype(F32).astype(BF))
         acc[...] += dot(jnp.concatenate(left, axis=1), jnp.concatenate(right, axis=1), NT)
         return 0
 
@@ -243,13 +272,16 @@
 
 VMEM = pl.BlockSpec(memory_space=pltpu.VMEM)
 SMEM = pl.BlockSpec(memory_space=pltpu.SMEM)
-HBM = pl.BlockSpec(memory_space=pl.ANY)
-LIMIT = 56 * 1024 * 1024
-PARAMS = pltpu.CompilerParams(vmem_limit_bytes=LIMIT)
+HBM = pl.BlockSpec(memory_space=pltpu.HBM)
+
+
+def params(mebibytes):
+    return pltpu.CompilerParams(vmem_limit_bytes=mebibytes * 1024 * 1024)
+
+
 COST = pl.CostEstimate(flops=1024, bytes_accessed=1024, transcendentals=0)
 WEIGHT_SCRATCH = pltpu.VMEM((2, 8, 4, 32, COLS), BF)
 OUT_SCRATCH = pltpu.VMEM((2, 8, 4, 32, OUT), BF)
-PRE_SCRATCH = pltpu.VMEM((HEADS, SEQ, 4 * HD), F32)
 
 
 def shape(dims, dtype):
@@ -258,6 +290,26 @@
 
 def sems(count):
     return pltpu.SemaphoreType.DMA((count,))
+
+
+def prepare(scalars, events, cotangent):
+    return pl.pallas_call(
+        prepare_kernel,
+        out_shape=[
+            shape((SEQ, WIDTH), BF),
+            shape((WIDTH, SEQ), F32),
+            shape((8, SEQ), F32),
+            shape((SEQ, WIDTH), BF),
+            shape((WIDTH, SEQ), BF),
+            shape((SEQ, 4 * HD), BF),
+            shape((SEQ, 4 * HD), BF),
+        ],
+        in_specs=[SMEM, VMEM, VMEM],
+        out_specs=[VMEM] * 7,
+        compiler_params=params(16),
+        cost_estimate=COST,
+        name="prepare",
+    )(scalars, events, cotangent)
 
 
 def forward(scalars, normed, buffers):
@@ -271,9 +323,9 @@
             shape((WIDTH, SEQ), BF),
         ],
         in_specs=[SMEM, VMEM] + [HBM] * 6,
-        out_specs=[HBM] + [VMEM] * 4,
-        scratch_shapes=[PRE_SCRATCH, WEIGHT_SCRATCH, pltpu.SemaphoreType.DMA((PAIRS, 8)), sems(HEADS)],
-        compiler_params=PARAMS,
+        out_specs=[VMEM] * 5,
+        scratch_shapes=[WEIGHT_SCRATCH, pltpu.SemaphoreType.DMA((PAIRS, 8))],
+        compiler_params=params(22),
         cost_estimate=COST,
         name="forward",
     )(scalars, normed, *buffers)
@@ -282,10 +334,10 @@
 def weight_term(mixed, other_mixed, up, other_up):
     return pl.pallas_call(
         weight_kernel,
-        out_shape=shape((4, 32, 16, 2 * HD), BF),
+        out_shape=[shape((32, 16, 2 * HD), BF)] * 4,
         in_specs=[VMEM] * 4,
-        out_specs=VMEM,
-        compiler_params=PARAMS,
+        out_specs=[VMEM] * 4,
+        compiler_params=params(10),
         cost_estimate=COST,
         name="weight_term",
     )(mixed, other_mixed, up, other_up)
@@ -295,20 +347,18 @@
     return pl.pallas_call(
         backward_kernel,
         out_shape=shape((WIDTH, SEQ), BF),
-        in_specs=[SMEM] + [VMEM] * 7 + [HBM] * 9,
+        in_specs=[SMEM] + [VMEM] * 8 + [HBM] * 8,
         out_specs=VMEM,
         scratch_shapes=[
             WEIGHT_SCRATCH,
             OUT_SCRATCH,
-            PRE_SCRATCH,
             pltpu.VMEM((SEQ, WIDTH), F32),
             pltpu.VMEM((2, SEQ, COLS), BF),
             pltpu.VMEM((WIDTH, SEQ), F32),
             pltpu.SemaphoreType.DMA((PAIRS, 8)),
             sems(8),
-            sems(HEADS),
         ],
-        compiler_params=PARAMS,
+        compiler_params=params(32),
         cost_estimate=COST,
         name="backward",
     )(scalars, gate, natt, inv, upstream, normed_t, inv_t, up_t, pre, *buffers)
@@ -321,7 +371,7 @@
         in_specs=[VMEM, VMEM],
         out_specs=VMEM,
         scratch_shapes=[pltpu.VMEM((HI * 32, LO), F32)],
-        compiler_params=PARAMS,
+        compiler_params=params(16),
         cost_estimate=COST,
         name="table",
     )(ids, rows)
@@ -352,33 +402,20 @@
     return lax.optimization_barrier(values)
 
 
-def centre(values):
-    mean_val = jnp.mean(values, axis=-1, keepdims=True)
-    shifted = values - mean_val
-    scale_inv = lax.rsqrt(jnp.mean(shifted * shifted, axis=-1, keepdims=True) + EPSILON)
-    return (shifted * scale_inv, scale_inv)
-
-
 def per_device(events, item_ids, lengths, uvqk_weight, out_weight, cotangent):
-    zl, c = lax.axis_index("zl"), lax.axis_index("c")
+    zl, x, c = (lax.axis_index(name) for name in ("zl", "x", "c"))
     length = lengths[0]
-    scalars = jnp.stack([length, zl, c, 1 - 2 * lax.rem(zl + c, 2)]).astype(jnp.int32)
+    scalars = jnp.stack([length, zl, c, 1 - 2 * lax.rem(zl + c, 2), x]).astype(jnp.int32)
 
     kinds = lax.dynamic_slice_in_dim(uvqk_weight.reshape(32, 4, HEADS, HD), 2 * c, 2, 1)
     kinds = jnp.swapaxes(kinds, 1, 2).reshape(32, COLS)
     out_w = lax.dynamic_slice_in_dim(out_weight, c * OUT, OUT, 1)
     own = spread(jnp.concatenate([kinds, out_w], axis=1), "y", 8)
 
-    normed, inv_in = centre(events[0].astype(F32))
-    live = lax.broadcasted_iota(jnp.int32, (SEQ, 1), 0) < length
-    upstream = jnp.where(live, cotangent[0], jnp.zeros((), BF))
-    split = upstream.reshape(SEQ, 4, 2, HD)
-    half_up = lax.dynamic_slice_in_dim(split, c, 1, 2).reshape(SEQ, 4 * HD)
-    send_up = lax.dynamic_slice_in_dim(split, 1 - c, 1, 2).reshape(SEQ, 4 * HD)
-    normed_b, normed_t, up_t = normed.astype(BF), normed.T, upstream.T
-    own, normed_b, normed_t, up_t, half_up, send_up = tie(
-        own, normed_b, normed_t, up_t, half_up, send_up
+    normed, normed_t, inv_t, upstream, up_t, half_up, send_up = prepare(
+        scalars, events[0], cotangent[0]
     )
+    own, normed, send_up = tie(own, normed, send_up)
 
     near = to_z(own, 0)
     own_swapped = swap(own)
@@ -389,17 +426,19 @@
     far, near_swapped, out_w, other_up = tie(far, near_swapped, out_w, other_up)
     buffers = [own, near, far, own_swapped, near_swapped, swap(far)]
     out_far = to_z(out_w, 1)
-    pre, gate, natt, inv_att, mixed_t = forward(scalars, normed_b, buffers)
+    pre, gate, natt, inv_att, mixed_t = forward(scalars, normed, buffers)
     mixed_t, out_far = tie(mixed_t, out_far)
     out_w = [out_far, swap(out_far)]
-    part = weight_term(mixed_t, swap(mixed_t), half_up, other_up)
-    part, natt = tie(part, natt)
-    part = lax.all_to_all(part, "x", 0, 0, tiled=True)
+    parts = weight_term(mixed_t, swap(mixed_t), half_up, other_up)
+    *parts, natt = tie(*parts, natt)
+    parts = [parts[0]] + [
+        lax.ppermute(parts[k], "x", [(i, (i + k) % 4) for i in range(4)]) for k in (1, 2, 3)
+    ]
     rows_t = backward(
-        scalars, gate, natt, inv_att, upstream, normed_t, inv_in.T, up_t, pre, buffers + out_w
+        scalars, gate, natt, inv_att, upstream, normed_t, inv_t, up_t, pre, buffers + out_w
     )
-    part, rows_t = tie(part, rows_t)
-    part = jnp.sum(part.astype(F32), axis=0).astype(BF)
+    *parts, rows_t = tie(*parts, rows_t)
+    part = sum(part.astype(F32) for part in parts).astype(BF)
     digits = jnp.concatenate([item_ids // LO, item_ids % LO, jnp.zeros((6, SEQ), jnp.int32)])
     digits = jnp.broadcast_to(digits.astype(BF)[None], (32, 8, SEQ))
     both = jnp.concatenate([rows_t.reshape(32, 32, SEQ), part, digits], axis=1)

time: 207 us -> 191 us (0.923)
  Pallas kernels: 36.5 us -> 23.5 us
  starting transfers between devices: 55.6 us -> 63.3 us
  other arithmetic: 7.68 us -> 0.66 us
  local copies, waits for them, and re-layouts: 13.2 us -> 8.28 us
  waiting for transfers between devices: 62.8 us -> 66.3 us
  blocking collectives: 27.9 us -> 25.2 us
    ppermute x0 -> x3, starting transfers between devices: none -> 10.1 us  [per_device(): lax.ppermute(parts[k], 'x', [(i, (i + k) % 4) for i in range(4)])]
    pallas_call x1, Pallas kernels: 14.5 us -> 8.68 us  [backward(): pl.pallas_call(backward_kernel, out_shape=shape((WIDTH, SEQ), BF), in_spe...]
    pallas_call x1, Pallas kernels: 10.6 us -> 6.46 us  [forward(): pl.pallas_call(forward_kernel, out_shape=[shape((HEADS, SEQ, 4 * HD), F32...]
    all_to_all x1 -> x0, starting transfers between devices: 4.15 us -> none  [per_device(): part = lax.all_to_all(part, 'x', 0, 0, tiled=True)]
    all_to_all x2, starting transfers between devices: 16.2 us -> 19.5 us  [spread(): return lax.all_to_all(many, axes, 0, 0, tiled=True)]
    all_to_all x1, blocking collectives: 27.9 us -> 25.2 us  [per_device(): both = lax.all_to_all(both, COL, 0, 0, tiled=True)]
    pallas_call x1, Pallas kernels: 8.36 us -> 6.25 us  [table_sum(): pl.pallas_call(table_kernel, out_shape=shape((32, ITEMS), F32), in_specs=...]
    unnamed x31 -> x25, local copies, waits for them, and re-layouts: 6.69 us -> 5.07 us
  transfers between devices with their start and end apart: 12 -> 14, of which waited for: 8 -> 7; matrix products, arithmetic and copies ran while one was open for 5% -> 0% of each run, Pallas kernels for 16% -> 12%
where the time goes in v3:
time: 191 us; the launch traced here: 189 us
  waiting for transfers between devices  66.3 us (35%)
  starting transfers between devices  63.3 us (33%)
  blocking collectives  25.2 us (13%)
  Pallas kernels  23.5 us (12%)
  local copies, waits for them, and re-layouts  8.28 us (4%)
    all_to_all x2, waiting for transfers between devices, spread(): return lax.all_to_all(many, axes, 0, 0, tiled=True)  33.5 us
    ppermute x3, waiting for transfers between devices, to_z(): return lax.ppermute(value, ('zl', 'zh', 'c'), pairs)  29.3 us
    all_to_all x1, blocking collectives, per_device(): both = lax.all_to_all(both, COL, 0, 0, tiled=True)  25.2 us
    all_to_all x2, starting transfers between devices, spread(): return lax.all_to_all(many, axes, 0, 0, tiled=True)  19.5 us
    ppermute x6, starting transfers between devices, swap(): return lax.ppermute(value, 'c', [(0, 1), (1, 0)])  19.1 us
    ppermute x3, starting transfers between devices, to_z(): return lax.ppermute(value, ('zl', 'zh', 'c'), pairs)  14.6 us
    ppermute x3, starting transfers between devices, per_device(): lax.ppermute(parts[k], 'x', [(i, (i + k) % 4) for i in range(4)])  10.1 us
    pallas_call x1, Pallas kernels, backward(): pl.pallas_call(backward_kernel, out_shape=shape((WIDTH, SEQ), BF), in_spe...  8.68 us
  transfers between devices with their start and end apart: 14, of which 7 were waited for; matrix products, arithmetic and copies ran while one was open for 0% of the time, Pallas kernels for 12%

profile of v3, /device:TPU:1, one launch (start us, length us, event | category | flops | bytes accessed | tf_op | source)
XLA Modules:
  0.0 189.0 jit_solution(13175908356276075410)
XLA Ops:
  0.6 0.0 copy-start
  0.7 1.0 copy.13
  1.7 0.1 copy.10
  1.8 0.1 reshape.41
  1.9 0.0 copy-done
  2.0 0.0 copy-start.1
  2.0 1.2 broadcast_in_dim.10
  3.1 7.7 %all-to-all-start = ((bf16[8,32,2560]{2,1,0:T(8,128)(2,1)}), bf16[8,32,2560]{2,1,0:T(8,128)(2,1)S(1)}, u32[]{:S(2)}, u32[]{:S(2)}) async-start(bf16[8,32,2560]{2,1,0:T(8,128)(2,1)} %broadcast_in_dim.10), calls=%async_computation | async-start | bytes 2621440 | tf_op jit(solution)/shard_map/all_to_all | solution.py:398
  11.4 0.1 stack.37.scalars
  11.5 0.0 copy-done.1
  11.5 1.0 copy-done.2
  12.6 1.4 prepare.1
  14.0 0.0 copy-start.3
  14.0 0.8 copy-done.3
  14.8 0.8 copy-done.5
  15.6 0.7 copy-done.7
  16.3 0.7 copy-done.9
  17.0 28.6 %all-to-all-done.refs_0_ = bf16[8,32,2560]{2,1,0:T(8,128)(2,1)S(1)} async-done(((bf16[8,32,2560]{2,1,0:T(8,128)(2,1)}), bf16[8,32,2560]{2,1,0:T(8,128)(2,1)S(1)}, u32[]{:S(2)}, u32[]{:S(2)}) %all-to-all-start) | async-done | bytes 1310752 | tf_op jit(solution)/shard_map/all_to_all | solution.py:398
  45.6 10.7 %collective-permute-start = (bf16[8,32,2560]{2,1,0:T(8,128)(2,1)S(1)}, bf16[8,32,2560]{2,1,0:T(8,128)(2,1)S(1)}, u32[]{:S(2)}, u32[]{:S(2)}) collective-permute-start(bf16[8,32,2560]{2,1,0:T(8,128)(2,1)S(1)} %all-to-all-done.refs_0_), channel_id=1, source_target_pairs={{0,16},{1,57},{16,0},{17,33},{32,48},{33,17},{48,32},{49,9},{8,24}... | collective-permute-start | bytes 3932168 | tf_op jit(solution)/shard_map/ppermute | solution.py:389
  56.4 1.9 %collective-permute-start.1 = (bf16[8,32,2560]{2,1,0:T(8,128)(2,1)S(1)}, bf16[8,32,2560]{2,1,0:T(8,128)(2,1)S(1)}, u32[]{:S(2)}, u32[]{:S(2)}) collective-permute-start(bf16[8,32,2560]{2,1,0:T(8,128)(2,1)S(1)} %all-to-all-done.refs_0_), channel_id=1, source_target_pairs={{0,1},{1,0},{2,3},{3,2},{4,5},{5,4},{6,7},{7,6},{8,9},{9,8},{10,11... | collective-permute-start | bytes 3932168 | tf_op jit(solution)/shard_map/ppermute | solution.py:393
  58.3 0.1 slice_bitcast_fusion.1
  58.4 12.9 %collective-permute-done.refs_1_ = bf16[8,32,2560]{2,1,0:T(8,128)(2,1)S(1)} collective-permute-done((bf16[8,32,2560]{2,1,0:T(8,128)(2,1)S(1)}, bf16[8,32,2560]{2,1,0:T(8,128)(2,1)S(1)}, u32[]{:S(2)}, u32[]{:S(2)}) %collective-permute-start) | collective-permute-done | bytes 1310752 | tf_op jit(solution)/shard_map/ppermute | solution.py:389
  71.3 0.0 collective-permute-done.1.refs_3_
  71.3 0.1 slice_bitcast_fusion
  71.5 0.0 copy-start.10
  71.5 0.2 pad_maximum_fusion
  71.7 1.9 %collective-permute-start.2 = (bf16[2,8,32,2048]{3,2,1,0:T(8,128)(2,1)S(1)}, bf16[2,8,32,2048]{3,2,1,0:T(8,128)(2,1)S(1)}, u32[]{:S(2)}, u32[]{:S(2)}) collective-permute-start(bf16[2,8,32,2048]{3,2,1,0:T(8,128)(2,1)S(1)} %pad_maximum_fusion), channel_id=1, source_target_pairs={{0,56},{1,17},{16,32},{17,1},{32,16},{33,49},{48,8},{49,33},{8,48}... | collective-permute-start | bytes 6291464 | tf_op jit(solution)/shard_map/ppermute | solution.py:389
  73.6 5.3 %collective-permute-start.3 = (bf16[8,32,2560]{2,1,0:T(8,128)(2,1)S(1)}, bf16[8,32,2560]{2,1,0:T(8,128)(2,1)S(1)}, u32[]{:S(2)}, u32[]{:S(2)}) collective-permute-start(bf16[8,32,2560]{2,1,0:T(8,128)(2,1)S(1)} %collective-permute-done.refs_1_), channel_id=1, source_target_pairs={{0,1},{1,0},{2,3},{3,2},{4,5},{5,4},{6,7},{7,6},{8,9},{9,8},{10,11... | collective-permute-start | bytes 3932168 | tf_op jit(solution)/shard_map/ppermute | solution.py:393
  78.9 0.0 copy-done.10
  78.9 1.9 %collective-permute-start.4 = (bf16[256,512]{1,0:T(8,128)(2,1)S(1)}, bf16[256,512]{1,0:T(8,128)(2,1)S(1)}, u32[]{:S(2)}, u32[]{:S(2)}) collective-permute-start(bf16[256,512]{1,0:T(8,128)(2,1)S(1)} %copy-done.10), channel_id=1, source_target_pairs={{0,1},{1,0},{2,3},{3,2},{4,5},{5,4},{6,7},{7,6},{8,9},{9,8},{10,11... | collective-permute-start | bytes 786440 | tf_op jit(solution)/shard_map/ppermute | solution.py:393
  80.9 0.1 pad_maximum_fusion.2
  80.9 0.0 copy-start.11
  81.0 1.4 collective-permute-done.4.other_up
  82.3 0.0 collective-permute-done.3.refs_4_
  82.4 16.4 %collective-permute-done.2.refs_2_ = bf16[2,8,32,2048]{3,2,1,0:T(8,128)(2,1)S(1)} collective-permute-done((bf16[2,8,32,2048]{3,2,1,0:T(8,128)(2,1)S(1)}, bf16[2,8,32,2048]{3,2,1,0:T(8,128)(2,1)S(1)}, u32[]{:S(2)}, u32[]{:S(2)}) %collective-permute-start.2) | collective-permute-done | bytes 2097184 | tf_op jit(solution)/shard_map/ppermute | solution.py:389
  98.7 4.1 %collective-permute-start.5 = (bf16[2,8,32,2048]{3,2,1,0:T(8,128)(2,1)S(1)}, bf16[2,8,32,2048]{3,2,1,0:T(8,128)(2,1)S(1)}, u32[]{:S(2)}, u32[]{:S(2)}) collective-permute-start(bf16[2,8,32,2048]{3,2,1,0:T(8,128)(2,1)S(1)} %collective-permute-done.2.refs_2_), channel_id=1, source_target_pairs={{0,1},{1,0},{2,3},{3,2},{4,5},{5,4},{6,7},{7,6},{8,9},{9,8},{10,11... | collective-permute-start | bytes 6291464 | tf_op jit(solution)/shard_map/ppermute | solution.py:393
  102.9 1.9 %collective-permute-start.6 = (bf16[2,8,32,512]{3,2,1,0:T(8,128)(2,1)S(1)}, bf16[2,8,32,512]{3,2,1,0:T(8,128)(2,1)S(1)}, u32[]{:S(2)}, u32[]{:S(2)}) collective-permute-start(bf16[2,8,32,512]{3,2,1,0:T(8,128)(2,1)S(1)} %pad_maximum_fusion.2), channel_id=1, source_target_pairs={{0,56},{1,17},{16,32},{17,1},{32,16},{33,49},{48,8},{49,33},{8,48}... | collective-permute-start | bytes 1572872 | tf_op jit(solution)/shard_map/ppermute | solution.py:389
  104.8 1.8 collective-permute-done.5.refs_5_
  106.6 6.5 %forward.1 = (f32[8,256,512]{2,1,0:T(8,128)S(1)}, f32[8,256,128]{2,1,0:T(8,128)S(1)}, f32[8,256,128]{2,1,0:T(8,128)S(1)}, f32[256,128]{1,0:T(8,128)S(1)}, bf16[1024,256]{1,0:T(8,128)(2,1)S(1)}) custom-call(s32[5]{0:T(128)S(1)} %stack.37.scalars, bf16[256,1024]{1,0:T(8,128)(2,1)S(1)} %get-tuple-element.45.normed, ...), custom_call_target="tpu_custom_call" | custom-call | flops 1024 | bytes 1024 | tf_op jit(solution)/shard_map/forward/pallas_call | solution.py:316
  113.1 0.0 copy-start.4
  113.1 0.0 collective-permute-done.6.refs_6_
  113.1 3.9 %collective-permute-start.7 = (bf16[1024,256]{1,0:T(8,128)(2,1)S(1)}, bf16[1024,256]{1,0:T(8,128)(2,1)S(1)}, u32[]{:S(2)}, u32[]{:S(2)}) collective-permute-start(bf16[1024,256]{1,0:T(8,128)(2,1)S(1)} %get-tuple-element.55.mixed_t), channel_id=1, source_target_pairs={{0,1},{1,0},{2,3},{3,2},{4,5},{5,4},{6,7},{7,6},{8,9},{9,8},{10,11... | collective-permute-start | bytes 1572872 | tf_op jit(solution)/shard_map/ppermute | solution.py:393
  117.1 1.9 %collective-permute-start.11 = (bf16[2,8,32,512]{3,2,1,0:T(8,128)(2,1)S(1)}, bf16[2,8,32,512]{3,2,1,0:T(8,128)(2,1)S(1)}, u32[]{:S(2)}, u32[]{:S(2)}) collective-permute-start(bf16[2,8,32,512]{3,2,1,0:T(8,128)(2,1)S(1)} %collective-permute-done.6.refs_6_), channel_id=1, source_target_pairs={{0,1},{1,0},{2,3},{3,2},{4,5},{5,4},{6,7},{7,6},{8,9},{9,8},{10,11... | collective-permute-start | bytes 1572872 | tf_op jit(solution)/shard_map/ppermute | solution.py:393
  119.0 0.0 collective-permute-done.7.other_mixed_t
  119.0 0.7 weight_term.1
  119.8 4.4 %collective-permute-start.10 = (bf16[32,16,256]{2,1,0:T(8,128)(2,1)S(1)}, bf16[32,16,256]{2,1,0:T(8,128)(2,1)S(1)}, u32[]{:S(2)}, u32[]{:S(2)}) collective-permute-start(bf16[32,16,256]{2,1,0:T(8,128)(2,1)S(1)} %get-tuple-element.66), channel_id=1, source_target_pairs={{0,6},{2,0},{4,2},{6,4},{1,7},{3,1},{5,3},{7,5},{8,14},{10,8},{12,... | collective-permute-start | bytes 786440 | tf_op jit(solution)/shard_map/ppermute | solution.py:435
  124.2 1.9 %collective-permute-start.8 = (bf16[32,16,256]{2,1,0:T(8,128)(2,1)S(1)}, bf16[32,16,256]{2,1,0:T(8,128)(2,1)S(1)}, u32[]{:S(2)}, u32[]{:S(2)}) collective-permute-start(bf16[32,16,256]{2,1,0:T(8,128)(2,1)S(1)} %get-tuple-element.64), channel_id=1, source_target_pairs={{0,2},{2,4},{4,6},{6,0},{1,3},{3,5},{5,7},{7,1},{8,10},{10,12},{12... | collective-permute-start | bytes 786440 | tf_op jit(solution)/shard_map/ppermute | solution.py:435
  126.1 3.8 %collective-permute-start.9 = (bf16[32,16,256]{2,1,0:T(8,128)(2,1)S(1)}, bf16[32,16,256]{2,1,0:T(8,128)(2,1)S(1)}, u32[]{:S(2)}, u32[]{:S(2)}) collective-permute-start(bf16[32,16,256]{2,1,0:T(8,128)(2,1)S(1)} %get-tuple-element.65), channel_id=1, source_target_pairs={{0,4},{2,6},{4,0},{6,2},{1,5},{3,7},{5,1},{7,3},{8,12},{10,14},{12... | collective-permute-start | bytes 786440 | tf_op jit(solution)/shard_map/ppermute | solution.py:435
  129.9 0.1 pad.7.clone
  130.0 0.1 maximum_maximum_fusion
  130.1 0.0 collective-permute-done.11.refs_7_
  130.1 0.0 copy-done.6
  130.1 8.7 %backward.1 = bf16[1024,256]{1,0:T(8,128)(2,1)S(1)} custom-call(s32[5]{0:T(128)S(1)} %stack.37.scalars, f32[8,256,128]{2,1,0:T(8,128)S(1)} %get-tuple-element.67.gate_in, f32[8,256,128]{2,1,0:T(8,128)S(1)} %get-tuple-element.68.natt_in, f32[256,128]{1,0:T(8,128)S(1)} %get-tuple-element.69.inv_in, bf16[256,1024]{1,0:T(8,128)(2,1)S(1)} %copy-done.4, ...), custom_call_target="tpu_custom_call" | custom-call | flops 1024 | bytes 1024 | tf_op jit(solution)/shard_map/backward/pallas_call | solution.py:347
  138.8 0.0 collective-permute-done.10
  138.8 0.0 collective-permute-done.8
  138.8 0.2 collective-permute-done.9
  139.0 0.1 add_convert_fusion
  139.2 0.1 pad_maximum_fusion.1
  139.3 25.2 %all_to_all.15.rows = bf16[32,56,256]{2,1,0:T(8,128)(2,1)S(1)} all-to-all(bf16[32,56,256]{2,1,0:T(8,128)(2,1)S(1)} %pad_maximum_fusion.1), channel_id=1, replica_groups=mesh['y'=8,'zl'=4,'zh'=2,'x'=4,'c'=2] {'y','zl'}, dimensions={0} | all-to-all | bytes 1835008 | tf_op jit(solution)/shard_map/all_to_all | solution.py:445
  164.6 0.7 broadcast_in_dim.28
  165.3 11.9 %all-to-all-start.2 = ((f32[16,32,128]{2,1,0:T(8,128)}), f32[16,32,128]{2,1,0:T(8,128)S(1)}, u32[]{:S(2)}, u32[]{:S(2)}) async-start(f32[16,32,128]{2,1,0:T(8,128)} %broadcast_in_dim.28), calls=%async_computation.2 | async-start | bytes 524288 | tf_op jit(solution)/shard_map/all_to_all | solution.py:398
  177.2 6.2 %table.1 = f32[32,8192]{1,0:T(8,128)} custom-call(s32[32,8,256]{2,1,0:T(8,128)S(1)} %slice_convert_fusion.ids, bf16[32,56,256]{2,1,0:T(8,128)(2,1)S(1)} %all_to_all.15.rows), custom_call_target="tpu_custom_call" | custom-call | flops 1024 | bytes 1024 | tf_op jit(solution)/shard_map/table/pallas_call | solution.py:368
  183.5 4.8 %all-to-all-done.2 = f32[16,32,128]{2,1,0:T(8,128)S(1)} async-done(((f32[16,32,128]{2,1,0:T(8,128)}), f32[16,32,128]{2,1,0:T(8,128)S(1)}, u32[]{:S(2)}, u32[]{:S(2)}) %all-to-all-start.2) | async-done | bytes 262176 | tf_op jit(solution)/shard_map/all_to_all | solution.py:398
  188.3 0.7 copy_bitcast_fusion
  (23 shorter events, 0.2 us)
Async XLA Ops:
  0.6 1.3 copy-start
  2.0 9.6 %copy-start.1 = (bf16[1,256,1024]{2,1,0:T(8,128)(2,1)S(1)}, bf16[1,256,1024]{2,1,0:T(8,128)(2,1)}, u32[]{:S(2)}) copy-start(bf16[1,256,1024]{2,1,0:T(8,128)(2,1)} %param.6) | copy-start | bytes 1572868
  3.1 42.5 %all-to-all-start = ((bf16[8,32,2560]{2,1,0:T(8,128)(2,1)}), bf16[8,32,2560]{2,1,0:T(8,128)(2,1)S(1)}, u32[]{:S(2)}, u32[]{:S(2)}) async-start(bf16[8,32,2560]{2,1,0:T(8,128)(2,1)} %broadcast_in_dim.10), calls=%async_computation | async-start | bytes 2621440 | tf_op jit(solution)/shard_map/all_to_all | solution.py:398
  11.5 1.0 copy-start.2
  14.0 0.8 copy-start.3
  14.8 0.8 copy-start.5
  15.6 0.7 copy-start.7
  16.3 0.7 copy-start.9
  45.6 25.7 %collective-permute-start = (bf16[8,32,2560]{2,1,0:T(8,128)(2,1)S(1)}, bf16[8,32,2560]{2,1,0:T(8,128)(2,1)S(1)}, u32[]{:S(2)}, u32[]{:S(2)}) collective-permute-start(bf16[8,32,2560]{2,1,0:T(8,128)(2,1)S(1)} %all-to-all-done.refs_0_), channel_id=1, source_target_pairs={{0,16},{1,57},{16,0},{17,33},{32,48},{33,17},{48,32},{49,9},{8,24}... | collective-permute-start | bytes 3932168 | tf_op jit(solution)/shard_map/ppermute | solution.py:389
  56.4 15.0 %collective-permute-start.1 = (bf16[8,32,2560]{2,1,0:T(8,128)(2,1)S(1)}, bf16[8,32,2560]{2,1,0:T(8,128)(2,1)S(1)}, u32[]{:S(2)}, u32[]{:S(2)}) collective-permute-start(bf16[8,32,2560]{2,1,0:T(8,128)(2,1)S(1)} %all-to-all-done.refs_0_), channel_id=1, source_target_pairs={{0,1},{1,0},{2,3},{3,2},{4,5},{5,4},{6,7},{7,6},{8,9},{9,8},{10,11... | collective-permute-start | bytes 3932168 | tf_op jit(solution)/shard_map/ppermute | solution.py:393
  71.5 7.5 %copy-start.10 = (bf16[256,512]{1,0:T(8,128)(2,1)S(1)}, bf16[256,512]{1,0:T(8,128)(2,1)}, u32[]{:S(2)}) copy-start(bf16[256,512]{1,0:T(8,128)(2,1)} %copy-done.9) | copy-start | bytes 786436
  71.7 27.1 %collective-permute-start.2 = (bf16[2,8,32,2048]{3,2,1,0:T(8,128)(2,1)S(1)}, bf16[2,8,32,2048]{3,2,1,0:T(8,128)(2,1)S(1)}, u32[]{:S(2)}, u32[]{:S(2)}) collective-permute-start(bf16[2,8,32,2048]{3,2,1,0:T(8,128)(2,1)S(1)} %pad_maximum_fusion), channel_id=1, source_target_pairs={{0,56},{1,17},{16,32},{17,1},{32,16},{33,49},{48,8},{49,33},{8,48}... | collective-permute-start | bytes 6291464 | tf_op jit(solution)/shard_map/ppermute | solution.py:389
  73.6 8.8 %collective-permute-start.3 = (bf16[8,32,2560]{2,1,0:T(8,128)(2,1)S(1)}, bf16[8,32,2560]{2,1,0:T(8,128)(2,1)S(1)}, u32[]{:S(2)}, u32[]{:S(2)}) collective-permute-start(bf16[8,32,2560]{2,1,0:T(8,128)(2,1)S(1)} %collective-permute-done.refs_1_), channel_id=1, source_target_pairs={{0,1},{1,0},{2,3},{3,2},{4,5},{5,4},{6,7},{7,6},{8,9},{9,8},{10,11... | collective-permute-start | bytes 3932168 | tf_op jit(solution)/shard_map/ppermute | solution.py:393
  78.9 3.4 %collective-permute-start.4 = (bf16[256,512]{1,0:T(8,128)(2,1)S(1)}, bf16[256,512]{1,0:T(8,128)(2,1)S(1)}, u32[]{:S(2)}, u32[]{:S(2)}) collective-permute-start(bf16[256,512]{1,0:T(8,128)(2,1)S(1)} %copy-done.10), channel_id=1, source_target_pairs={{0,1},{1,0},{2,3},{3,2},{4,5},{5,4},{6,7},{7,6},{8,9},{9,8},{10,11... | collective-permute-start | bytes 786440 | tf_op jit(solution)/shard_map/ppermute | solution.py:393
  80.9 38.1 %copy-start.11 = (s32[1,256]{1,0:T(1,128)S(1)}, s32[1,256]{1,0:T(1,128)}, u32[]{:S(2)}) copy-start(s32[1,256]{1,0:T(1,128)} %param.7) | copy-start | bytes 3076
  80.9 38.1 %copy-start.8 = (bf16[256,512]{1,0:T(8,128)(2,1)S(1)}, bf16[256,512]{1,0:T(8,128)(2,1)}, u32[]{:S(2)}) copy-start(bf16[256,512]{1,0:T(8,128)(2,1)} %copy-done.7) | copy-start | bytes 786436
  98.7 7.9 %collective-permute-start.5 = (bf16[2,8,32,2048]{3,2,1,0:T(8,128)(2,1)S(1)}, bf16[2,8,32,2048]{3,2,1,0:T(8,128)(2,1)S(1)}, u32[]{:S(2)}, u32[]{:S(2)}) collective-permute-start(bf16[2,8,32,2048]{3,2,1,0:T(8,128)(2,1)S(1)} %collective-permute-done.2.refs_2_), channel_id=1, source_target_pairs={{0,1},{1,0},{2,3},{3,2},{4,5},{5,4},{6,7},{7,6},{8,9},{9,8},{10,11... | collective-permute-start | bytes 6291464 | tf_op jit(solution)/shard_map/ppermute | solution.py:393
  102.9 10.3 %collective-permute-start.6 = (bf16[2,8,32,512]{3,2,1,0:T(8,128)(2,1)S(1)}, bf16[2,8,32,512]{3,2,1,0:T(8,128)(2,1)S(1)}, u32[]{:S(2)}, u32[]{:S(2)}) collective-permute-start(bf16[2,8,32,512]{3,2,1,0:T(8,128)(2,1)S(1)} %pad_maximum_fusion.2), channel_id=1, source_target_pairs={{0,56},{1,17},{16,32},{17,1},{32,16},{33,49},{48,8},{49,33},{8,48}... | collective-permute-start | bytes 1572872 | tf_op jit(solution)/shard_map/ppermute | solution.py:389
  113.1 17.0 %copy-start.4 = (bf16[256,1024]{1,0:T(8,128)(2,1)S(1)}, bf16[256,1024]{1,0:T(8,128)(2,1)}, u32[]{:S(2)}) copy-start(bf16[256,1024]{1,0:T(8,128)(2,1)} %copy-done.3) | copy-start | bytes 1572868
  113.1 17.0 %copy-start.6 = (bf16[1024,256]{1,0:T(8,128)(2,1)S(1)}, bf16[1024,256]{1,0:T(8,128)(2,1)}, u32[]{:S(2)}) copy-start(bf16[1024,256]{1,0:T(8,128)(2,1)} %copy-done.5) | copy-start | bytes 1572868
  113.1 5.9 %collective-permute-start.7 = (bf16[1024,256]{1,0:T(8,128)(2,1)S(1)}, bf16[1024,256]{1,0:T(8,128)(2,1)S(1)}, u32[]{:S(2)}, u32[]{:S(2)}) collective-permute-start(bf16[1024,256]{1,0:T(8,128)(2,1)S(1)} %get-tuple-element.55.mixed_t), channel_id=1, source_target_pairs={{0,1},{1,0},{2,3},{3,2},{4,5},{5,4},{6,7},{7,6},{8,9},{9,8},{10,11... | collective-permute-start | bytes 1572872 | tf_op jit(solution)/shard_map/ppermute | solution.py:393
  117.1 13.0 %collective-permute-start.11 = (bf16[2,8,32,512]{3,2,1,0:T(8,128)(2,1)S(1)}, bf16[2,8,32,512]{3,2,1,0:T(8,128)(2,1)S(1)}, u32[]{:S(2)}, u32[]{:S(2)}) collective-permute-start(bf16[2,8,32,512]{3,2,1,0:T(8,128)(2,1)S(1)} %collective-permute-done.6.refs_6_), channel_id=1, source_target_pairs={{0,1},{1,0},{2,3},{3,2},{4,5},{5,4},{6,7},{7,6},{8,9},{9,8},{10,11... | collective-permute-start | bytes 1572872 | tf_op jit(solution)/shard_map/ppermute | solution.py:393
  119.8 19.0 %collective-permute-start.10 = (bf16[32,16,256]{2,1,0:T(8,128)(2,1)S(1)}, bf16[32,16,256]{2,1,0:T(8,128)(2,1)S(1)}, u32[]{:S(2)}, u32[]{:S(2)}) collective-permute-start(bf16[32,16,256]{2,1,0:T(8,128)(2,1)S(1)} %get-tuple-element.66), channel_id=1, source_target_pairs={{0,6},{2,0},{4,2},{6,4},{1,7},{3,1},{5,3},{7,5},{8,14},{10,8},{12,... | collective-permute-start | bytes 786440 | tf_op jit(solution)/shard_map/ppermute | solution.py:435
  124.2 14.6 %collective-permute-start.8 = (bf16[32,16,256]{2,1,0:T(8,128)(2,1)S(1)}, bf16[32,16,256]{2,1,0:T(8,128)(2,1)S(1)}, u32[]{:S(2)}, u32[]{:S(2)}) collective-permute-start(bf16[32,16,256]{2,1,0:T(8,128)(2,1)S(1)} %get-tuple-element.64), channel_id=1, source_target_pairs={{0,2},{2,4},{4,6},{6,0},{1,3},{3,5},{5,7},{7,1},{8,10},{10,12},{12... | collective-permute-start | bytes 786440 | tf_op jit(solution)/shard_map/ppermute | solution.py:435
  126.1 12.9 %collective-permute-start.9 = (bf16[32,16,256]{2,1,0:T(8,128)(2,1)S(1)}, bf16[32,16,256]{2,1,0:T(8,128)(2,1)S(1)}, u32[]{:S(2)}, u32[]{:S(2)}) collective-permute-start(bf16[32,16,256]{2,1,0:T(8,128)(2,1)S(1)} %get-tuple-element.65), channel_id=1, source_target_pairs={{0,4},{2,6},{4,0},{6,2},{1,5},{3,7},{5,1},{7,3},{8,12},{10,14},{12... | collective-permute-start | bytes 786440 | tf_op jit(solution)/shard_map/ppermute | solution.py:435
  165.3 23.0 %all-to-all-start.2 = ((f32[16,32,128]{2,1,0:T(8,128)}), f32[16,32,128]{2,1,0:T(8,128)S(1)}, u32[]{:S(2)}, u32[]{:S(2)}) async-start(f32[16,32,128]{2,1,0:T(8,128)} %broadcast_in_dim.28), calls=%async_computation.2 | async-start | bytes 524288 | tf_op jit(solution)/shard_map/all_to_all | solution.py:398

commit v4 on v3

--- a/solution.py
+++ b/solution.py
@@ -46,6 +46,7 @@
 
 
 COLS = HEADS * 256
+SIDE = COLS // 2
 OUT = 512
 PAIRS = 4
 PAIR = 512
@@ -54,24 +55,27 @@
 ORDER = (0, 1, -1, -2)
 
 
-def block_copies(scalars, buffers, part, sems, at, first, size):
+def block_copies(scalars, buffers, part, sems, side, at, first, size):
     zl, c, sz = scalars[1], scalars[2], scalars[3]
+    place = lax.rem(scalars[5] + side, 2)
+    cols, to = slice(first, first + size), slice(at, at + size)
     copies = []
     for core in range(2):
         half, sign = (c, sz) if core == 0 else (1 - c, -sz)
         own, near, far = buffers[core * 3 : core * 3 + 3]
-        cols = slice(first, first + size)
-        blocks = [own.at[:, :, cols], near.at[:, :, cols]]
-        blocks += [far.at[k, :, :, at : at + size] for k in range(2)]
+        blocks = [own.at[place, :, :, cols], near.at[place, :, :, cols]]
+        blocks += [far.at[k, place, :, :, to] for k in range(2)]
         for block, by in zip(blocks, ORDER):
-            dst = part.at[half, :, lax.rem(zl + 8 + by * sign, 4), :, at : at + size]
+            dst = part.at[half, side, :, lax.rem(zl + 8 + by * sign, 4), :, to]
             copies.append(pltpu.make_async_copy(block, dst, sems.at[len(copies)]))
     return copies
 
 
 def weight_copies(scalars, buffers, weights, sems):
     return [
-        block_copies(scalars, buffers, weights, sems.at[n], n * PAIR, n * PAIR, PAIR)
+        block_copies(
+            scalars, buffers, weights, sems.at[n], n // 2, n % 2 * PAIR, n % 2 * PAIR, PAIR
+        )
         for n in range(PAIRS)
     ]
 
@@ -87,7 +91,8 @@
 
 
 def columns(weights, half, head):
-    return weights[half, :, :, :, head * 256 : (head + 1) * 256].reshape(WIDTH, 256)
+    at = head % 4 * 256
+    return weights[half, head // 4, :, :, :, at : at + 256].reshape(WIDTH, 256)
 
 
 def row_mean(value):
@@ -171,15 +176,20 @@
 ):
     out, weights, out_w, grad_mixed, grad_pre, grad_normed, sems, out_sems = refs[8:]
     out_buffers = [*refs[0:2], refs[6], *refs[3:5], refs[7]]
-    out_moves = block_copies(scalars, out_buffers, out_w, out_sems, 0, COLS, OUT)
+    out_moves = []
+    for side in range(2):
+        args = out_w, out_sems.at[side], side, 0, SIDE, OUT // 2
+        out_moves += block_copies(scalars, out_buffers, *args)
     moves = weight_copies(scalars, refs[:6], weights, sems)
     start(out_moves)
     for pair in moves:
         start(pair)
     mask = score_mask(scalars[0])
     wait(out_moves)
-    gm = dot(upstream[:, :OUT], out_w[0].reshape(WIDTH, OUT), NT)
-    gm = gm + dot(upstream[:, OUT:], out_w[1].reshape(WIDTH, OUT), NT)
+    gm = jnp.zeros((SEQ, WIDTH), F32)
+    for b in range(4):
+        cols = slice(b * OUT // 2, (b + 1) * OUT // 2)
+        gm = gm + dot(upstream[:, cols], out_w[b // 2, b % 2].reshape(WIDTH, OUT // 2), NT)
     grad_mixed[...] = gm
     first = jnp.zeros((SEQ, HD), F32)
     second = jnp.zeros((SEQ, HD), F32)
@@ -230,8 +240,10 @@
     mean_2 = jnp.zeros((1, SEQ), F32)
     for m in range(4):
         rows = slice(m * 256, (m + 1) * 256)
-        left, right = (weights[k, 2 * m : 2 * m + 2].reshape(256, COLS) for k in range(2))
-        gn = dot(left, grad_pre[0], NT) + dot(right, grad_pre[1], NT)
+        gn = jnp.zeros((256, SEQ), F32)
+        for b in range(4):
+            left = weights[b // 2, b % 2, 2 * m : 2 * m + 2].reshape(256, SIDE)
+            gn = gn + dot(left, grad_pre[b // 2, :, b % 2 * SIDE : (b % 2 + 1) * SIDE], NT)
         grad_normed[rows, :] = gn
         mean_1 = mean_1 + jnp.sum(gn, axis=0, keepdims=True)
         mean_2 = mean_2 + jnp.sum(gn * normed_t[rows, :], axis=0, keepdims=True)
@@ -280,8 +292,8 @@
 
 
 COST = pl.CostEstimate(flops=1024, bytes_accessed=1024, transcendentals=0)
-WEIGHT_SCRATCH = pltpu.VMEM((2, 8, 4, 32, COLS), BF)
-OUT_SCRATCH = pltpu.VMEM((2, 8, 4, 32, OUT), BF)
+WEIGHT_SCRATCH = pltpu.VMEM((2, 2, 8, 4, 32, SIDE), BF)
+OUT_SCRATCH = pltpu.VMEM((2, 2, 8, 4, 32, OUT // 2), BF)
 
 
 def shape(dims, dtype):
@@ -356,7 +368,7 @@
             pltpu.VMEM((2, SEQ, COLS), BF),
             pltpu.VMEM((WIDTH, SEQ), F32),
             pltpu.SemaphoreType.DMA((PAIRS, 8)),
-            sems(8),
+            pltpu.SemaphoreType.DMA((2, 8)),
         ],
         compiler_params=params(32),
         cost_estimate=COST,
@@ -389,6 +401,13 @@
     return lax.ppermute(value, ("zl", "zh", "c"), pairs)
 
 
+def to_x(value):
+    pairs = [
+        (x * 2 + c, (x + (1 - 2 * ((x + c) % 2))) % 4 * 2 + c) for x in range(4) for c in range(2)
+    ]
+    return lax.ppermute(value, ("x", "c"), pairs)
+
+
 def swap(value):
     return lax.ppermute(value, "c", [(0, 1), (1, 0)])
 
@@ -405,11 +424,14 @@
 def per_device(events, item_ids, lengths, uvqk_weight, out_weight, cotangent):
     zl, x, c = (lax.axis_index(name) for name in ("zl", "x", "c"))
     length = lengths[0]
-    scalars = jnp.stack([length, zl, c, 1 - 2 * lax.rem(zl + c, 2), x]).astype(jnp.int32)
+    scalars = jnp.stack([length, zl, c, 1 - 2 * lax.rem(zl + c, 2), x, lax.rem(x, 2)])
+    scalars = scalars.astype(jnp.int32)
 
     kinds = lax.dynamic_slice_in_dim(uvqk_weight.reshape(32, 4, HEADS, HD), 2 * c, 2, 1)
     kinds = jnp.swapaxes(kinds, 1, 2).reshape(32, COLS)
-    out_w = lax.dynamic_slice_in_dim(out_weight, c * OUT, OUT, 1)
+    side = lax.rem(x, 2)
+    out_w = lax.dynamic_slice_in_dim(out_weight, c * OUT + side * OUT // 2, OUT // 2, 1)
+    kinds = lax.dynamic_slice_in_dim(kinds, side * SIDE, SIDE, 1)
     own = spread(jnp.concatenate([kinds, out_w], axis=1), "y", 8)
 
     normed, normed_t, inv_t, upstream, up_t, half_up, send_up = prepare(
@@ -417,13 +439,18 @@
     )
     own, normed, send_up = tie(own, normed, send_up)
 
-    near = to_z(own, 0)
+    near, beside = tie(to_z(own, 0), to_x(own))
+    near_beside = to_z(beside, 0)
+    near = jnp.stack([near, near_beside])
+    near, own, beside, send_up = tie(near, own, beside, send_up)
+    own = jnp.stack([own, beside])
     own_swapped = swap(own)
-    near, own_swapped, send_up = tie(near, own_swapped, send_up)
-    far = to_z(jnp.stack([own[:, :, :COLS], near[:, :, :COLS]]), 1)
+    far = to_z(jnp.stack([own[..., :SIDE], near[..., :SIDE]]), 1)
     near_swapped, other_up = swap(near), swap(send_up)
-    out_w = jnp.stack([own[:, :, COLS:], near[:, :, COLS:]])
-    far, near_swapped, out_w, other_up = tie(far, near_swapped, out_w, other_up)
+    out_w = jnp.stack([own[..., SIDE:], near[..., SIDE:]])
+    far, own_swapped, near_swapped, out_w, other_up = tie(
+        far, own_swapped, near_swapped, out_w, other_up
+    )
     buffers = [own, near, far, own_swapped, near_swapped, swap(far)]
     out_far = to_z(out_w, 1)
     pre, gate, natt, inv_att, mixed_t = forward(scalars, normed, buffers)

time: 191 us -> 187 us (0.979)
  waiting for transfers between devices: 66.3 us -> 55.1 us
  starting transfers between devices: 63.3 us -> 68.4 us
  other arithmetic: 0.66 us -> 4.07 us
  local copies, waits for them, and re-layouts: 8.28 us -> 5.39 us
    all_to_all x2, waiting for transfers between devices: 33.5 us -> 19.1 us  [spread(): return lax.all_to_all(many, axes, 0, 0, tiled=True)]
    ppermute x3 -> x4, starting transfers between devices: 14.6 us -> 19.5 us  [to_z(): return lax.ppermute(value, ('zl', 'zh', 'c'), pairs)]
    ppermute x0 -> x1, waiting for transfers between devices: none -> 4.58 us  [to_x(): return lax.ppermute(value, ('x', 'c'), pairs)]
    ppermute x0 -> x1, starting transfers between devices: none -> 4.39 us  [to_x(): return lax.ppermute(value, ('x', 'c'), pairs)]
    ppermute x6, starting transfers between devices: 19.1 us -> 15.6 us  [swap(): return lax.ppermute(value, 'c', [(0, 1), (1, 0)])]
    another operation x4 -> x8, other arithmetic: 0.27 us -> 3.68 us  [the longest x2 1.34 us: per_device(): far = to_z(jnp.stack([own[..., :SIDE], near[..., :SIDE]]), 1)]
    unnamed x25 -> x17, local copies, waits for them, and re-layouts: 5.07 us -> 2.52 us
    ppermute x3 -> x4, waiting for transfers between devices: 29.3 us -> 29.4 us  [to_z(): return lax.ppermute(value, ('zl', 'zh', 'c'), pairs)]
  transfers between devices with their start and end apart: 14 -> 16, of which waited for: 7 -> 8; matrix products, arithmetic and copies ran while one was open for 0% -> 1% of each run, Pallas kernels for 12% -> 13%
where the time goes in v4:
time: 187 us; the launch traced here: 185 us
  starting transfers between devices  68.4 us (37%)
  waiting for transfers between devices  55.1 us (29%)
  blocking collectives  26.9 us (14%)
  Pallas kernels  23.7 us (13%)
  local copies, waits for them, and re-layouts  5.39 us (3%)
  other arithmetic  4.07 us (2%)
    ppermute x4, waiting for transfers between devices, to_z(): return lax.ppermute(value, ('zl', 'zh', 'c'), pairs)  29.4 us
    all_to_all x1, blocking collectives, per_device(): both = lax.all_to_all(both, COL, 0, 0, tiled=True)  26.9 us
    ppermute x4, starting transfers between devices, to_z(): return lax.ppermute(value, ('zl', 'zh', 'c'), pairs)  19.5 us
    all_to_all x2, waiting for transfers between devices, spread(): return lax.all_to_all(many, axes, 0, 0, tiled=True)  19.1 us
    all_to_all x2, starting transfers between devices, spread(): return lax.all_to_all(many, axes, 0, 0, tiled=True)  18.3 us
    ppermute x6, starting transfers between devices, swap(): return lax.ppermute(value, 'c', [(0, 1), (1, 0)])  15.6 us
    ppermute x3, starting transfers between devices, per_device(): lax.ppermute(parts[k], 'x', [(i, (i + k) % 4) for i in range(4)])  10.6 us
    pallas_call x1, Pallas kernels, backward(): pl.pallas_call(backward_kernel, out_shape=shape((WIDTH, SEQ), BF), in_spe...  8.88 us
  transfers between devices with their start and end apart: 16, of which 8 were waited for; matrix products, arithmetic and copies ran while one was open for 1% of the time, Pallas kernels for 13%

profile of v4, /device:TPU:1, one launch (start us, length us, event | category | flops | bytes accessed | tf_op | source)
XLA Modules:
  0.0 185.3 jit_solution(3277460762538467743)
XLA Ops:
  0.6 0.0 copy-start
  0.7 1.0 copy.13
  1.7 0.1 copy.10
  1.8 0.0 copy-start.1
  1.8 0.0 copy-start.2
  1.8 0.1 reshape.41
  1.9 0.1 constant_dynamic-slice_fusion
  2.0 0.9 broadcast_in_dim.10
  2.9 7.7 %all-to-all-start = ((bf16[8,32,1280]{2,1,0:T(8,128)(2,1)}), bf16[8,32,1280]{2,1,0:T(8,128)(2,1)}, u32[]{:S(2)}, u32[]{:S(2)}) async-start(bf16[8,32,1280]{2,1,0:T(8,128)(2,1)} %broadcast_in_dim.10), calls=%async_computation | async-start | bytes 1310720 | tf_op jit(solution)/shard_map/all_to_all | solution.py:417
  11.2 0.1 stack.59.scalars
  11.3 0.0 copy-done.2
  11.3 1.4 prepare.1
  12.8 0.8 copy-done.3
  13.5 0.7 copy-done.5
  14.2 14.2 %all-to-all-done = bf16[8,32,1280]{2,1,0:T(8,128)(2,1)} async-done(((bf16[8,32,1280]{2,1,0:T(8,128)(2,1)}), bf16[8,32,1280]{2,1,0:T(8,128)(2,1)}, u32[]{:S(2)}, u32[]{:S(2)}) %all-to-all-start) | async-done | bytes 655392 | tf_op jit(solution)/shard_map/all_to_all | solution.py:417
  28.5 13.7 %collective-permute-start = (bf16[8,32,1280]{2,1,0:T(8,128)(2,1)}, bf16[8,32,1280]{2,1,0:T(8,128)(2,1)S(1)}, u32[]{:S(2)}, u32[]{:S(2)}) collective-permute-start(bf16[8,32,1280]{2,1,0:T(8,128)(2,1)} %all-to-all-done), channel_id=1, source_target_pairs={{0,16},{1,57},{16,0},{17,33},{32,48},{33,17},{48,32},{49,9},{8,24}... | collective-permute-start | bytes 1966088 | tf_op jit(solution)/shard_map/ppermute | solution.py:401
  42.1 4.4 %collective-permute-start.1 = (bf16[8,32,1280]{2,1,0:T(8,128)(2,1)}, bf16[8,32,1280]{2,1,0:T(8,128)(2,1)S(1)}, u32[]{:S(2)}, u32[]{:S(2)}) collective-permute-start(bf16[8,32,1280]{2,1,0:T(8,128)(2,1)} %all-to-all-done), channel_id=1, source_target_pairs={{0,2},{1,7},{2,0},{3,5},{4,6},{5,3},{6,4},{7,1},{8,10},{9,15},{10,... | collective-permute-start | bytes 1966088 | tf_op jit(solution)/shard_map/ppermute | solution.py:408
  46.5 3.8 %collective-permute-done = bf16[8,32,1280]{2,1,0:T(8,128)(2,1)S(1)} collective-permute-done((bf16[8,32,1280]{2,1,0:T(8,128)(2,1)}, bf16[8,32,1280]{2,1,0:T(8,128)(2,1)S(1)}, u32[]{:S(2)}, u32[]{:S(2)}) %collective-permute-start) | collective-permute-done | bytes 655392 | tf_op jit(solution)/shard_map/ppermute | solution.py:401
  50.3 4.6 %collective-permute-done.1 = bf16[8,32,1280]{2,1,0:T(8,128)(2,1)S(1)} collective-permute-done((bf16[8,32,1280]{2,1,0:T(8,128)(2,1)}, bf16[8,32,1280]{2,1,0:T(8,128)(2,1)S(1)}, u32[]{:S(2)}, u32[]{:S(2)}) %collective-permute-start.1) | collective-permute-done | bytes 655392 | tf_op jit(solution)/shard_map/ppermute | solution.py:408
  54.9 1.9 %collective-permute-start.2 = (bf16[8,32,1280]{2,1,0:T(8,128)(2,1)S(1)}, bf16[8,32,1280]{2,1,0:T(8,128)(2,1)S(1)}, u32[]{:S(2)}, u32[]{:S(2)}) collective-permute-start(bf16[8,32,1280]{2,1,0:T(8,128)(2,1)S(1)} %collective-permute-done.1), channel_id=1, source_target_pairs={{0,16},{1,57},{16,0},{17,33},{32,48},{33,17},{48,32},{49,9},{8,24}... | collective-permute-start | bytes 1966088 | tf_op jit(solution)/shard_map/ppermute | solution.py:401
  56.8 10.6 %collective-permute-done.2 = bf16[8,32,1280]{2,1,0:T(8,128)(2,1)S(1)} collective-permute-done((bf16[8,32,1280]{2,1,0:T(8,128)(2,1)S(1)}, bf16[8,32,1280]{2,1,0:T(8,128)(2,1)S(1)}, u32[]{:S(2)}, u32[]{:S(2)}) %collective-permute-start.2) | collective-permute-done | bytes 655392 | tf_op jit(solution)/shard_map/ppermute | solution.py:401
  67.4 0.1 pad_maximum_fusion.2.refs_1_
  67.5 0.1 slice_bitcast_fusion
  67.7 1.1 fusion.1
  68.8 0.2 pad_maximum_fusion
  69.0 2.1 %collective-permute-start.3 = (bf16[2,2,8,32,1024]{4,3,2,1,0:T(8,128)(2,1)S(1)}, bf16[2,2,8,32,1024]{4,3,2,1,0:T(8,128)(2,1)S(1)}, u32[]{:S(2)}, u32[]{:S(2)}) collective-permute-start(bf16[2,2,8,32,1024]{4,3,2,1,0:T(8,128)(2,1)S(1)} %pad_maximum_fusion), channel_id=1, source_target_pairs={{0,56},{1,17},{16,32},{17,1},{32,16},{33,49},{48,8},{49,33},{8,48}... | collective-permute-start | bytes 6291464 | tf_op jit(solution)/shard_map/ppermute | solution.py:401
  71.1 1.2 pad_maximum_fusion.1.refs_0_
  72.3 3.1 %collective-permute-start.4 = (bf16[2,8,32,1280]{3,2,1,0:T(8,128)(2,1)S(1)}, bf16[2,8,32,1280]{3,2,1,0:T(8,128)(2,1)S(1)}, u32[]{:S(2)}, u32[]{:S(2)}) collective-permute-start(bf16[2,8,32,1280]{3,2,1,0:T(8,128)(2,1)S(1)} %pad_maximum_fusion.1.refs_0_), channel_id=1, source_target_pairs={{0,1},{1,0},{2,3},{3,2},{4,5},{5,4},{6,7},{7,6},{8,9},{9,8},{10,11... | collective-permute-start | bytes 3932168 | tf_op jit(solution)/shard_map/ppermute | solution.py:412
  75.4 1.9 %collective-permute-start.5 = (bf16[2,8,32,1280]{3,2,1,0:T(8,128)(2,1)S(1)}, bf16[2,8,32,1280]{3,2,1,0:T(8,128)(2,1)S(1)}, u32[]{:S(2)}, u32[]{:S(2)}) collective-permute-start(bf16[2,8,32,1280]{3,2,1,0:T(8,128)(2,1)S(1)} %pad_maximum_fusion.2.refs_1_), channel_id=1, source_target_pairs={{0,1},{1,0},{2,3},{3,2},{4,5},{5,4},{6,7},{7,6},{8,9},{9,8},{10,11... | collective-permute-start | bytes 3932168 | tf_op jit(solution)/shard_map/ppermute | solution.py:412
  77.3 2.4 %collective-permute-start.6 = (bf16[256,512]{1,0:T(8,128)(2,1)S(1)}, bf16[256,512]{1,0:T(8,128)(2,1)S(1)}, u32[]{:S(2)}, u32[]{:S(2)}) collective-permute-start(bf16[256,512]{1,0:T(8,128)(2,1)S(1)} %copy-done.6), channel_id=1, source_target_pairs={{0,1},{1,0},{2,3},{3,2},{4,5},{5,4},{6,7},{7,6},{8,9},{9,8},{10,11... | collective-permute-start | bytes 786440 | tf_op jit(solution)/shard_map/ppermute | solution.py:412
  79.8 0.9 fusion.3
  80.7 0.1 pad_maximum_fusion.4
  80.8 0.0 copy-start.7
  80.8 0.1 collective-permute-done.6.other_up
  80.9 0.0 collective-permute-done.4.refs_3_
  80.9 0.0 collective-permute-done.5.refs_4_
  80.9 15.0 %collective-permute-done.3.refs_2_ = bf16[2,2,8,32,1024]{4,3,2,1,0:T(8,128)(2,1)S(1)} collective-permute-done((bf16[2,2,8,32,1024]{4,3,2,1,0:T(8,128)(2,1)S(1)}, bf16[2,2,8,32,1024]{4,3,2,1,0:T(8,128)(2,1)S(1)}, u32[]{:S(2)}, u32[]{:S(2)}) %collective-permute-start.3) | collective-permute-done | bytes 2097184 | tf_op jit(solution)/shard_map/ppermute | solution.py:401
  95.9 2.2 %collective-permute-start.7 = (bf16[2,2,8,32,1024]{4,3,2,1,0:T(8,128)(2,1)S(1)}, bf16[2,2,8,32,1024]{4,3,2,1,0:T(8,128)(2,1)S(1)}, u32[]{:S(2)}, u32[]{:S(2)}) collective-permute-start(bf16[2,2,8,32,1024]{4,3,2,1,0:T(8,128)(2,1)S(1)} %collective-permute-done.3.refs_2_), channel_id=1, source_target_pairs={{0,1},{1,0},{2,3},{3,2},{4,5},{5,4},{6,7},{7,6},{8,9},{9,8},{10,11... | collective-permute-start | bytes 6291464 | tf_op jit(solution)/shard_map/ppermute | solution.py:412
  98.2 1.9 %collective-permute-start.8 = (bf16[2,2,8,32,256]{4,3,2,1,0:T(8,128)(2,1)S(1)}, bf16[2,2,8,32,256]{4,3,2,1,0:T(8,128)(2,1)S(1)}, u32[]{:S(2)}, u32[]{:S(2)}) collective-permute-start(bf16[2,2,8,32,256]{4,3,2,1,0:T(8,128)(2,1)S(1)} %pad_maximum_fusion.4), channel_id=1, source_target_pairs={{0,56},{1,17},{16,32},{17,1},{32,16},{33,49},{48,8},{49,33},{8,48}... | collective-permute-start | bytes 1572872 | tf_op jit(solution)/shard_map/ppermute | solution.py:401
  100.1 1.9 %collective-permute-done.7.refs_5_ = bf16[2,2,8,32,1024]{4,3,2,1,0:T(8,128)(2,1)S(1)} collective-permute-done((bf16[2,2,8,32,1024]{4,3,2,1,0:T(8,128)(2,1)S(1)}, bf16[2,2,8,32,1024]{4,3,2,1,0:T(8,128)(2,1)S(1)}, u32[]{:S(2)}, u32[]{:S(2)}) %collective-permute-start.7) | collective-permute-done | bytes 2097184 | tf_op jit(solution)/shard_map/ppermute | solution.py:412
  102.0 6.5 %forward.1 = (f32[8,256,512]{2,1,0:T(8,128)S(1)}, f32[8,256,128]{2,1,0:T(8,128)S(1)}, f32[8,256,128]{2,1,0:T(8,128)S(1)}, f32[256,128]{1,0:T(8,128)S(1)}, bf16[1024,256]{1,0:T(8,128)(2,1)S(1)}) custom-call(s32[6]{0:T(128)S(1)} %stack.59.scalars, bf16[256,1024]{1,0:T(8,128)(2,1)S(1)} %get-tuple-element.49.normed, ...), custom_call_target="tpu_custom_call" | custom-call | flops 1024 | bytes 1024 | tf_op jit(solution)/shard_map/forward/pallas_call | solution.py:328
  108.5 0.0 collective-permute-done.8.refs_6_
  108.5 4.1 %collective-permute-start.9 = (bf16[1024,256]{1,0:T(8,128)(2,1)S(1)}, bf16[1024,256]{1,0:T(8,128)(2,1)S(1)}, u32[]{:S(2)}, u32[]{:S(2)}) collective-permute-start(bf16[1024,256]{1,0:T(8,128)(2,1)S(1)} %get-tuple-element.63.mixed_t), channel_id=1, source_target_pairs={{0,1},{1,0},{2,3},{3,2},{4,5},{5,4},{6,7},{7,6},{8,9},{9,8},{10,11... | collective-permute-start | bytes 1572872 | tf_op jit(solution)/shard_map/ppermute | solution.py:412
  112.5 1.9 %collective-permute-start.13 = (bf16[2,2,8,32,256]{4,3,2,1,0:T(8,128)(2,1)S(1)}, bf16[2,2,8,32,256]{4,3,2,1,0:T(8,128)(2,1)S(1)}, u32[]{:S(2)}, u32[]{:S(2)}) collective-permute-start(bf16[2,2,8,32,256]{4,3,2,1,0:T(8,128)(2,1)S(1)} %collective-permute-done.8.refs_6_), channel_id=1, source_target_pairs={{0,1},{1,0},{2,3},{3,2},{4,5},{5,4},{6,7},{7,6},{8,9},{9,8},{10,11... | collective-permute-start | bytes 1572872 | tf_op jit(solution)/shard_map/ppermute | solution.py:412
  114.5 0.0 collective-permute-done.9.other_mixed_t
  114.5 0.7 weight_term.1
  115.2 3.0 %collective-permute-start.10 = (bf16[32,16,256]{2,1,0:T(8,128)(2,1)S(1)}, bf16[32,16,256]{2,1,0:T(8,128)(2,1)S(1)}, u32[]{:S(2)}, u32[]{:S(2)}) collective-permute-start(bf16[32,16,256]{2,1,0:T(8,128)(2,1)S(1)} %get-tuple-element.72), channel_id=1, source_target_pairs={{0,2},{2,4},{4,6},{6,0},{1,3},{3,5},{5,7},{7,1},{8,10},{10,12},{12... | collective-permute-start | bytes 786440 | tf_op jit(solution)/shard_map/ppermute | solution.py:462
  118.2 4.5 %collective-permute-start.11 = (bf16[32,16,256]{2,1,0:T(8,128)(2,1)S(1)}, bf16[32,16,256]{2,1,0:T(8,128)(2,1)S(1)}, u32[]{:S(2)}, u32[]{:S(2)}) collective-permute-start(bf16[32,16,256]{2,1,0:T(8,128)(2,1)S(1)} %get-tuple-element.73), channel_id=1, source_target_pairs={{0,4},{2,6},{4,0},{6,2},{1,5},{3,7},{5,1},{7,3},{8,12},{10,14},{12... | collective-permute-start | bytes 786440 | tf_op jit(solution)/shard_map/ppermute | solution.py:462
  122.7 3.1 %collective-permute-start.12 = (bf16[32,16,256]{2,1,0:T(8,128)(2,1)S(1)}, bf16[32,16,256]{2,1,0:T(8,128)(2,1)S(1)}, u32[]{:S(2)}, u32[]{:S(2)}) collective-permute-start(bf16[32,16,256]{2,1,0:T(8,128)(2,1)S(1)} %get-tuple-element.74), channel_id=1, source_target_pairs={{0,6},{2,0},{4,2},{6,4},{1,7},{3,1},{5,3},{7,5},{8,14},{10,8},{12,... | collective-permute-start | bytes 786440 | tf_op jit(solution)/shard_map/ppermute | solution.py:462
  125.8 0.1 pad.7.clone
  125.9 0.1 maximum_maximum_fusion
  126.0 0.0 collective-permute-done.13.refs_7_
  126.0 8.9 %backward.1 = bf16[1024,256]{1,0:T(8,128)(2,1)S(1)} custom-call(s32[6]{0:T(128)S(1)} %stack.59.scalars, f32[8,256,128]{2,1,0:T(8,128)S(1)} %get-tuple-element.75.gate_in, f32[8,256,128]{2,1,0:T(8,128)S(1)} %get-tuple-element.76.natt_in, f32[256,128]{1,0:T(8,128)S(1)} %get-tuple-element.77.inv_in, bf16[256,1024]{1,0:T(8,128)(2,1)S(1)} %get-tuple-element.78.upstream, ...), custom_call_target="tpu_custom_call" | custom-call | flops 1024 | bytes 1024 | tf_op jit(solution)/shard_map/backward/pallas_call | solution.py:359
  134.9 0.0 collective-permute-done.10
  134.9 0.0 collective-permute-done.11
  134.9 0.0 collective-permute-done.12
  134.9 0.1 add_convert_fusion
  135.1 0.1 pad_maximum_fusion.3
  135.1 26.9 %all_to_all.15.rows = bf16[32,56,256]{2,1,0:T(8,128)(2,1)S(1)} all-to-all(bf16[32,56,256]{2,1,0:T(8,128)(2,1)S(1)} %pad_maximum_fusion.3), channel_id=1, replica_groups=mesh['y'=8,'zl'=4,'zh'=2,'x'=4,'c'=2] {'y','zl'}, dimensions={0} | all-to-all | bytes 1835008 | tf_op jit(solution)/shard_map/all_to_all | solution.py:472
  162.2 0.7 broadcast_in_dim.28
  162.9 10.6 %all-to-all-start.2 = ((f32[16,32,128]{2,1,0:T(8,128)}), f32[16,32,128]{2,1,0:T(8,128)S(1)}, u32[]{:S(2)}, u32[]{:S(2)}) async-start(f32[16,32,128]{2,1,0:T(8,128)} %broadcast_in_dim.28), calls=%async_computation.2 | async-start | bytes 524288 | tf_op jit(solution)/shard_map/all_to_all | solution.py:417
  173.5 6.2 %table.1 = f32[32,8192]{1,0:T(8,128)} custom-call(s32[32,8,256]{2,1,0:T(8,128)S(1)} %slice_convert_fusion.ids, bf16[32,56,256]{2,1,0:T(8,128)(2,1)S(1)} %all_to_all.15.rows), custom_call_target="tpu_custom_call" | custom-call | flops 1024 | bytes 1024 | tf_op jit(solution)/shard_map/table/pallas_call | solution.py:380
  179.8 4.8 %all-to-all-done.2 = f32[16,32,128]{2,1,0:T(8,128)S(1)} async-done(((f32[16,32,128]{2,1,0:T(8,128)}), f32[16,32,128]{2,1,0:T(8,128)S(1)}, u32[]{:S(2)}, u32[]{:S(2)}) %all-to-all-start.2) | async-done | bytes 262176 | tf_op jit(solution)/shard_map/all_to_all | solution.py:417
  184.6 0.7 copy_bitcast_fusion
  (21 shorter events, 0.2 us)
Async XLA Ops:
  0.6 1.3 copy-start
  1.8 9.5 %copy-start.1 = (bf16[1,256,1024]{2,1,0:T(8,128)(2,1)S(1)}, bf16[1,256,1024]{2,1,0:T(8,128)(2,1)}, u32[]{:S(2)}) copy-start(bf16[1,256,1024]{2,1,0:T(8,128)(2,1)} %param.6) | copy-start | bytes 1572868
  1.8 9.5 %copy-start.2 = (bf16[1,256,1024]{2,1,0:T(8,128)(2,1)S(1)}, bf16[1,256,1024]{2,1,0:T(8,128)(2,1)}, u32[]{:S(2)}) copy-start(bf16[1,256,1024]{2,1,0:T(8,128)(2,1)} %param.11) | copy-start | bytes 1572868
  2.9 25.5 %all-to-all-start = ((bf16[8,32,1280]{2,1,0:T(8,128)(2,1)}), bf16[8,32,1280]{2,1,0:T(8,128)(2,1)}, u32[]{:S(2)}, u32[]{:S(2)}) async-start(bf16[8,32,1280]{2,1,0:T(8,128)(2,1)} %broadcast_in_dim.10), calls=%async_computation | async-start | bytes 1310720 | tf_op jit(solution)/shard_map/all_to_all | solution.py:417
  12.7 0.8 copy-start.3
  13.5 0.7 copy-start.5
  28.5 21.8 %collective-permute-start = (bf16[8,32,1280]{2,1,0:T(8,128)(2,1)}, bf16[8,32,1280]{2,1,0:T(8,128)(2,1)S(1)}, u32[]{:S(2)}, u32[]{:S(2)}) collective-permute-start(bf16[8,32,1280]{2,1,0:T(8,128)(2,1)} %all-to-all-done), channel_id=1, source_target_pairs={{0,16},{1,57},{16,0},{17,33},{32,48},{33,17},{48,32},{49,9},{8,24}... | collective-permute-start | bytes 1966088 | tf_op jit(solution)/shard_map/ppermute | solution.py:401
  42.1 12.8 %collective-permute-start.1 = (bf16[8,32,1280]{2,1,0:T(8,128)(2,1)}, bf16[8,32,1280]{2,1,0:T(8,128)(2,1)S(1)}, u32[]{:S(2)}, u32[]{:S(2)}) collective-permute-start(bf16[8,32,1280]{2,1,0:T(8,128)(2,1)} %all-to-all-done), channel_id=1, source_target_pairs={{0,2},{1,7},{2,0},{3,5},{4,6},{5,3},{6,4},{7,1},{8,10},{9,15},{10,... | collective-permute-start | bytes 1966088 | tf_op jit(solution)/shard_map/ppermute | solution.py:408
  54.9 12.5 %collective-permute-start.2 = (bf16[8,32,1280]{2,1,0:T(8,128)(2,1)S(1)}, bf16[8,32,1280]{2,1,0:T(8,128)(2,1)S(1)}, u32[]{:S(2)}, u32[]{:S(2)}) collective-permute-start(bf16[8,32,1280]{2,1,0:T(8,128)(2,1)S(1)} %collective-permute-done.1), channel_id=1, source_target_pairs={{0,16},{1,57},{16,0},{17,33},{32,48},{33,17},{48,32},{49,9},{8,24}... | collective-permute-start | bytes 1966088 | tf_op jit(solution)/shard_map/ppermute | solution.py:401
  69.0 8.3 %copy-start.6 = (bf16[256,512]{1,0:T(8,128)(2,1)S(1)}, bf16[256,512]{1,0:T(8,128)(2,1)}, u32[]{:S(2)}) copy-start(bf16[256,512]{1,0:T(8,128)(2,1)} %copy-done.5) | copy-start | bytes 786436
  69.0 26.9 %collective-permute-start.3 = (bf16[2,2,8,32,1024]{4,3,2,1,0:T(8,128)(2,1)S(1)}, bf16[2,2,8,32,1024]{4,3,2,1,0:T(8,128)(2,1)S(1)}, u32[]{:S(2)}, u32[]{:S(2)}) collective-permute-start(bf16[2,2,8,32,1024]{4,3,2,1,0:T(8,128)(2,1)S(1)} %pad_maximum_fusion), channel_id=1, source_target_pairs={{0,56},{1,17},{16,32},{17,1},{32,16},{33,49},{48,8},{49,33},{8,48}... | collective-permute-start | bytes 6291464 | tf_op jit(solution)/shard_map/ppermute | solution.py:401
  72.3 8.6 %collective-permute-start.4 = (bf16[2,8,32,1280]{3,2,1,0:T(8,128)(2,1)S(1)}, bf16[2,8,32,1280]{3,2,1,0:T(8,128)(2,1)S(1)}, u32[]{:S(2)}, u32[]{:S(2)}) collective-permute-start(bf16[2,8,32,1280]{3,2,1,0:T(8,128)(2,1)S(1)} %pad_maximum_fusion.1.refs_0_), channel_id=1, source_target_pairs={{0,1},{1,0},{2,3},{3,2},{4,5},{5,4},{6,7},{7,6},{8,9},{9,8},{10,11... | collective-permute-start | bytes 3932168 | tf_op jit(solution)/shard_map/ppermute | solution.py:412
  75.4 5.5 %collective-permute-start.5 = (bf16[2,8,32,1280]{3,2,1,0:T(8,128)(2,1)S(1)}, bf16[2,8,32,1280]{3,2,1,0:T(8,128)(2,1)S(1)}, u32[]{:S(2)}, u32[]{:S(2)}) collective-permute-start(bf16[2,8,32,1280]{3,2,1,0:T(8,128)(2,1)S(1)} %pad_maximum_fusion.2.refs_1_), channel_id=1, source_target_pairs={{0,1},{1,0},{2,3},{3,2},{4,5},{5,4},{6,7},{7,6},{8,9},{9,8},{10,11... | collective-permute-start | bytes 3932168 | tf_op jit(solution)/shard_map/ppermute | solution.py:412
  77.3 3.6 %collective-permute-start.6 = (bf16[256,512]{1,0:T(8,128)(2,1)S(1)}, bf16[256,512]{1,0:T(8,128)(2,1)S(1)}, u32[]{:S(2)}, u32[]{:S(2)}) collective-permute-start(bf16[256,512]{1,0:T(8,128)(2,1)S(1)} %copy-done.6), channel_id=1, source_target_pairs={{0,1},{1,0},{2,3},{3,2},{4,5},{5,4},{6,7},{7,6},{8,9},{9,8},{10,11... | collective-permute-start | bytes 786440 | tf_op jit(solution)/shard_map/ppermute | solution.py:412
  80.8 33.7 %copy-start.7 = (s32[1,256]{1,0:T(1,128)S(1)}, s32[1,256]{1,0:T(1,128)}, u32[]{:S(2)}) copy-start(s32[1,256]{1,0:T(1,128)} %param.7) | copy-start | bytes 3076
  95.9 6.0 %collective-permute-start.7 = (bf16[2,2,8,32,1024]{4,3,2,1,0:T(8,128)(2,1)S(1)}, bf16[2,2,8,32,1024]{4,3,2,1,0:T(8,128)(2,1)S(1)}, u32[]{:S(2)}, u32[]{:S(2)}) collective-permute-start(bf16[2,2,8,32,1024]{4,3,2,1,0:T(8,128)(2,1)S(1)} %collective-permute-done.3.refs_2_), channel_id=1, source_target_pairs={{0,1},{1,0},{2,3},{3,2},{4,5},{5,4},{6,7},{7,6},{8,9},{9,8},{10,11... | collective-permute-start | bytes 6291464 | tf_op jit(solution)/shard_map/ppermute | solution.py:412
  98.2 10.3 %collective-permute-start.8 = (bf16[2,2,8,32,256]{4,3,2,1,0:T(8,128)(2,1)S(1)}, bf16[2,2,8,32,256]{4,3,2,1,0:T(8,128)(2,1)S(1)}, u32[]{:S(2)}, u32[]{:S(2)}) collective-permute-start(bf16[2,2,8,32,256]{4,3,2,1,0:T(8,128)(2,1)S(1)} %pad_maximum_fusion.4), channel_id=1, source_target_pairs={{0,56},{1,17},{16,32},{17,1},{32,16},{33,49},{48,8},{49,33},{8,48}... | collective-permute-start | bytes 1572872 | tf_op jit(solution)/shard_map/ppermute | solution.py:401
  108.5 17.5 %copy-start.4 = (bf16[1024,256]{1,0:T(8,128)(2,1)S(1)}, bf16[1024,256]{1,0:T(8,128)(2,1)}, u32[]{:S(2)}) copy-start(bf16[1024,256]{1,0:T(8,128)(2,1)} %copy-done.3) | copy-start | bytes 1572868
  108.5 6.0 %collective-permute-start.9 = (bf16[1024,256]{1,0:T(8,128)(2,1)S(1)}, bf16[1024,256]{1,0:T(8,128)(2,1)S(1)}, u32[]{:S(2)}, u32[]{:S(2)}) collective-permute-start(bf16[1024,256]{1,0:T(8,128)(2,1)S(1)} %get-tuple-element.63.mixed_t), channel_id=1, source_target_pairs={{0,1},{1,0},{2,3},{3,2},{4,5},{5,4},{6,7},{7,6},{8,9},{9,8},{10,11... | collective-permute-start | bytes 1572872 | tf_op jit(solution)/shard_map/ppermute | solution.py:412
  112.5 13.4 %collective-permute-start.13 = (bf16[2,2,8,32,256]{4,3,2,1,0:T(8,128)(2,1)S(1)}, bf16[2,2,8,32,256]{4,3,2,1,0:T(8,128)(2,1)S(1)}, u32[]{:S(2)}, u32[]{:S(2)}) collective-permute-start(bf16[2,2,8,32,256]{4,3,2,1,0:T(8,128)(2,1)S(1)} %collective-permute-done.8.refs_6_), channel_id=1, source_target_pairs={{0,1},{1,0},{2,3},{3,2},{4,5},{5,4},{6,7},{7,6},{8,9},{9,8},{10,11... | collective-permute-start | bytes 1572872 | tf_op jit(solution)/shard_map/ppermute | solution.py:412
  115.2 19.7 %collective-permute-start.10 = (bf16[32,16,256]{2,1,0:T(8,128)(2,1)S(1)}, bf16[32,16,256]{2,1,0:T(8,128)(2,1)S(1)}, u32[]{:S(2)}, u32[]{:S(2)}) collective-permute-start(bf16[32,16,256]{2,1,0:T(8,128)(2,1)S(1)} %get-tuple-element.72), channel_id=1, source_target_pairs={{0,2},{2,4},{4,6},{6,0},{1,3},{3,5},{5,7},{7,1},{8,10},{10,12},{12... | collective-permute-start | bytes 786440 | tf_op jit(solution)/shard_map/ppermute | solution.py:462
  118.2 16.7 %collective-permute-start.11 = (bf16[32,16,256]{2,1,0:T(8,128)(2,1)S(1)}, bf16[32,16,256]{2,1,0:T(8,128)(2,1)S(1)}, u32[]{:S(2)}, u32[]{:S(2)}) collective-permute-start(bf16[32,16,256]{2,1,0:T(8,128)(2,1)S(1)} %get-tuple-element.73), channel_id=1, source_target_pairs={{0,4},{2,6},{4,0},{6,2},{1,5},{3,7},{5,1},{7,3},{8,12},{10,14},{12... | collective-permute-start | bytes 786440 | tf_op jit(solution)/shard_map/ppermute | solution.py:462
  122.7 12.2 %collective-permute-start.12 = (bf16[32,16,256]{2,1,0:T(8,128)(2,1)S(1)}, bf16[32,16,256]{2,1,0:T(8,128)(2,1)S(1)}, u32[]{:S(2)}, u32[]{:S(2)}) collective-permute-start(bf16[32,16,256]{2,1,0:T(8,128)(2,1)S(1)} %get-tuple-element.74), channel_id=1, source_target_pairs={{0,6},{2,0},{4,2},{6,4},{1,7},{3,1},{5,3},{7,5},{8,14},{10,8},{12,... | collective-permute-start | bytes 786440 | tf_op jit(solution)/shard_map/ppermute | solution.py:462
  162.9 21.7 %all-to-all-start.2 = ((f32[16,32,128]{2,1,0:T(8,128)}), f32[16,32,128]{2,1,0:T(8,128)S(1)}, u32[]{:S(2)}, u32[]{:S(2)}) async-start(f32[16,32,128]{2,1,0:T(8,128)} %broadcast_in_dim.28), calls=%async_computation.2 | async-start | bytes 524288 | tf_op jit(solution)/shard_map/all_to_all | solution.py:417

commit v5 on v4

--- a/solution.py
+++ b/solution.py
@@ -55,19 +55,19 @@
 ORDER = (0, 1, -1, -2)
 
 
-def block_copies(scalars, buffers, part, sems, side, at, first, size):
+def block_copies(scalars, buffers, part, sems, rel, at, first, size):
     zl, c, sz = scalars[1], scalars[2], scalars[3]
-    place = lax.rem(scalars[5] + side, 2)
+    side = lax.rem(scalars[5] + rel, 2)
     cols, to = slice(first, first + size), slice(at, at + size)
     copies = []
     for core in range(2):
         half, sign = (c, sz) if core == 0 else (1 - c, -sz)
-        own, near, far = buffers[core * 3 : core * 3 + 3]
-        blocks = [own.at[place, :, :, cols], near.at[place, :, :, cols]]
-        blocks += [far.at[k, place, :, :, to] for k in range(2)]
+        own, near, *fars = buffers[core * 4 : core * 4 + 4]
+        blocks = [own.at[rel], near.at[rel], fars[rel].at[0], fars[rel].at[1]]
         for block, by in zip(blocks, ORDER):
             dst = part.at[half, side, :, lax.rem(zl + 8 + by * sign, 4), :, to]
-            copies.append(pltpu.make_async_copy(block, dst, sems.at[len(copies)]))
+            sem = sems.at[len(copies)]
+            copies.append(pltpu.make_async_copy(block.at[:, :, cols], dst, sem))
     return copies
 
 
@@ -90,9 +90,8 @@
         copy.wait()
 
 
-def columns(weights, half, head):
-    at = head % 4 * 256
-    return weights[half, head // 4, :, :, :, at : at + 256].reshape(WIDTH, 256)
+def columns(weights, half, side, k):
+    return weights[half, side, :, :, :, k * 256 : (k + 1) * 256].reshape(WIDTH, 256)
 
 
 def row_mean(value):
@@ -120,8 +119,8 @@
 
 
 def forward_kernel(scalars, normed, *refs):
-    buffers = refs[:6]
-    pre, gate_out, natt_out, inv_out, mixed_out, weights, sems = refs[6:]
+    buffers = refs[:8]
+    pre, gate_out, natt_out, inv_out, mixed_out, weights, sems = refs[8:]
     copies = weight_copies(scalars, buffers, weights, sems)
     for pair in copies:
         start(pair)
@@ -133,20 +132,22 @@
         if h < HEADS:
             if h % 2 == 0:
                 wait(copies[h // 2])
-            pre_a = dot(normed[...], columns(weights, 0, h))
-            pre_b = dot(normed[...], columns(weights, 1, h))
-            pre[h, :, :256] = pre_a
-            pre[h, :, 256:] = pre_b
+            side = lax.rem(scalars[5] + h // 4, 2)
+            head = side * 4 + h % 4
+            pre_a = dot(normed[...], columns(weights, 0, side, h % 4))
+            pre_b = dot(normed[...], columns(weights, 1, side, h % 4))
+            pre[head, :, :256] = pre_a
+            pre[head, :, 256:] = pre_b
             act_a = pre_a * sigmoid(pre_a)
             act_b = (pre_b * sigmoid(pre_b)).astype(BF)
-            gate_out[h] = act_a[:, :HD]
-            now = act_b[:, :HD], act_b[:, HD:], act_a[:, HD:].astype(BF)
+            gate_out[head] = act_a[:, :HD]
+            now = head, act_b[:, :HD], act_b[:, HD:], act_a[:, HD:].astype(BF)
         if h > 0:
-            query, key, val = last
+            last_head, query, key, val = last
             scores = dot(query, key, NT) * SCALE
             attn = (scores * sigmoid(scores) * mask).astype(BF)
             att = dot(attn, val)
-            natt_out[h - 1] = att
+            natt_out[last_head] = att
             total = total + att
         last = now
     mean = row_mean(total)
@@ -175,12 +176,11 @@
     scalars, gate_in, natt_in, inv_in, upstream, normed_t, inv_t, up_t, pre, *refs
 ):
     out, weights, out_w, grad_mixed, grad_pre, grad_normed, sems, out_sems = refs[8:]
-    out_buffers = [*refs[0:2], refs[6], *refs[3:5], refs[7]]
     out_moves = []
-    for side in range(2):
-        args = out_w, out_sems.at[side], side, 0, SIDE, OUT // 2
-        out_moves += block_copies(scalars, out_buffers, *args)
-    moves = weight_copies(scalars, refs[:6], weights, sems)
+    for rel in range(2):
+        args = out_w, out_sems.at[rel], rel, 0, SIDE, OUT // 2
+        out_moves += block_copies(scalars, refs[:8], *args)
+    moves = weight_copies(scalars, refs[:8], weights, sems)
     start(out_moves)
     for pair in moves:
         start(pair)
@@ -334,7 +334,7 @@
             shape((SEQ, HD), F32),
             shape((WIDTH, SEQ), BF),
         ],
-        in_specs=[SMEM, VMEM] + [HBM] * 6,
+        in_specs=[SMEM, VMEM] + [HBM] * 8,
         out_specs=[VMEM] * 5,
         scratch_shapes=[WEIGHT_SCRATCH, pltpu.SemaphoreType.DMA((PAIRS, 8))],
         compiler_params=params(22),
@@ -439,30 +439,27 @@
     )
     own, normed, send_up = tie(own, normed, send_up)
 
-    near, beside = tie(to_z(own, 0), to_x(own))
-    near_beside = to_z(beside, 0)
-    near = jnp.stack([near, near_beside])
-    near, own, beside, send_up = tie(near, own, beside, send_up)
+    near, beside, send_up = tie(to_z(own, 0), to_x(own), send_up)
+    far = to_z(jnp.stack([own, near]), 1)
+    near_beside = to_x(near)
     own = jnp.stack([own, beside])
-    own_swapped = swap(own)
-    far = to_z(jnp.stack([own[..., :SIDE], near[..., :SIDE]]), 1)
-    near_swapped, other_up = swap(near), swap(send_up)
-    out_w = jnp.stack([own[..., SIDE:], near[..., SIDE:]])
-    far, own_swapped, near_swapped, out_w, other_up = tie(
-        far, own_swapped, near_swapped, out_w, other_up
+    own_swapped, other_up = swap(own), swap(send_up)
+    far, near_beside, near, own_swapped, other_up = tie(
+        far, near_beside, near, own_swapped, other_up
     )
-    buffers = [own, near, far, own_swapped, near_swapped, swap(far)]
-    out_far = to_z(out_w, 1)
+    far_beside = to_x(far)
+    mine = [own, jnp.stack([near, near_beside]), far]
+    others = [own_swapped, swap(mine[1]), swap(far)]
+    far_beside, *others = tie(far_beside, *others)
+    buffers = mine + [far_beside] + others + [swap(far_beside)]
     pre, gate, natt, inv_att, mixed_t = forward(scalars, normed, buffers)
-    mixed_t, out_far = tie(mixed_t, out_far)
-    out_w = [out_far, swap(out_far)]
     parts = weight_term(mixed_t, swap(mixed_t), half_up, other_up)
     *parts, natt = tie(*parts, natt)
     parts = [parts[0]] + [
         lax.ppermute(parts[k], "x", [(i, (i + k) % 4) for i in range(4)]) for k in (1, 2, 3)
     ]
     rows_t = backward(
-        scalars, gate, natt, inv_att, upstream, normed_t, inv_t, up_t, pre, buffers + out_w
+        scalars, gate, natt, inv_att, upstream, normed_t, inv_t, up_t, pre, buffers
     )
     *parts, rows_t = tie(*parts, rows_t)
     part = sum(part.astype(F32) for part in parts).astype(BF)

time: 187 us -> 185 us (0.989)
  starting transfers between devices: 68.4 us -> 71.4 us
  waiting for transfers between devices: 55.1 us -> 52.3 us
  other arithmetic: 4.07 us -> 1.86 us
    ppermute x4 -> x2, waiting for transfers between devices: 29.4 us -> 4.2 us  [to_z(): return lax.ppermute(value, ('zl', 'zh', 'c'), pairs)]
    ppermute x1 -> x3, waiting for transfers between devices: 4.58 us -> 22.8 us  [to_x(): return lax.ppermute(value, ('x', 'c'), pairs)]
    ppermute x1 -> x3, starting transfers between devices: 4.39 us -> 13.2 us  [to_x(): return lax.ppermute(value, ('x', 'c'), pairs)]
    ppermute x6, waiting for transfers between devices: 2 us -> 6.18 us  [swap(): return lax.ppermute(value, 'c', [(0, 1), (1, 0)])]
    ppermute x4 -> x2, starting transfers between devices: 19.5 us -> 15.6 us  [to_z(): return lax.ppermute(value, ('zl', 'zh', 'c'), pairs)]
    another operation x8 -> x4, other arithmetic: 3.68 us -> 1.47 us  [the longest x1 1.33 us: per_device(): far = to_z(jnp.stack([own, near]), 1)]
    ppermute x6, starting transfers between devices: 15.6 us -> 13.4 us  [swap(): return lax.ppermute(value, 'c', [(0, 1), (1, 0)])]
  transfers between devices with their start and end apart: 16 -> 16, of which waited for: 8 -> 10; matrix products, arithmetic and copies ran while one was open for 1% -> 0% of each run, Pallas kernels for 13% -> 9%
where the time goes in v5:
time: 185 us; the launch traced here: 183 us
  starting transfers between devices  71.4 us (39%)
  waiting for transfers between devices  52.3 us (28%)
  blocking collectives  27 us (15%)
  Pallas kernels  23.7 us (13%)
  local copies, waits for them, and re-layouts  5.26 us (3%)
  other arithmetic  1.86 us (1%)
    all_to_all x1, blocking collectives, per_device(): both = lax.all_to_all(both, COL, 0, 0, tiled=True)  27 us
    ppermute x3, waiting for transfers between devices, to_x(): return lax.ppermute(value, ('x', 'c'), pairs)  22.8 us
    all_to_all x2, waiting for transfers between devices, spread(): return lax.all_to_all(many, axes, 0, 0, tiled=True)  19.1 us
    all_to_all x2, starting transfers between devices, spread(): return lax.all_to_all(many, axes, 0, 0, tiled=True)  18.9 us
    ppermute x2, starting transfers between devices, to_z(): return lax.ppermute(value, ('zl', 'zh', 'c'), pairs)  15.6 us
    ppermute x6, starting transfers between devices, swap(): return lax.ppermute(value, 'c', [(0, 1), (1, 0)])  13.4 us
    ppermute x3, starting transfers between devices, to_x(): return lax.ppermute(value, ('x', 'c'), pairs)  13.2 us
    ppermute x3, starting transfers between devices, per_device(): lax.ppermute(parts[k], 'x', [(i, (i + k) % 4) for i in range(4)])  10.3 us
  transfers between devices with their start and end apart: 16, of which 10 were waited for; matrix products, arithmetic and copies ran while one was open for 0% of the time, Pallas kernels for 9%

profile of v5, /device:TPU:1, one launch (start us, length us, event | category | flops | bytes accessed | tf_op | source)
XLA Modules:
  0.0 183.2 jit_solution(16695841580920904161)
XLA Ops:
  0.6 0.0 copy-start
  0.7 1.0 copy.13
  1.7 0.1 copy.10
  1.8 0.0 copy-start.1
  1.8 0.0 copy-start.2
  1.8 0.1 reshape.41
  1.9 0.0 copy-done
  1.9 0.1 constant_dynamic-slice_fusion
  2.0 0.9 broadcast_in_dim.10
  2.9 7.7 %all-to-all-start = ((bf16[8,32,1280]{2,1,0:T(8,128)(2,1)}), bf16[8,32,1280]{2,1,0:T(8,128)(2,1)}, u32[]{:S(2)}, u32[]{:S(2)}) async-start(bf16[8,32,1280]{2,1,0:T(8,128)(2,1)} %broadcast_in_dim.10), calls=%async_computation | async-start | bytes 1310720 | tf_op jit(solution)/shard_map/all_to_all | solution.py:417
  11.2 0.1 stack.48.scalars
  11.3 0.0 copy-done.1
  11.3 0.0 copy-done.2
  11.3 1.4 prepare.1
  12.7 0.0 copy-start.3
  12.8 0.8 copy-done.3
  13.5 0.7 copy-done.5
  14.2 14.2 %all-to-all-done = bf16[8,32,1280]{2,1,0:T(8,128)(2,1)} async-done(((bf16[8,32,1280]{2,1,0:T(8,128)(2,1)}), bf16[8,32,1280]{2,1,0:T(8,128)(2,1)}, u32[]{:S(2)}, u32[]{:S(2)}) %all-to-all-start) | async-done | bytes 655392 | tf_op jit(solution)/shard_map/all_to_all | solution.py:417
  28.5 13.7 %collective-permute-start = (bf16[8,32,1280]{2,1,0:T(8,128)(2,1)}, bf16[8,32,1280]{2,1,0:T(8,128)(2,1)S(1)}, u32[]{:S(2)}, u32[]{:S(2)}) collective-permute-start(bf16[8,32,1280]{2,1,0:T(8,128)(2,1)} %all-to-all-done), channel_id=1, source_target_pairs={{0,16},{1,57},{16,0},{17,33},{32,48},{33,17},{48,32},{49,9},{8,24}... | collective-permute-start | bytes 1966088 | tf_op jit(solution)/shard_map/ppermute | solution.py:401
  42.1 4.4 %collective-permute-start.1 = (bf16[8,32,1280]{2,1,0:T(8,128)(2,1)}, bf16[8,32,1280]{2,1,0:T(8,128)(2,1)S(1)}, u32[]{:S(2)}, u32[]{:S(2)}) collective-permute-start(bf16[8,32,1280]{2,1,0:T(8,128)(2,1)} %all-to-all-done), channel_id=1, source_target_pairs={{0,2},{1,7},{2,0},{3,5},{4,6},{5,3},{6,4},{7,1},{8,10},{9,15},{10,... | collective-permute-start | bytes 1966088 | tf_op jit(solution)/shard_map/ppermute | solution.py:408
  46.5 3.8 %collective-permute-done = bf16[8,32,1280]{2,1,0:T(8,128)(2,1)S(1)} collective-permute-done((bf16[8,32,1280]{2,1,0:T(8,128)(2,1)}, bf16[8,32,1280]{2,1,0:T(8,128)(2,1)S(1)}, u32[]{:S(2)}, u32[]{:S(2)}) %collective-permute-start) | collective-permute-done | bytes 655392 | tf_op jit(solution)/shard_map/ppermute | solution.py:401
  50.3 4.6 %collective-permute-done.1 = bf16[8,32,1280]{2,1,0:T(8,128)(2,1)S(1)} collective-permute-done((bf16[8,32,1280]{2,1,0:T(8,128)(2,1)}, bf16[8,32,1280]{2,1,0:T(8,128)(2,1)S(1)}, u32[]{:S(2)}, u32[]{:S(2)}) %collective-permute-start.1) | collective-permute-done | bytes 655392 | tf_op jit(solution)/shard_map/ppermute | solution.py:408
  54.9 1.3 pad_maximum_fusion
  56.2 1.9 %collective-permute-start.2 = (bf16[2,8,32,1280]{3,2,1,0:T(8,128)(2,1)S(1)}, bf16[2,8,32,1280]{3,2,1,0:T(8,128)(2,1)S(1)}, u32[]{:S(2)}, u32[]{:S(2)}) collective-permute-start(bf16[2,8,32,1280]{3,2,1,0:T(8,128)(2,1)S(1)} %get-tuple-element.92), channel_id=1, source_target_pairs={{0,56},{1,17},{16,32},{17,1},{32,16},{33,49},{48,8},{49,33},{8,48}... | collective-permute-start | bytes 3932168 | tf_op jit(solution)/shard_map/ppermute | solution.py:401
  58.1 3.2 %collective-permute-start.4 = (bf16[2,8,32,1280]{3,2,1,0:T(8,128)(2,1)S(1)}, bf16[2,8,32,1280]{3,2,1,0:T(8,128)(2,1)S(1)}, u32[]{:S(2)}, u32[]{:S(2)}) collective-permute-start(bf16[2,8,32,1280]{3,2,1,0:T(8,128)(2,1)S(1)} %get-tuple-element.93.refs_0_), channel_id=1, source_target_pairs={{0,1},{1,0},{2,3},{3,2},{4,5},{5,4},{6,7},{7,6},{8,9},{9,8},{10,11... | collective-permute-start | bytes 3932168 | tf_op jit(solution)/shard_map/ppermute | solution.py:412
  61.3 4.4 %collective-permute-start.3 = (bf16[8,32,1280]{2,1,0:T(8,128)(2,1)S(1)}, bf16[8,32,1280]{2,1,0:T(8,128)(2,1)S(1)}, u32[]{:S(2)}, u32[]{:S(2)}) collective-permute-start(bf16[8,32,1280]{2,1,0:T(8,128)(2,1)S(1)} %collective-permute-done), channel_id=1, source_target_pairs={{0,2},{1,7},{2,0},{3,5},{4,6},{5,3},{6,4},{7,1},{8,10},{9,15},{10,... | collective-permute-start | bytes 1966088 | tf_op jit(solution)/shard_map/ppermute | solution.py:408
  65.7 0.0 copy-done.6
  65.7 1.9 %collective-permute-start.5 = (bf16[256,512]{1,0:T(8,128)(2,1)S(1)}, bf16[256,512]{1,0:T(8,128)(2,1)S(1)}, u32[]{:S(2)}, u32[]{:S(2)}) collective-permute-start(bf16[256,512]{1,0:T(8,128)(2,1)S(1)} %copy-done.6), channel_id=1, source_target_pairs={{0,1},{1,0},{2,3},{3,2},{4,5},{5,4},{6,7},{7,6},{8,9},{9,8},{10,11... | collective-permute-start | bytes 786440 | tf_op jit(solution)/shard_map/ppermute | solution.py:412
  67.6 1.5 collective-permute-done.5.other_up
  69.1 5.0 %collective-permute-done.3 = bf16[8,32,1280]{2,1,0:T(8,128)(2,1)S(1)} collective-permute-done((bf16[8,32,1280]{2,1,0:T(8,128)(2,1)S(1)}, bf16[8,32,1280]{2,1,0:T(8,128)(2,1)S(1)}, u32[]{:S(2)}, u32[]{:S(2)}) %collective-permute-start.3) | collective-permute-done | bytes 655392 | tf_op jit(solution)/shard_map/ppermute | solution.py:408
  74.1 0.4 collective-permute-done.2.refs_2_
  74.6 0.0 collective-permute-done.4.refs_4_
  74.6 0.1 pad_maximum_fusion.2.refs_1_
  74.7 0.0 copy-start.7
  74.7 2.3 %collective-permute-start.7 = (bf16[2,8,32,1280]{3,2,1,0:T(8,128)(2,1)S(1)}, bf16[2,8,32,1280]{3,2,1,0:T(8,128)(2,1)S(1)}, u32[]{:S(2)}, u32[]{:S(2)}) collective-permute-start(bf16[2,8,32,1280]{3,2,1,0:T(8,128)(2,1)S(1)} %pad_maximum_fusion.2.refs_1_), channel_id=1, source_target_pairs={{0,1},{1,0},{2,3},{3,2},{4,5},{5,4},{6,7},{7,6},{8,9},{9,8},{10,11... | collective-permute-start | bytes 3932168 | tf_op jit(solution)/shard_map/ppermute | solution.py:412
  77.0 4.4 %collective-permute-start.6 = (bf16[2,8,32,1280]{3,2,1,0:T(8,128)(2,1)S(1)}, bf16[2,8,32,1280]{3,2,1,0:T(8,128)(2,1)S(1)}, u32[]{:S(2)}, u32[]{:S(2)}) collective-permute-start(bf16[2,8,32,1280]{3,2,1,0:T(8,128)(2,1)S(1)} %collective-permute-done.2.refs_2_), channel_id=1, source_target_pairs={{0,2},{1,7},{2,0},{3,5},{4,6},{5,3},{6,4},{7,1},{8,10},{9,15},{10,... | collective-permute-start | bytes 3932168 | tf_op jit(solution)/shard_map/ppermute | solution.py:408
  81.4 1.9 %collective-permute-start.8 = (bf16[2,8,32,1280]{3,2,1,0:T(8,128)(2,1)S(1)}, bf16[2,8,32,1280]{3,2,1,0:T(8,128)(2,1)S(1)}, u32[]{:S(2)}, u32[]{:S(2)}) collective-permute-start(bf16[2,8,32,1280]{3,2,1,0:T(8,128)(2,1)S(1)} %collective-permute-done.2.refs_2_), channel_id=1, source_target_pairs={{0,1},{1,0},{2,3},{3,2},{4,5},{5,4},{6,7},{7,6},{8,9},{9,8},{10,11... | collective-permute-start | bytes 3932168 | tf_op jit(solution)/shard_map/ppermute | solution.py:412
  83.3 0.0 collective-permute-done.7.refs_5_
  83.3 13.2 %collective-permute-done.6.refs_3_ = bf16[2,8,32,1280]{3,2,1,0:T(8,128)(2,1)S(1)} collective-permute-done((bf16[2,8,32,1280]{3,2,1,0:T(8,128)(2,1)S(1)}, bf16[2,8,32,1280]{3,2,1,0:T(8,128)(2,1)S(1)}, u32[]{:S(2)}, u32[]{:S(2)}) %collective-permute-start.6) | collective-permute-done | bytes 1310752 | tf_op jit(solution)/shard_map/ppermute | solution.py:408
  96.6 0.0 collective-permute-done.8.refs_6_
  96.6 2.0 %collective-permute-start.9 = (bf16[2,8,32,1280]{3,2,1,0:T(8,128)(2,1)S(1)}, bf16[2,8,32,1280]{3,2,1,0:T(8,128)(2,1)S(1)}, u32[]{:S(2)}, u32[]{:S(2)}) collective-permute-start(bf16[2,8,32,1280]{3,2,1,0:T(8,128)(2,1)S(1)} %collective-permute-done.6.refs_3_), channel_id=1, source_target_pairs={{0,1},{1,0},{2,3},{3,2},{4,5},{5,4},{6,7},{7,6},{8,9},{9,8},{10,11... | collective-permute-start | bytes 3932168 | tf_op jit(solution)/shard_map/ppermute | solution.py:412
  98.5 3.0 %collective-permute-done.9.refs_7_ = bf16[2,8,32,1280]{3,2,1,0:T(8,128)(2,1)S(1)} collective-permute-done((bf16[2,8,32,1280]{3,2,1,0:T(8,128)(2,1)S(1)}, bf16[2,8,32,1280]{3,2,1,0:T(8,128)(2,1)S(1)}, u32[]{:S(2)}, u32[]{:S(2)}) %collective-permute-start.9) | collective-permute-done | bytes 1310752 | tf_op jit(solution)/shard_map/ppermute | solution.py:412
  101.5 6.5 %forward.1 = (f32[8,256,512]{2,1,0:T(8,128)S(1)}, f32[8,256,128]{2,1,0:T(8,128)S(1)}, f32[8,256,128]{2,1,0:T(8,128)S(1)}, f32[256,128]{1,0:T(8,128)S(1)}, bf16[1024,256]{1,0:T(8,128)(2,1)S(1)}) custom-call(s32[6]{0:T(128)S(1)} %stack.48.scalars, bf16[256,1024]{1,0:T(8,128)(2,1)S(1)} %get-tuple-element.48.normed, ...), custom_call_target="tpu_custom_call" | custom-call | flops 1024 | bytes 1024 | tf_op jit(solution)/shard_map/forward/pallas_call | solution.py:328
  108.0 2.2 %collective-permute-start.10 = (bf16[1024,256]{1,0:T(8,128)(2,1)S(1)}, bf16[1024,256]{1,0:T(8,128)(2,1)S(1)}, u32[]{:S(2)}, u32[]{:S(2)}) collective-permute-start(bf16[1024,256]{1,0:T(8,128)(2,1)S(1)} %get-tuple-element.62.mixed_t), channel_id=1, source_target_pairs={{0,1},{1,0},{2,3},{3,2},{4,5},{5,4},{6,7},{7,6},{8,9},{9,8},{10,11... | collective-permute-start | bytes 1572872 | tf_op jit(solution)/shard_map/ppermute | solution.py:412
  110.2 1.7 collective-permute-done.10.other_mixed_t
  112.0 0.7 weight_term.1
  112.7 2.7 %collective-permute-start.11 = (bf16[32,16,256]{2,1,0:T(8,128)(2,1)S(1)}, bf16[32,16,256]{2,1,0:T(8,128)(2,1)S(1)}, u32[]{:S(2)}, u32[]{:S(2)}) collective-permute-start(bf16[32,16,256]{2,1,0:T(8,128)(2,1)S(1)} %get-tuple-element.71), channel_id=1, source_target_pairs={{0,2},{2,4},{4,6},{6,0},{1,3},{3,5},{5,7},{7,1},{8,10},{10,12},{12... | collective-permute-start | bytes 786440 | tf_op jit(solution)/shard_map/ppermute | solution.py:459
  115.4 4.8 %collective-permute-start.12 = (bf16[32,16,256]{2,1,0:T(8,128)(2,1)S(1)}, bf16[32,16,256]{2,1,0:T(8,128)(2,1)S(1)}, u32[]{:S(2)}, u32[]{:S(2)}) collective-permute-start(bf16[32,16,256]{2,1,0:T(8,128)(2,1)S(1)} %get-tuple-element.72), channel_id=1, source_target_pairs={{0,4},{2,6},{4,0},{6,2},{1,5},{3,7},{5,1},{7,3},{8,12},{10,14},{12... | collective-permute-start | bytes 786440 | tf_op jit(solution)/shard_map/ppermute | solution.py:459
  120.2 2.8 %collective-permute-start.13 = (bf16[32,16,256]{2,1,0:T(8,128)(2,1)S(1)}, bf16[32,16,256]{2,1,0:T(8,128)(2,1)S(1)}, u32[]{:S(2)}, u32[]{:S(2)}) collective-permute-start(bf16[32,16,256]{2,1,0:T(8,128)(2,1)S(1)} %get-tuple-element.73), channel_id=1, source_target_pairs={{0,6},{2,0},{4,2},{6,4},{1,7},{3,1},{5,3},{7,5},{8,14},{10,8},{12,... | collective-permute-start | bytes 786440 | tf_op jit(solution)/shard_map/ppermute | solution.py:459
  123.0 0.1 pad.7.clone
  123.1 0.1 maximum_maximum_fusion
  123.2 0.0 copy-done.4
  123.2 8.8 %backward.1 = bf16[1024,256]{1,0:T(8,128)(2,1)S(1)} custom-call(s32[6]{0:T(128)S(1)} %stack.48.scalars, f32[8,256,128]{2,1,0:T(8,128)S(1)} %get-tuple-element.74.gate_in, f32[8,256,128]{2,1,0:T(8,128)S(1)} %get-tuple-element.75.natt_in, f32[256,128]{1,0:T(8,128)S(1)} %get-tuple-element.76.inv_in, bf16[256,1024]{1,0:T(8,128)(2,1)S(1)} %get-tuple-element.77.upstream, ...), custom_call_target="tpu_custom_call" | custom-call | flops 1024 | bytes 1024 | tf_op jit(solution)/shard_map/backward/pallas_call | solution.py:359
  132.0 0.0 collective-permute-done.11
  132.0 0.0 collective-permute-done.12
  132.0 0.0 collective-permute-done.13
  132.0 0.1 add_convert_fusion
  132.2 0.1 pad_maximum_fusion.3
  132.3 27.0 %all_to_all.15.rows = bf16[32,56,256]{2,1,0:T(8,128)(2,1)S(1)} all-to-all(bf16[32,56,256]{2,1,0:T(8,128)(2,1)S(1)} %pad_maximum_fusion.3), channel_id=1, replica_groups=mesh['y'=8,'zl'=4,'zh'=2,'x'=4,'c'=2] {'y','zl'}, dimensions={0} | all-to-all | bytes 1835008 | tf_op jit(solution)/shard_map/all_to_all | solution.py:469
  159.4 0.7 broadcast_in_dim.28
  160.1 11.3 %all-to-all-start.2 = ((f32[16,32,128]{2,1,0:T(8,128)}), f32[16,32,128]{2,1,0:T(8,128)S(1)}, u32[]{:S(2)}, u32[]{:S(2)}) async-start(f32[16,32,128]{2,1,0:T(8,128)} %broadcast_in_dim.28), calls=%async_computation.2 | async-start | bytes 524288 | tf_op jit(solution)/shard_map/all_to_all | solution.py:417
  171.4 6.2 %table.1 = f32[32,8192]{1,0:T(8,128)} custom-call(s32[32,8,256]{2,1,0:T(8,128)S(1)} %slice_convert_fusion.ids, bf16[32,56,256]{2,1,0:T(8,128)(2,1)S(1)} %all_to_all.15.rows), custom_call_target="tpu_custom_call" | custom-call | flops 1024 | bytes 1024 | tf_op jit(solution)/shard_map/table/pallas_call | solution.py:380
  177.6 4.8 %all-to-all-done.2 = f32[16,32,128]{2,1,0:T(8,128)S(1)} async-done(((f32[16,32,128]{2,1,0:T(8,128)}), f32[16,32,128]{2,1,0:T(8,128)S(1)}, u32[]{:S(2)}, u32[]{:S(2)}) %all-to-all-start.2) | async-done | bytes 262176 | tf_op jit(solution)/shard_map/all_to_all | solution.py:417
  182.5 0.7 copy_bitcast_fusion
  (16 shorter events, 0.2 us)
Async XLA Ops:
  0.6 1.3 copy-start
  1.8 9.5 %copy-start.1 = (bf16[1,256,1024]{2,1,0:T(8,128)(2,1)S(1)}, bf16[1,256,1024]{2,1,0:T(8,128)(2,1)}, u32[]{:S(2)}) copy-start(bf16[1,256,1024]{2,1,0:T(8,128)(2,1)} %param.6) | copy-start | bytes 1572868
  1.8 9.5 %copy-start.2 = (bf16[1,256,1024]{2,1,0:T(8,128)(2,1)S(1)}, bf16[1,256,1024]{2,1,0:T(8,128)(2,1)}, u32[]{:S(2)}) copy-start(bf16[1,256,1024]{2,1,0:T(8,128)(2,1)} %param.11) | copy-start | bytes 1572868
  2.9 25.5 %all-to-all-start = ((bf16[8,32,1280]{2,1,0:T(8,128)(2,1)}), bf16[8,32,1280]{2,1,0:T(8,128)(2,1)}, u32[]{:S(2)}, u32[]{:S(2)}) async-start(bf16[8,32,1280]{2,1,0:T(8,128)(2,1)} %broadcast_in_dim.10), calls=%async_computation | async-start | bytes 1310720 | tf_op jit(solution)/shard_map/all_to_all | solution.py:417
  12.7 0.8 copy-start.3
  13.5 0.7 copy-start.5
  28.5 21.8 %collective-permute-start = (bf16[8,32,1280]{2,1,0:T(8,128)(2,1)}, bf16[8,32,1280]{2,1,0:T(8,128)(2,1)S(1)}, u32[]{:S(2)}, u32[]{:S(2)}) collective-permute-start(bf16[8,32,1280]{2,1,0:T(8,128)(2,1)} %all-to-all-done), channel_id=1, source_target_pairs={{0,16},{1,57},{16,0},{17,33},{32,48},{33,17},{48,32},{49,9},{8,24}... | collective-permute-start | bytes 1966088 | tf_op jit(solution)/shard_map/ppermute | solution.py:401
  42.1 12.8 %collective-permute-start.1 = (bf16[8,32,1280]{2,1,0:T(8,128)(2,1)}, bf16[8,32,1280]{2,1,0:T(8,128)(2,1)S(1)}, u32[]{:S(2)}, u32[]{:S(2)}) collective-permute-start(bf16[8,32,1280]{2,1,0:T(8,128)(2,1)} %all-to-all-done), channel_id=1, source_target_pairs={{0,2},{1,7},{2,0},{3,5},{4,6},{5,3},{6,4},{7,1},{8,10},{9,15},{10,... | collective-permute-start | bytes 1966088 | tf_op jit(solution)/shard_map/ppermute | solution.py:408
  54.9 10.8 %copy-start.6 = (bf16[256,512]{1,0:T(8,128)(2,1)S(1)}, bf16[256,512]{1,0:T(8,128)(2,1)}, u32[]{:S(2)}) copy-start(bf16[256,512]{1,0:T(8,128)(2,1)} %copy-done.5) | copy-start | bytes 786436
  56.2 18.4 %collective-permute-start.2 = (bf16[2,8,32,1280]{3,2,1,0:T(8,128)(2,1)S(1)}, bf16[2,8,32,1280]{3,2,1,0:T(8,128)(2,1)S(1)}, u32[]{:S(2)}, u32[]{:S(2)}) collective-permute-start(bf16[2,8,32,1280]{3,2,1,0:T(8,128)(2,1)S(1)} %get-tuple-element.92), channel_id=1, source_target_pairs={{0,56},{1,17},{16,32},{17,1},{32,16},{33,49},{48,8},{49,33},{8,48}... | collective-permute-start | bytes 3932168 | tf_op jit(solution)/shard_map/ppermute | solution.py:401
  58.1 16.4 %collective-permute-start.4 = (bf16[2,8,32,1280]{3,2,1,0:T(8,128)(2,1)S(1)}, bf16[2,8,32,1280]{3,2,1,0:T(8,128)(2,1)S(1)}, u32[]{:S(2)}, u32[]{:S(2)}) collective-permute-start(bf16[2,8,32,1280]{3,2,1,0:T(8,128)(2,1)S(1)} %get-tuple-element.93.refs_0_), channel_id=1, source_target_pairs={{0,1},{1,0},{2,3},{3,2},{4,5},{5,4},{6,7},{7,6},{8,9},{9,8},{10,11... | collective-permute-start | bytes 3932168 | tf_op jit(solution)/shard_map/ppermute | solution.py:412
  61.3 12.8 %collective-permute-start.3 = (bf16[8,32,1280]{2,1,0:T(8,128)(2,1)S(1)}, bf16[8,32,1280]{2,1,0:T(8,128)(2,1)S(1)}, u32[]{:S(2)}, u32[]{:S(2)}) collective-permute-start(bf16[8,32,1280]{2,1,0:T(8,128)(2,1)S(1)} %collective-permute-done), channel_id=1, source_target_pairs={{0,2},{1,7},{2,0},{3,5},{4,6},{5,3},{6,4},{7,1},{8,10},{9,15},{10,... | collective-permute-start | bytes 1966088 | tf_op jit(solution)/shard_map/ppermute | solution.py:408
  65.7 3.4 %collective-permute-start.5 = (bf16[256,512]{1,0:T(8,128)(2,1)S(1)}, bf16[256,512]{1,0:T(8,128)(2,1)S(1)}, u32[]{:S(2)}, u32[]{:S(2)}) collective-permute-start(bf16[256,512]{1,0:T(8,128)(2,1)S(1)} %copy-done.6), channel_id=1, source_target_pairs={{0,1},{1,0},{2,3},{3,2},{4,5},{5,4},{6,7},{7,6},{8,9},{9,8},{10,11... | collective-permute-start | bytes 786440 | tf_op jit(solution)/shard_map/ppermute | solution.py:412
  74.7 35.5 %copy-start.7 = (s32[1,256]{1,0:T(1,128)S(1)}, s32[1,256]{1,0:T(1,128)}, u32[]{:S(2)}) copy-start(s32[1,256]{1,0:T(1,128)} %param.7) | copy-start | bytes 3076
  74.7 8.6 %collective-permute-start.7 = (bf16[2,8,32,1280]{3,2,1,0:T(8,128)(2,1)S(1)}, bf16[2,8,32,1280]{3,2,1,0:T(8,128)(2,1)S(1)}, u32[]{:S(2)}, u32[]{:S(2)}) collective-permute-start(bf16[2,8,32,1280]{3,2,1,0:T(8,128)(2,1)S(1)} %pad_maximum_fusion.2.refs_1_), channel_id=1, source_target_pairs={{0,1},{1,0},{2,3},{3,2},{4,5},{5,4},{6,7},{7,6},{8,9},{9,8},{10,11... | collective-permute-start | bytes 3932168 | tf_op jit(solution)/shard_map/ppermute | solution.py:412
  77.0 19.6 %collective-permute-start.6 = (bf16[2,8,32,1280]{3,2,1,0:T(8,128)(2,1)S(1)}, bf16[2,8,32,1280]{3,2,1,0:T(8,128)(2,1)S(1)}, u32[]{:S(2)}, u32[]{:S(2)}) collective-permute-start(bf16[2,8,32,1280]{3,2,1,0:T(8,128)(2,1)S(1)} %collective-permute-done.2.refs_2_), channel_id=1, source_target_pairs={{0,2},{1,7},{2,0},{3,5},{4,6},{5,3},{6,4},{7,1},{8,10},{9,15},{10,... | collective-permute-start | bytes 3932168 | tf_op jit(solution)/shard_map/ppermute | solution.py:408
  81.4 15.2 %collective-permute-start.8 = (bf16[2,8,32,1280]{3,2,1,0:T(8,128)(2,1)S(1)}, bf16[2,8,32,1280]{3,2,1,0:T(8,128)(2,1)S(1)}, u32[]{:S(2)}, u32[]{:S(2)}) collective-permute-start(bf16[2,8,32,1280]{3,2,1,0:T(8,128)(2,1)S(1)} %collective-permute-done.2.refs_2_), channel_id=1, source_target_pairs={{0,1},{1,0},{2,3},{3,2},{4,5},{5,4},{6,7},{7,6},{8,9},{9,8},{10,11... | collective-permute-start | bytes 3932168 | tf_op jit(solution)/shard_map/ppermute | solution.py:412
  96.6 4.9 %collective-permute-start.9 = (bf16[2,8,32,1280]{3,2,1,0:T(8,128)(2,1)S(1)}, bf16[2,8,32,1280]{3,2,1,0:T(8,128)(2,1)S(1)}, u32[]{:S(2)}, u32[]{:S(2)}) collective-permute-start(bf16[2,8,32,1280]{3,2,1,0:T(8,128)(2,1)S(1)} %collective-permute-done.6.refs_3_), channel_id=1, source_target_pairs={{0,1},{1,0},{2,3},{3,2},{4,5},{5,4},{6,7},{7,6},{8,9},{9,8},{10,11... | collective-permute-start | bytes 3932168 | tf_op jit(solution)/shard_map/ppermute | solution.py:412
  108.0 15.2 %copy-start.4 = (bf16[1024,256]{1,0:T(8,128)(2,1)S(1)}, bf16[1024,256]{1,0:T(8,128)(2,1)}, u32[]{:S(2)}) copy-start(bf16[1024,256]{1,0:T(8,128)(2,1)} %copy-done.3) | copy-start | bytes 1572868
  108.0 3.9 %collective-permute-start.10 = (bf16[1024,256]{1,0:T(8,128)(2,1)S(1)}, bf16[1024,256]{1,0:T(8,128)(2,1)S(1)}, u32[]{:S(2)}, u32[]{:S(2)}) collective-permute-start(bf16[1024,256]{1,0:T(8,128)(2,1)S(1)} %get-tuple-element.62.mixed_t), channel_id=1, source_target_pairs={{0,1},{1,0},{2,3},{3,2},{4,5},{5,4},{6,7},{7,6},{8,9},{9,8},{10,11... | collective-permute-start | bytes 1572872 | tf_op jit(solution)/shard_map/ppermute | solution.py:412
  112.7 19.3 %collective-permute-start.11 = (bf16[32,16,256]{2,1,0:T(8,128)(2,1)S(1)}, bf16[32,16,256]{2,1,0:T(8,128)(2,1)S(1)}, u32[]{:S(2)}, u32[]{:S(2)}) collective-permute-start(bf16[32,16,256]{2,1,0:T(8,128)(2,1)S(1)} %get-tuple-element.71), channel_id=1, source_target_pairs={{0,2},{2,4},{4,6},{6,0},{1,3},{3,5},{5,7},{7,1},{8,10},{10,12},{12... | collective-permute-start | bytes 786440 | tf_op jit(solution)/shard_map/ppermute | solution.py:459
  115.4 16.6 %collective-permute-start.12 = (bf16[32,16,256]{2,1,0:T(8,128)(2,1)S(1)}, bf16[32,16,256]{2,1,0:T(8,128)(2,1)S(1)}, u32[]{:S(2)}, u32[]{:S(2)}) collective-permute-start(bf16[32,16,256]{2,1,0:T(8,128)(2,1)S(1)} %get-tuple-element.72), channel_id=1, source_target_pairs={{0,4},{2,6},{4,0},{6,2},{1,5},{3,7},{5,1},{7,3},{8,12},{10,14},{12... | collective-permute-start | bytes 786440 | tf_op jit(solution)/shard_map/ppermute | solution.py:459
  120.2 11.9 %collective-permute-start.13 = (bf16[32,16,256]{2,1,0:T(8,128)(2,1)S(1)}, bf16[32,16,256]{2,1,0:T(8,128)(2,1)S(1)}, u32[]{:S(2)}, u32[]{:S(2)}) collective-permute-start(bf16[32,16,256]{2,1,0:T(8,128)(2,1)S(1)} %get-tuple-element.73), channel_id=1, source_target_pairs={{0,6},{2,0},{4,2},{6,4},{1,7},{3,1},{5,3},{7,5},{8,14},{10,8},{12,... | collective-permute-start | bytes 786440 | tf_op jit(solution)/shard_map/ppermute | solution.py:459
  160.1 22.4 %all-to-all-start.2 = ((f32[16,32,128]{2,1,0:T(8,128)}), f32[16,32,128]{2,1,0:T(8,128)S(1)}, u32[]{:S(2)}, u32[]{:S(2)}) async-start(f32[16,32,128]{2,1,0:T(8,128)} %broadcast_in_dim.28), calls=%async_computation.2 | async-start | bytes 524288 | tf_op jit(solution)/shard_map/all_to_all | solution.py:417
